TPU v7x, 512 devices: a whole 4x4x16 slice. The times are simulated.
512 devices in a mesh: blk: 64 (over y, z_lo, core), hid: 8 (over x, z_hi).
Axes of the slice: x: 4, y: 4, z: 16 (z_hi: 2, z_lo: 8; z = z_hi * 8 + z_lo), core: 2. Of those that a mesh axis runs over, the one named last changes fastest.
Arguments:
- features: bfloat16 [8192, 128], P('blk'), may hold values from -6 to 6
- tile_values: bfloat16 [64, 8, 32, 128, 128], P('blk', 'hid'), may hold values from -0.03125 to 0.03125
- tile_block: int32 [64, 8, 32], P('blk', 'hid'), may hold values from 0 to 63, as said below
- weight: bfloat16 [128, 256], P(None, 'hid'), may hold values from -0.5 to 0.5
- bias: float32 [256], P('hid'), may hold values from -3 to 3
- cotangent: bfloat16 [8192, 256], P('blk', 'hid'), may hold values from -6 to 6
Outputs:
- activations: bfloat16 [8192, 256], P('blk', 'hid')
- feature_grad: float32 [8192, 128], P('blk')
- weight_grad: float32 [128, 256], P(None, 'hid')
- bias_grad: float32 [256], P('hid')
Inputs may be any that keep to these rules, and one draw needn't show every extreme that they name: `tile_block`: each device's list (fixed i, j) is sorted by source block and names each block at most 3 times; it names its own row block i exactly 3 times and at least one other block exactly 3 times.
All inputs are finite; a program needn't handle non-finite values.
Results may differ from a plain program's by a relative error of at most 0.017.
Values may be sent and summed in bfloat16 or wider, within the bound.
No kernel may reach another device: no remote copies, remote signals or barrier semaphores. Data moves between devices by JAX's collectives and lax.ppermute only.
A program may use at most 64 MiB of HBM per device.

v0:
```python
import jax
import jax.numpy as jnp
from jax import lax
from jax.sharding import PartitionSpec as P

KSTEP = 3


def tile_window(sources, base_block, span_blocks):
    n_tiles = sources.shape[0]
    window_len = min(n_tiles, KSTEP * span_blocks)
    first_tile = jnp.sum((sources < base_block).astype(jnp.int32))
    end_tile = jnp.sum((sources < base_block + span_blocks).astype(jnp.int32))
    begin_tile = jnp.minimum(first_tile, n_tiles - window_len)
    picked = begin_tile + jnp.arange(window_len, dtype=jnp.int32)
    usable = (picked >= first_tile) & (picked < end_tile)
    return (picked, usable)


def on_device(features, tile_values, tile_block, weight, bias, cotangent):
    tile_len = tile_values.shape[-1]
    feat_dim = features.shape[1]
    tile_vals = tile_values.reshape(-1, tile_len, tile_len)
    sources = tile_block.reshape(-1)
    block_count = lax.axis_size("blk")
    shard_rows = lax.all_gather(features, "blk", axis=0, tiled=True)
    span_blocks = shard_rows.shape[0] // tile_len
    base_block = jnp.int32(0) // tile_len
    picked, usable = tile_window(sources, base_block, span_blocks)
    chosen = jnp.take(tile_vals, picked, axis=0)
    local_pos = jnp.clip(jnp.take(sources, picked), 0, span_blocks - 1)
    inputs = jnp.take(shard_rows.reshape(span_blocks, tile_len, feat_dim), local_pos, axis=0)
    products = jnp.einsum("wab,wbf->waf", chosen, inputs, preferred_element_type=jnp.float32)
    partial_sum = jnp.einsum("w,waf->af", usable.astype(jnp.float32), products)
    aggregated = lax.psum(partial_sum, "hid").astype(jnp.bfloat16)
    preact = jnp.dot(aggregated, weight, preferred_element_type=jnp.float32) + bias
    activations = jax.nn.gelu(preact).astype(jnp.bfloat16)
    _, pullback = jax.vjp(jax.nn.gelu, preact)
    pre_grad = pullback(cotangent.astype(jnp.float32))[0].astype(jnp.bfloat16)
    partial_back = jnp.dot(pre_grad, weight.T, preferred_element_type=jnp.float32)
    back_feat = lax.psum(partial_back, "hid").astype(jnp.bfloat16)
    local_wgrad = lax.dot_general(
        aggregated, pre_grad, (((0,), (0,)), ((), ())), preferred_element_type=jnp.float32
    )
    local_bgrad = jnp.sum(pre_grad.astype(jnp.float32), axis=0)
    weight_grad, bias_grad = lax.psum((local_wgrad, local_bgrad), "blk")
    contrib = jnp.einsum("kab,af->kbf", tile_vals, back_feat, preferred_element_type=jnp.float32)
    onehot = (sources[:, None] == jnp.arange(block_count, dtype=jnp.int32)[None, :]).astype(
        jnp.float32
    )
    placed = jnp.einsum("kn,kbf->nbf", onehot, contrib).reshape(block_count * tile_len, feat_dim)
    block_part = lax.psum_scatter(placed, "blk", scatter_dimension=0, tiled=True)
    feature_grad = lax.psum(block_part, "hid")
    return (activations, feature_grad, weight_grad, bias_grad)


def solution(mesh):
    placed = (
        P("blk", None),
        P("blk", "hid", None, None, None),
        P("blk", "hid", None),
        P(None, "hid"),
        P("hid"),
        P("blk", "hid"),
    )
    return jax.shard_map(
        on_device,
        mesh=mesh,
        in_specs=placed,
        out_specs=(P("blk", "hid"), P("blk", None), P(None, "hid"), P("hid")),
        check_vma=False,
    )
```

profile of v0, /device:TPU:6, one launch (start us, length us, event | category | flops | bytes accessed | tf_op | source)
XLA Modules:
  0.0 1162.1 jit_solution(5238277465043286385)
XLA Ops:
  7.2 0.0 copy-start
  7.2 0.0 copy-start.1
  7.2 0.0 all-gather.2.cloned.1.call-start
  7.2 0.7 all-gather.2.cloned.1.call-update
  7.9 0.0 reduce-scatter.2.cloned.1.call-start
  8.0 1.9 copy.13
  9.9 1.3 fusion.37
  11.9 2.0 gather_fusion
  13.9 0.0 copy-start.2
  13.9 0.0 copy-start.3
  13.9 0.0 copy-done.1
  13.9 0.7 gather_fusion.1
  14.7 120.7 %all-gather.2.cloned.1.call-done = bf16[8192,128]{1,0:T(8,128)(2,1)} async-done(((bf16[128,128]{1,0:T(8,128)(2,1)}), bf16[8192,128]{1,0:T(8,128)(2,1)}) %all-gather.2.cloned.1.call-update) | async-done | bytes 2097168 | tf_op jit(solution)/shard_map/all_gather | solution.py:26
  135.3 2.3 gather_fusion.2
  137.7 0.5 fusion.6
  138.2 2.0 fusion.2
  140.2 72.8 %psum.35 = bf16[128,128]{1,0:T(8,128)(2,1)S(1)} all-reduce(f32[128,128]{1,0:T(8,128)S(1)} %bitcast.42), channel_id=1, replica_groups=mesh['blk'=64,'hid'=8] {'hid'}, use_global_device_ids=true, to_apply=%region_2.3 | all-reduce | flops 16384 | bytes 98304 | tf_op jit(solution)/shard_map/psum | solution.py:35
  212.9 0.0 copy-done
  212.9 0.0 copy-done.2
  212.9 0.0 copy-done.3
  212.9 0.9 convert_reduce_fusion
  213.8 0.2 fusion.45
  214.0 68.6 %psum.36 = bf16[128,128]{1,0:T(8,128)(2,1)S(1)} all-reduce(f32[128,128]{1,0:T(8,128)S(1)} %fusion.45), channel_id=1, replica_groups=mesh['blk'=64,'hid'=8] {'hid'}, use_global_device_ids=true, to_apply=%region_3.4 | all-reduce | flops 16384 | bytes 98304 | tf_op jit(solution)/shard_map/psum | solution.py:41
  282.6 3.0 fusion
  285.7 6.5 copy.10
  292.2 0.0 reduce-scatter.2.cloned.1.call-update
  292.2 0.0 all-reduce.3.cloned.1.call-start
  292.3 441.0 %reduce-scatter.2.cloned.1.call-done = f32[128,128]{1,0:T(8,128)} async-done(((f32[8192,128]{1,0:T(8,128)}), f32[128,128]{1,0:T(8,128)}) %reduce-scatter.2.cloned.1.call-update) | async-done | bytes 65552 | tf_op jit(solution)/shard_map/reduce_scatter | solution.py:52
  733.2 0.0 all-reduce.3.cloned.1.call-update
  733.3 0.1 fusion.46
  733.4 420.8 %all-reduce = (f32[128,32]{0,1:T(8,128)}, f32[32]{0:T(128)}) all-reduce(f32[128,32]{0,1:T(8,128)S(1)} %fusion.46, f32[32]{0:T(128)S(1)} %get-tuple-element.8), channel_id=1, replica_groups=mesh['blk'=64,'hid'=8] {'blk'}, use_global_device_ids=true, to_apply=%region_6.7 | all-reduce | flops 4128 | bytes 33024 | tf_op jit(solution)/shard_map/psum | solution.py:46
  1154.1 1.5 copy.17
  (6 shorter events, 0.0 us)
Async XLA Ops:
  7.2 205.8 %copy-start = (bf16[128,32]{0,1:T(8,128)(2,1)S(1)}, bf16[128,32]{0,1:T(8,128)(2,1)}, u32[]{:S(2)}) copy-start(bf16[128,32]{0,1:T(8,128)(2,1)} %param.9) | copy-start | bytes 24580
  7.2 6.7 copy-start.1
  7.2 128.1 %all-gather.2.cloned.1.call-start = ((), (), s32[]{:S(2)}) async-start(), calls=%async_computation.1 | async-start | bytes 2129920 | tf_op jit(solution)/shard_map/all_gather | solution.py:26
  7.9 725.3 %reduce-scatter.2.cloned.1.call-start = ((), (), s32[]{:S(2)}) async-start(), calls=%async_computation.2 | async-start | bytes 4259840 | tf_op jit(solution)/shard_map/reduce_scatter | solution.py:52
  13.9 199.1 %copy-start.2 = (bf16[128,32]{0,1:T(8,128)(2,1)S(1)}, bf16[128,32]{0,1:T(8,128)(2,1)}, u32[]{:S(2)}) copy-start(bf16[128,32]{0,1:T(8,128)(2,1)} %param.11) | copy-start | bytes 24580
  13.9 199.1 %copy-start.3 = (f32[32]{0:T(128)S(1)}, f32[32]{0:T(128)}, u32[]{:S(2)}) copy-start(f32[32]{0:T(128)} %param.10) | copy-start | bytes 388
  292.2 861.9 %all-reduce.3.cloned.1.call-start = ((), (), s32[]{:S(2)}) async-start(), calls=%async_computation.3 | async-start | bytes 131072 | tf_op jit(solution)/shard_map/psum | solution.py:53
Sparse Core Ops, SparseCore 0:
  10.2 125.1 all-gather.1
  292.3 440.8 reduce-scatter.1
  736.4 139.7 all-reduce.2
where the time goes:
time: 1160 us
  waiting for transfers between devices  562 us (48%)
  blocking collectives  562 us (48%)
  local copies, waits for them, and re-layouts  15 us (1%)
  between operations  14.5 us (1%)
    reduce_scatter x1, waiting for transfers between devices, on_device(): lax.psum_scatter(placed, 'blk', scatter_dimension=0, tiled=True)  441 us
    psum x1, blocking collectives, on_device(): weight_grad, bias_grad = lax.psum((local_wgrad, local_bgrad), 'blk')  421 us
    all_gather x1, waiting for transfers between devices, on_device(): shard_rows = lax.all_gather(features, 'blk', axis=0, tiled=True)  121 us
    psum x1, blocking collectives, on_device(): aggregated = lax.psum(partial_sum, 'hid').astype(jnp.bfloat16)  72.8 us
    psum x1, blocking collectives, on_device(): back_feat = lax.psum(partial_back, 'hid').astype(jnp.bfloat16)  68.6 us
  transfers between devices with their start and end apart: 3, of which 2 were waited for; matrix products, arithmetic and copies ran while one was open for 1% of the time, Pallas kernels for 0%

commit v1 on v0

v1 whole, which is shorter than its diff:
```python
import functools

import jax
import jax.numpy as jnp
from jax import lax
from jax.experimental import pallas as pl
from jax.experimental.pallas import tpu as pltpu
from jax.sharding import Mesh
from jax.sharding import PartitionSpec as P

BF16 = jnp.bfloat16
F32 = jnp.float32
AXES = ("y", "zl", "c", "x", "zh")
BLK = ("y", "zl", "c")
HID = ("x", "zh")
EXTRA = 16
SCALE = 0.7978845608028654
CUBIC = 0.044715
PARAMS = pltpu.CompilerParams(vmem_limit_bytes=48 * 1024 * 1024)


def mm(a, b, ca, cb):
    return lax.dot_general(a, b, (((ca,), (cb,)), ((), ())), preferred_element_type=F32)


def slope(v):
    t = jnp.tanh(SCALE * (v + CUBIC * (v * v * v)))
    du = SCALE * (1.0 + (3.0 * CUBIC) * (v * v))
    return 0.5 * (1.0 + t) + 0.5 * v * (1.0 - t * t) * du


def place(src, zl_n):
    return src // (2 * zl_n), (src // 2) % zl_n, src % 2


def forward_kernel(zl_n, x_n, src_ref, tiles_ref, own_ref, oth_ref, out_ref):
    my_c = lax.axis_index("c")
    tile = tiles_ref.shape[-1]
    feat = own_ref.shape[-1]
    acc = jnp.zeros((tile, feat), F32)
    n = tiles_ref.shape[0]
    for k in range(0, n, 2):
        blocks = []
        for q in range(k, k + 2):
            y, zl, c = place(src_ref[q], zl_n)
            a = own_ref[pl.ds(y, 1), :, pl.ds(zl, 1)].reshape(tile, feat)
            b = oth_ref[pl.ds(y, 1), :, pl.ds(zl, 1)].reshape(tile, feat)
            blocks.append(jnp.where(c == my_c, a, b))
        lhs = jnp.concatenate([tiles_ref[k], tiles_ref[k + 1]], axis=1)
        acc = acc + mm(lhs, jnp.concatenate(blocks, axis=0), 1, 0)
    part = acc.astype(BF16)
    for x in range(x_n):
        out_ref[x] = part


def backward_kernel(
    zl_n, src_ref, sum_ref, other_ref, packs_ref, pack_ref, bias_ref, tiles_ref, act_ref, own_ref, oth_ref
):
    my_c = lax.axis_index("c")
    x_n, zh_n = packs_ref.shape[:2]
    hidden = bias_ref.shape[1]
    tile = tiles_ref.shape[-1]
    y_n = own_ref.shape[0] // x_n
    rows = tile // x_n
    agg = (sum_ref[...].astype(F32) + other_ref[...].astype(F32)).astype(BF16)

    def gather(start, size):
        parts = [packs_ref[x, z, start : start + size, :] for x in range(x_n) for z in range(zh_n)]
        return jnp.concatenate(parts, axis=0)

    def bias_of(three):
        return mm(three, jnp.ones((three.shape[0], tile), BF16), 0, 0)[:hidden]

    w_t = gather(0, hidden)
    cot_t = gather(hidden, hidden)
    bias_t = jnp.concatenate(
        [bias_of(packs_ref[x, z, 2 * hidden :, :]) for x in range(x_n) for z in range(zh_n)], axis=0
    )
    pre_t = mm(w_t, agg, 1, 1) + bias_t
    grad_t = (cot_t.astype(F32) * slope(pre_t)).astype(BF16)
    back = mm(grad_t, w_t, 0, 0).astype(BF16)

    w_mine = pack_ref[0:hidden, :]
    pre = mm(agg, w_mine, 1, 1) + bias_ref[...]
    t = jnp.tanh(SCALE * (pre + CUBIC * (pre * pre * pre)))
    act_ref[...] = (pre * (0.5 * (1.0 + t))).astype(BF16)
    mine_t = mm(w_mine, agg, 1, 1) + bias_of(pack_ref[2 * hidden :, :])
    grad_mine = (pack_ref[hidden : 2 * hidden, :].astype(F32) * slope(mine_t)).astype(BF16)
    wgrad = mm(grad_mine, agg, 1, 0).astype(BF16)
    bgrad = mm(jnp.ones((8, tile), BF16), grad_mine, 1, 1)
    bgrad = jnp.concatenate([bgrad, jnp.zeros((8, tile - hidden), F32)], axis=1).astype(BF16)

    body = zl_n * rows
    share = hidden // y_n
    assert share <= 8
    own_ref[:, :body, :] = jnp.zeros((y_n * x_n, body, tile), BF16)
    oth_ref[:, :body, :] = jnp.zeros((y_n * x_n, body, tile), BF16)
    for y in range(y_n):
        piece = [wgrad[y * share : (y + 1) * share].astype(F32), bgrad.astype(F32)]
        if share < 8:
            piece.insert(1, jnp.zeros((8 - share, tile), F32))
        piece = jnp.concatenate(piece, axis=0).astype(BF16)
        for x in range(x_n):
            own_ref[y * x_n + x, body:, :] = piece
            oth_ref[y * x_n + x, body:, :] = piece

    acc = jnp.zeros((tile, tile), F32)
    for k in range(tiles_ref.shape[0]):
        src = src_ref[k]
        contrib = mm(tiles_ref[k], back, 0, 0)
        if k:
            acc = contrib + jnp.where(src == src_ref[k - 1], acc, 0.0)
        else:
            acc = contrib
        y, zl, c = place(src, zl_n)
        out = acc.astype(BF16).reshape(x_n, rows, tile)
        at = (pl.ds(y * x_n, x_n), pl.ds(pl.multiple_of(zl * rows, rows), rows), slice(None))

        @pl.when(c == my_c)
        def _():
            own_ref[at] = out

        @pl.when(c != my_c)
        def _():
            oth_ref[at] = out


def plane_sum_kernel(y_n, x_n, in_ref, out_ref):
    my_x = lax.axis_index("x")
    zl_n, zh_n, size, _ = out_ref.shape
    rows = size - EXTRA
    body = zl_n * rows
    total = in_ref[0, :body, :].astype(F32)
    for s in range(1, y_n * x_n):
        total = total + in_ref[s, :body, :].astype(F32)
    extra = in_ref[my_x, body:, :].astype(F32)
    for y in range(1, y_n):
        extra = extra + in_ref[y * x_n + my_x, body:, :].astype(F32)
    total = total.astype(BF16)
    extra = extra.astype(BF16)
    for z in range(zl_n):
        for h in range(zh_n):
            out_ref[z, h, :rows, :] = total[z * rows : (z + 1) * rows]
            out_ref[z, h, rows:, :] = extra


def column_sum_kernel(zl_n, zh_n, in_ref, out_ref):
    my_zh = lax.axis_index("zh")
    rows = in_ref.shape[1] - EXTRA
    total = in_ref[0, :rows, :].astype(F32)
    for s in range(1, zl_n * zh_n):
        total = total + in_ref[s, :rows, :].astype(F32)
    extra = in_ref[my_zh, rows:, :].astype(F32)
    for z in range(1, zl_n):
        extra = extra + in_ref[z * zh_n + my_zh, rows:, :].astype(F32)
    for s in range(out_ref.shape[0]):
        out_ref[s, :rows, :] = total.astype(out_ref.dtype)
        out_ref[s, rows:, :] = extra.astype(out_ref.dtype)


def finish_kernel(y_n, x_n, in_ref, feat_ref, wgrad_ref, bgrad_ref):
    my_x, my_y = lax.axis_index("x"), lax.axis_index("y")
    rows = in_ref.shape[1] - EXTRA
    hidden = bgrad_ref.shape[1]
    share = hidden // y_n
    for x in range(x_n):
        feat_ref[x * rows : (x + 1) * rows, :] = in_ref[my_y * x_n + x, :rows, :].astype(F32)
    pieces = [in_ref[y * x_n + my_x, rows:, :].astype(F32) for y in range(y_n)]
    wgrad_ref[...] = jnp.concatenate([p[:share] for p in pieces], axis=0).T
    bgrad_ref[...] = pieces[0][8:9, :hidden]


VMEM = pl.BlockSpec(memory_space=pltpu.VMEM)
SMEM = pl.BlockSpec(memory_space=pltpu.SMEM)


def shape(*dims, dtype=BF16):
    return jax.ShapeDtypeStruct(dims, dtype)


def call(kernel, out, *args, smem=0):
    many = isinstance(out, (tuple, list))
    return pl.pallas_call(
        kernel,
        out_shape=out,
        in_specs=[SMEM] * smem + [VMEM] * (len(args) - smem),
        out_specs=[VMEM] * len(out) if many else VMEM,
        compiler_params=PARAMS,
    )(*args)


def to_all(v, axes):
    return lax.all_to_all(v, axes, 0, 0, tiled=True)


def swap(v, axis):
    return lax.ppermute(v, axis, [(0, 1), (1, 0)])


def on_device(sizes, features, tile_values, tile_block, weight, bias, cotangent):
    y_n, zl_n, c_n, x_n, zh_n = (sizes[a] for a in AXES)
    tile = tile_values.shape[-1]
    feat = features.shape[1]
    hidden = bias.shape[0]
    rows = tile // x_n
    tiles = tile_values.reshape(-1, tile, tile)
    sources = tile_block.reshape(-1)
    my_x, my_zh = lax.axis_index("x"), lax.axis_index("zh")

    b_hi = bias.astype(BF16)
    b_mid = (bias - b_hi.astype(F32)).astype(BF16)
    b_lo = (bias - b_hi.astype(F32) - b_mid.astype(F32)).astype(BF16)
    terms = jnp.pad(jnp.stack([b_hi, b_mid, b_lo]), ((0, 13), (0, feat - hidden)))
    pack = jnp.concatenate([weight.T, cotangent.T, terms], axis=0)
    pack_other = swap(pack, "zh")

    mine = lax.dynamic_slice_in_dim(features, my_x * rows, rows, 0)
    column = to_all(jnp.broadcast_to(mine[None], (zl_n, rows, feat)), "zl")
    pair = jnp.where(my_zh == 0, jnp.stack([pack, pack_other]), jnp.stack([pack_other, pack]))
    packs = to_all(jnp.broadcast_to(pair[None], (x_n,) + pair.shape), "x")
    plane = to_all(jnp.broadcast_to(column[None], (y_n * x_n, zl_n, rows, feat)), ("y", "x"))
    own = plane.reshape(y_n, x_n, zl_n, rows, feat)
    other = swap(own, "c")

    part = call(
        functools.partial(forward_kernel, zl_n, x_n), shape(x_n, tile, feat), sources, tiles, own, other, smem=1
    )
    summed = jnp.sum(to_all(part, "x").astype(F32), axis=0).astype(BF16)
    summed_other = swap(summed, "zh")

    payload = shape(y_n * x_n, zl_n * rows + EXTRA, feat)
    activations, keep, give = call(
        functools.partial(backward_kernel, zl_n),
        (shape(tile, hidden), payload, payload),
        sources,
        summed,
        summed_other,
        packs,
        pack,
        bias[None],
        tiles,
        smem=1,
    )
    both = (keep.astype(F32) + swap(give, "c").astype(F32)).astype(BF16)
    across = to_all(both, ("y", "x"))
    up = call(
        functools.partial(plane_sum_kernel, y_n, x_n), shape(zl_n, zh_n, rows + EXTRA, feat), across
    ).reshape(zl_n * zh_n, rows + EXTRA, feat)
    down = to_all(up, ("zl", "zh"))
    last = call(
        functools.partial(column_sum_kernel, zl_n, zh_n), shape(y_n * x_n, rows + EXTRA, feat), down
    )
    feature_grad, weight_grad, bias_grad = call(
        functools.partial(finish_kernel, y_n, x_n),
        (shape(tile, feat, dtype=F32), shape(feat, hidden, dtype=F32), shape(1, hidden, dtype=F32)),
        to_all(last, ("y", "x")),
    )
    return activations, feature_grad, weight_grad, bias_grad[0]


def split_mesh(mesh, sizes):
    return Mesh(mesh.devices.reshape(tuple(sizes[a] for a in AXES)), AXES)


def solution(mesh, sizes=None):
    sizes = sizes or {"y": 4, "zl": 8, "c": 2, "x": 4, "zh": 2}
    placed = (
        P(BLK, None),
        P(BLK, HID, None, None, None),
        P(BLK, HID, None),
        P(None, HID),
        P(HID),
        P(BLK, HID),
    )
    return jax.shard_map(
        functools.partial(on_device, sizes),
        mesh=split_mesh(mesh, sizes),
        in_specs=placed,
        out_specs=(P(BLK, HID), P(BLK, None), P(None, HID), P(HID)),
        check_vma=False,
    )
```

time: 1160 us -> 161 us (0.14)
  the two profiles are of different devices: /device:TPU:6 before, /device:TPU:32 now
where the time goes in v1:
time: 161 us; the launch traced here: 160 us
  blocking collectives  91.1 us (57%)
  starting transfers between devices  28.8 us (18%)
  waiting for transfers between devices  25.4 us (16%)
  Pallas kernels  10.6 us (7%)
  local copies, waits for them, and re-layouts  3.05 us (2%)
    all_to_all x4, blocking collectives, to_all(): return lax.all_to_all(v, axes, 0, 0, tiled=True)  91.1 us
    ppermute x4, starting transfers between devices, swap(): return lax.ppermute(v, axis, [(0, 1), (1, 0)])  18.4 us
    ppermute x4, waiting for transfers between devices, swap(): return lax.ppermute(v, axis, [(0, 1), (1, 0)])  13.4 us
    all_to_all x3, waiting for transfers between devices, to_all(): return lax.all_to_all(v, axes, 0, 0, tiled=True)  12 us
    pallas_call x5, Pallas kernels, call(): pl.pallas_call(kernel, out_shape=out, in_specs=[SMEM] * smem + [VMEM] * (...  10.6 us
    all_to_all x3, starting transfers between devices, to_all(): return lax.all_to_all(v, axes, 0, 0, tiled=True)  10.4 us
  transfers between devices with their start and end apart: 7, of which 5 were waited for; matrix products, arithmetic and copies ran while one was open for 0% of the time, Pallas kernels for 1%

profile of v1, /device:TPU:32, one launch (start us, length us, event | category | flops | bytes accessed | tf_op | source)
XLA Modules:
  0.0 160.1 jit_solution(11878700113911856919)
XLA Ops:
  0.6 0.0 copy-start
  0.7 0.7 copy-done
  1.4 21.7 %all_to_all.35 = bf16[8,32,128]{2,1,0:T(8,128)(2,1)S(1)} all-to-all(bf16[8,32,128]{2,1,0:T(8,128)(2,1)S(1)} %broadcast_in_dim.8), channel_id=1, replica_groups=mesh['y'=4,'zl'=8,'c'=2,'x'=4,'zh'=2] {'zl'}, dimensions={0} | all-to-all | bytes 131072 | tf_op jit(solution)/shard_map/all_to_all | solution.py:193
  23.1 0.2 broadcast_in_dim.9
  23.3 0.0 copy-start.2
  23.3 0.0 copy-start.4
  23.3 0.0 copy-start.5
  23.3 0.0 copy-start.1
  23.4 23.1 %all_to_all.36 = bf16[16,8,32,128]{3,2,1,0:T(8,128)(2,1)S(1)} all-to-all(bf16[16,8,32,128]{3,2,1,0:T(8,128)(2,1)S(1)} %broadcast_in_dim.9), channel_id=1, replica_groups=mesh['y'=4,'zl'=8,'c'=2,'x'=4,'zh'=2] {'y','x'}, dimensions={0} | all-to-all | bytes 2097152 | tf_op jit(solution)/shard_map/all_to_all | solution.py:193
  46.4 1.9 %collective-permute-start = (bf16[4,4,8,32,128]{4,3,2,1,0:T(8,128)(2,1)S(1)}, bf16[4,4,8,32,128]{4,3,2,1,0:T(8,128)(2,1)S(1)}, u32[]{:S(2)}, u32[]{:S(2)}) collective-permute-start(bf16[4,4,8,32,128]{4,3,2,1,0:T(8,128)(2,1)S(1)} %bitcast.19), channel_id=1, source_target_pairs={{0,8},{8,0},{1,9},{9,1},{2,10},{10,2},{3,11},{11,3},{4,12},{12,4},... | collective-permute-start | bytes 3145736 | tf_op jit(solution)/shard_map/ppermute | solution.py:197
  48.4 8.2 %collective-permute-start.2 = (bf16[80,128]{1,0:T(8,128)(2,1)S(1)}, bf16[80,128]{1,0:T(8,128)(2,1)S(1)}, u32[]{:S(2)}, u32[]{:S(2)}) collective-permute-start(bf16[80,128]{1,0:T(8,128)(2,1)S(1)} %get-tuple-element.21.pack_ref), channel_id=1, source_target_pairs={{0,1},{1,0},{2,3},{3,2},{4,5},{5,4},{6,7},{7,6},{8,9},{9,8},{10,11... | collective-permute-start | bytes 61448 | tf_op jit(solution)/shard_map/ppermute | solution.py:197
  56.7 1.8 %shard_map.93 = bf16[4,128,128]{2,1,0:T(8,128)(2,1)} custom-call(s32[32]{0:T(128)S(1)} %bitcast.23, bf16[32,128,128]{2,1,0:T(8,128)(2,1)S(1)} %bitcast.17, bf16[4,4,8,32,128]{4,3,2,1,0:T(8,128)(2,1)S(1)} %bitcast.20, bf16[4,4,8,32,128]{4,3,2,1,0:T(8,128)(2,1)S(1)} %collective-permute-done.oth_ref), custom_call_target="tpu_custom_call" | custom-call | tf_op jit(solution)/shard_map/pallas_call | solution.py:183
  58.5 3.3 %all-to-all-start.2 = ((bf16[4,128,128]{2,1,0:T(8,128)(2,1)}), bf16[4,128,128]{2,1,0:T(8,128)(2,1)S(1)}, u32[]{:S(2)}, u32[]{:S(2)}) async-start(bf16[4,128,128]{2,1,0:T(8,128)(2,1)} %shard_map.93), calls=%async_computation.2 | async-start | bytes 262144 | tf_op jit(solution)/shard_map/all_to_all | solution.py:193
  61.9 1.6 collective-permute-done.2
  63.5 4.3 %all-to-all-done.2 = bf16[4,128,128]{2,1,0:T(8,128)(2,1)S(1)} async-done(((bf16[4,128,128]{2,1,0:T(8,128)(2,1)}), bf16[4,128,128]{2,1,0:T(8,128)(2,1)S(1)}, u32[]{:S(2)}, u32[]{:S(2)}) %all-to-all-start.2) | async-done | bytes 131104 | tf_op jit(solution)/shard_map/all_to_all | solution.py:193
  67.8 0.7 broadcast_in_dim.10
  68.5 3.3 %all-to-all-start.3 = ((bf16[4,2,80,128]{3,2,1,0:T(8,128)(2,1)}), bf16[4,2,80,128]{3,2,1,0:T(8,128)(2,1)S(1)}, u32[]{:S(2)}, u32[]{:S(2)}) async-start(bf16[4,2,80,128]{3,2,1,0:T(8,128)(2,1)} %broadcast_in_dim.10), calls=%async_computation.3 | async-start | bytes 327680 | tf_op jit(solution)/shard_map/all_to_all | solution.py:193
  71.9 6.3 %collective-permute-start.1 = (bf16[128,128]{1,0:T(8,128)(2,1)S(1)}, bf16[128,128]{1,0:T(8,128)(2,1)S(1)}, u32[]{:S(2)}, u32[]{:S(2)}) collective-permute-start(bf16[128,128]{1,0:T(8,128)(2,1)S(1)} %reduce_sum.12.sum_ref), channel_id=1, source_target_pairs={{0,1},{1,0},{2,3},{3,2},{4,5},{5,4},{6,7},{7,6},{8,9},{9,8},{10,11... | collective-permute-start | bytes 98312 | tf_op jit(solution)/shard_map/ppermute | solution.py:197
  78.2 9.1 %collective-permute-done.1.other_ref = bf16[128,128]{1,0:T(8,128)(2,1)S(1)} collective-permute-done((bf16[128,128]{1,0:T(8,128)(2,1)S(1)}, bf16[128,128]{1,0:T(8,128)(2,1)S(1)}, u32[]{:S(2)}, u32[]{:S(2)}) %collective-permute-start.1) | collective-permute-done | bytes 32800 | tf_op jit(solution)/shard_map/ppermute | solution.py:197
  87.3 7.3 %shard_map.94 = (bf16[128,32]{1,0:T(8,128)(2,1)S(1)}, bf16[16,272,128]{2,1,0:T(8,128)(2,1)S(1)}, bf16[16,272,128]{2,1,0:T(8,128)(2,1)S(1)}) custom-call(s32[32]{0:T(128)S(1)} %bitcast.24, bf16[128,128]{1,0:T(8,128)(2,1)S(1)} %reduce_sum.12.sum_ref, bf16[128,128]{1,0:T(8,128)(2,1)S(1)} %collective-permute-done.1.other_ref, ...), custom_call_target="tpu_custom_call" | custom-call | tf_op jit(solution)/shard_map/pallas_call | solution.py:183
  94.6 1.9 %collective-permute-start.3 = (bf16[16,272,128]{2,1,0:T(8,128)(2,1)S(1)}, bf16[16,272,128]{2,1,0:T(8,128)(2,1)S(1)}, u32[]{:S(2)}, u32[]{:S(2)}) collective-permute-start(bf16[16,272,128]{2,1,0:T(8,128)(2,1)S(1)} %get-tuple-element.12), channel_id=1, source_target_pairs={{0,8},{8,0},{1,9},{9,1},{2,10},{10,2},{3,11},{11,3},{4,12},{12,4},... | collective-permute-start | bytes 3342344 | tf_op jit(solution)/shard_map/ppermute | solution.py:197
  96.6 2.7 %collective-permute-done.3 = bf16[16,272,128]{2,1,0:T(8,128)(2,1)S(1)} collective-permute-done((bf16[16,272,128]{2,1,0:T(8,128)(2,1)S(1)}, bf16[16,272,128]{2,1,0:T(8,128)(2,1)S(1)}, u32[]{:S(2)}, u32[]{:S(2)}) %collective-permute-start.3) | collective-permute-done | bytes 1114144 | tf_op jit(solution)/shard_map/ppermute | solution.py:197
  99.3 0.3 add_convert_fusion
  99.6 22.9 %all_to_all.37.in_ref = bf16[16,272,128]{2,1,0:T(8,128)(2,1)S(1)} all-to-all(bf16[16,272,128]{2,1,0:T(8,128)(2,1)S(1)} %add_convert_fusion), channel_id=1, replica_groups=mesh['y'=4,'zl'=8,'c'=2,'x'=4,'zh'=2] {'y','x'}, dimensions={0} | all-to-all | bytes 2228224 | tf_op jit(solution)/shard_map/all_to_all | solution.py:193
  122.5 0.1 shard_map.95
  122.6 23.4 %all_to_all.38.in_ref = bf16[16,48,128]{2,1,0:T(8,128)(2,1)S(1)} all-to-all(bf16[16,48,128]{2,1,0:T(8,128)(2,1)S(1)} %bitcast.21), channel_id=1, replica_groups=mesh['y'=4,'zl'=8,'c'=2,'x'=4,'zh'=2] {'zl','zh'}, dimensions={0} | all-to-all | bytes 393216 | tf_op jit(solution)/shard_map/all_to_all | solution.py:193
  146.1 0.7 shard_map.96
  146.8 3.7 %all-to-all-start.6 = ((bf16[16,48,128]{2,1,0:T(8,128)(2,1)}), bf16[16,48,128]{2,1,0:T(8,128)(2,1)S(1)}, u32[]{:S(2)}, u32[]{:S(2)}) async-start(bf16[16,48,128]{2,1,0:T(8,128)(2,1)} %shard_map.96), calls=%async_computation.6 | async-start | bytes 393216 | tf_op jit(solution)/shard_map/all_to_all | solution.py:193
  150.5 0.7 copy.10
  151.2 7.7 %all-to-all-done.6.in_ref = bf16[16,48,128]{2,1,0:T(8,128)(2,1)S(1)} async-done(((bf16[16,48,128]{2,1,0:T(8,128)(2,1)}), bf16[16,48,128]{2,1,0:T(8,128)(2,1)S(1)}, u32[]{:S(2)}, u32[]{:S(2)}) %all-to-all-start.6) | async-done | bytes 196640 | tf_op jit(solution)/shard_map/all_to_all | solution.py:193
  158.8 0.6 shard_map.97
  159.5 0.7 copy.11
  (15 shorter events, 0.1 us)
Async XLA Ops:
  0.6 0.8 copy-start
  23.3 25.0 %copy-start.2 = (f32[32]{0:T(128)S(1)}, f32[32]{0:T(128)}, u32[]{:S(2)}) copy-start(f32[32]{0:T(128)} %param.10) | copy-start | bytes 388
  23.3 25.1 %copy-start.4 = (bf16[128,32]{0,1:T(8,128)(2,1)S(1)}, bf16[128,32]{0,1:T(8,128)(2,1)}, u32[]{:S(2)}) copy-start(bf16[128,32]{0,1:T(8,128)(2,1)} %param.11) | copy-start | bytes 24580
  23.3 25.1 %copy-start.5 = (bf16[128,32]{0,1:T(8,128)(2,1)S(1)}, bf16[128,32]{0,1:T(8,128)(2,1)}, u32[]{:S(2)}) copy-start(bf16[128,32]{0,1:T(8,128)(2,1)} %param.9) | copy-start | bytes 24580
  23.3 33.3 %copy-start.1 = (bf16[1,1,32,128,128]{4,3,2,1,0:T(8,128)(2,1)S(1)}, bf16[1,1,32,128,128]{4,3,2,1,0:T(8,128)(2,1)}, u32[]{:S(2)}) copy-start(bf16[1,1,32,128,128]{4,3,2,1,0:T(8,128)(2,1)} %param.7) | copy-start | bytes 3145732
  23.4 33.3 %copy-start.3 = (s32[1,1,32]{2,1,0:T(1,128)S(1)}, s32[1,1,32]{2,1,0:T(1,128)}, u32[]{:S(2)}) copy-start(s32[1,1,32]{2,1,0:T(1,128)} %param.8) | copy-start | bytes 388
  46.4 10.2 %collective-permute-start = (bf16[4,4,8,32,128]{4,3,2,1,0:T(8,128)(2,1)S(1)}, bf16[4,4,8,32,128]{4,3,2,1,0:T(8,128)(2,1)S(1)}, u32[]{:S(2)}, u32[]{:S(2)}) collective-permute-start(bf16[4,4,8,32,128]{4,3,2,1,0:T(8,128)(2,1)S(1)} %bitcast.19), channel_id=1, source_target_pairs={{0,8},{8,0},{1,9},{9,1},{2,10},{10,2},{3,11},{11,3},{4,12},{12,4},... | collective-permute-start | bytes 3145736 | tf_op jit(solution)/shard_map/ppermute | solution.py:197
  48.4 15.0 %collective-permute-start.2 = (bf16[80,128]{1,0:T(8,128)(2,1)S(1)}, bf16[80,128]{1,0:T(8,128)(2,1)S(1)}, u32[]{:S(2)}, u32[]{:S(2)}) collective-permute-start(bf16[80,128]{1,0:T(8,128)(2,1)S(1)} %get-tuple-element.21.pack_ref), channel_id=1, source_target_pairs={{0,1},{1,0},{2,3},{3,2},{4,5},{5,4},{6,7},{7,6},{8,9},{9,8},{10,11... | collective-permute-start | bytes 61448 | tf_op jit(solution)/shard_map/ppermute | solution.py:197
  58.5 9.3 %all-to-all-start.2 = ((bf16[4,128,128]{2,1,0:T(8,128)(2,1)}), bf16[4,128,128]{2,1,0:T(8,128)(2,1)S(1)}, u32[]{:S(2)}, u32[]{:S(2)}) async-start(bf16[4,128,128]{2,1,0:T(8,128)(2,1)} %shard_map.93), calls=%async_computation.2 | async-start | bytes 262144 | tf_op jit(solution)/shard_map/all_to_all | solution.py:193
  68.5 9.7 %all-to-all-start.3 = ((bf16[4,2,80,128]{3,2,1,0:T(8,128)(2,1)}), bf16[4,2,80,128]{3,2,1,0:T(8,128)(2,1)S(1)}, u32[]{:S(2)}, u32[]{:S(2)}) async-start(bf16[4,2,80,128]{3,2,1,0:T(8,128)(2,1)} %broadcast_in_dim.10), calls=%async_computation.3 | async-start | bytes 327680 | tf_op jit(solution)/shard_map/all_to_all | solution.py:193
  71.9 15.5 %collective-permute-start.1 = (bf16[128,128]{1,0:T(8,128)(2,1)S(1)}, bf16[128,128]{1,0:T(8,128)(2,1)S(1)}, u32[]{:S(2)}, u32[]{:S(2)}) collective-permute-start(bf16[128,128]{1,0:T(8,128)(2,1)S(1)} %reduce_sum.12.sum_ref), channel_id=1, source_target_pairs={{0,1},{1,0},{2,3},{3,2},{4,5},{5,4},{6,7},{7,6},{8,9},{9,8},{10,11... | collective-permute-start | bytes 98312 | tf_op jit(solution)/shard_map/ppermute | solution.py:197
  94.6 4.6 %collective-permute-start.3 = (bf16[16,272,128]{2,1,0:T(8,128)(2,1)S(1)}, bf16[16,272,128]{2,1,0:T(8,128)(2,1)S(1)}, u32[]{:S(2)}, u32[]{:S(2)}) collective-permute-start(bf16[16,272,128]{2,1,0:T(8,128)(2,1)S(1)} %get-tuple-element.12), channel_id=1, source_target_pairs={{0,8},{8,0},{1,9},{9,1},{2,10},{10,2},{3,11},{11,3},{4,12},{12,4},... | collective-permute-start | bytes 3342344 | tf_op jit(solution)/shard_map/ppermute | solution.py:197
  146.8 12.1 %all-to-all-start.6 = ((bf16[16,48,128]{2,1,0:T(8,128)(2,1)}), bf16[16,48,128]{2,1,0:T(8,128)(2,1)S(1)}, u32[]{:S(2)}, u32[]{:S(2)}) async-start(bf16[16,48,128]{2,1,0:T(8,128)(2,1)} %shard_map.96), calls=%async_computation.6 | async-start | bytes 393216 | tf_op jit(solution)/shard_map/all_to_all | solution.py:193

commit v2 on v1

--- a/solution.py
+++ b/solution.py
@@ -33,10 +33,11 @@
     return src // (2 * zl_n), (src // 2) % zl_n, src % 2
 
 
-def forward_kernel(zl_n, x_n, src_ref, tiles_ref, own_ref, oth_ref, out_ref):
+def forward_kernel(zl_n, x_n, src_ref, tiles_ref, own_ref, oth_ref, pack_ref, pack_other_ref, out_ref):
     my_c = lax.axis_index("c")
     tile = tiles_ref.shape[-1]
     feat = own_ref.shape[-1]
+    size = pack_ref.shape[0]
     acc = jnp.zeros((tile, feat), F32)
     n = tiles_ref.shape[0]
     for k in range(0, n, 2):
@@ -50,79 +51,69 @@
         acc = acc + mm(lhs, jnp.concatenate(blocks, axis=0), 1, 0)
     part = acc.astype(BF16)
     for x in range(x_n):
-        out_ref[x] = part
-
-
-def backward_kernel(
-    zl_n, src_ref, sum_ref, other_ref, packs_ref, pack_ref, bias_ref, tiles_ref, act_ref, own_ref, oth_ref
-):
+        out_ref[x, :tile, :] = part
+        out_ref[x, tile : tile + size, :] = pack_ref[...]
+        out_ref[x, tile + size :, :] = pack_other_ref[...]
+
+
+def backward_kernel(zl_n, src_ref, sum_ref, other_ref, packs_ref, pack_ref, tiles_ref, act_ref, out_ref):
     my_c = lax.axis_index("c")
-    x_n, zh_n = packs_ref.shape[:2]
-    hidden = bias_ref.shape[1]
+    x_n = packs_ref.shape[0]
+    hidden = act_ref.shape[0]
     tile = tiles_ref.shape[-1]
-    y_n = own_ref.shape[0] // x_n
+    size = pack_ref.shape[0]
+    y_n = out_ref.shape[1] // x_n
     rows = tile // x_n
     agg = (sum_ref[...].astype(F32) + other_ref[...].astype(F32)).astype(BF16)
-
-    def gather(start, size):
-        parts = [packs_ref[x, z, start : start + size, :] for x in range(x_n) for z in range(zh_n)]
-        return jnp.concatenate(parts, axis=0)
+    starts = [(x, tile + z * size) for x in range(x_n) for z in range(2)]
+
+    def gather(start, count):
+        return jnp.concatenate([packs_ref[x, at + start : at + start + count, :] for x, at in starts], axis=0)
 
     def bias_of(three):
         return mm(three, jnp.ones((three.shape[0], tile), BF16), 0, 0)[:hidden]
 
     w_t = gather(0, hidden)
     cot_t = gather(hidden, hidden)
-    bias_t = jnp.concatenate(
-        [bias_of(packs_ref[x, z, 2 * hidden :, :]) for x in range(x_n) for z in range(zh_n)], axis=0
-    )
+    bias_t = jnp.concatenate([bias_of(packs_ref[x, at + 2 * hidden : at + size, :]) for x, at in starts], axis=0)
     pre_t = mm(w_t, agg, 1, 1) + bias_t
     grad_t = (cot_t.astype(F32) * slope(pre_t)).astype(BF16)
-    back = mm(grad_t, w_t, 0, 0).astype(BF16)
+    back_t = mm(w_t, grad_t, 0, 0).astype(BF16)
 
     w_mine = pack_ref[0:hidden, :]
-    pre = mm(agg, w_mine, 1, 1) + bias_ref[...]
-    t = jnp.tanh(SCALE * (pre + CUBIC * (pre * pre * pre)))
-    act_ref[...] = (pre * (0.5 * (1.0 + t))).astype(BF16)
     mine_t = mm(w_mine, agg, 1, 1) + bias_of(pack_ref[2 * hidden :, :])
+    t = jnp.tanh(SCALE * (mine_t + CUBIC * (mine_t * mine_t * mine_t)))
+    act_ref[...] = (mine_t * (0.5 * (1.0 + t))).astype(BF16)
     grad_mine = (pack_ref[hidden : 2 * hidden, :].astype(F32) * slope(mine_t)).astype(BF16)
-    wgrad = mm(grad_mine, agg, 1, 0).astype(BF16)
+    wgrad = mm(grad_mine, agg, 1, 0)
     bgrad = mm(jnp.ones((8, tile), BF16), grad_mine, 1, 1)
-    bgrad = jnp.concatenate([bgrad, jnp.zeros((8, tile - hidden), F32)], axis=1).astype(BF16)
+    bgrad = jnp.concatenate([bgrad, jnp.zeros((8, tile - hidden), F32)], axis=1)
 
     body = zl_n * rows
     share = hidden // y_n
     assert share <= 8
-    own_ref[:, :body, :] = jnp.zeros((y_n * x_n, body, tile), BF16)
-    oth_ref[:, :body, :] = jnp.zeros((y_n * x_n, body, tile), BF16)
+    out_ref[:, :, :body, :] = jnp.zeros((2, y_n * x_n, body, tile), BF16)
     for y in range(y_n):
-        piece = [wgrad[y * share : (y + 1) * share].astype(F32), bgrad.astype(F32)]
+        piece = [wgrad[y * share : (y + 1) * share], bgrad]
         if share < 8:
             piece.insert(1, jnp.zeros((8 - share, tile), F32))
         piece = jnp.concatenate(piece, axis=0).astype(BF16)
         for x in range(x_n):
-            own_ref[y * x_n + x, body:, :] = piece
-            oth_ref[y * x_n + x, body:, :] = piece
-
-    acc = jnp.zeros((tile, tile), F32)
-    for k in range(tiles_ref.shape[0]):
-        src = src_ref[k]
-        contrib = mm(tiles_ref[k], back, 0, 0)
-        if k:
-            acc = contrib + jnp.where(src == src_ref[k - 1], acc, 0.0)
-        else:
+            out_ref[0, y * x_n + x, body:, :] = piece
+            out_ref[1, y * x_n + x, body:, :] = piece
+
+    acc = None
+    for k in range(0, tiles_ref.shape[0], 2):
+        pair = mm(back_t, jnp.concatenate([tiles_ref[k], tiles_ref[k + 1]], axis=1), 1, 0)
+        for q, contrib in ((k, pair[:, :tile]), (k + 1, pair[:, tile:])):
+            src = src_ref[q]
+            if q:
+                contrib = contrib + jnp.where(src == src_ref[q - 1], acc, 0.0)
             acc = contrib
-        y, zl, c = place(src, zl_n)
-        out = acc.astype(BF16).reshape(x_n, rows, tile)
-        at = (pl.ds(y * x_n, x_n), pl.ds(pl.multiple_of(zl * rows, rows), rows), slice(None))
-
-        @pl.when(c == my_c)
-        def _():
-            own_ref[at] = out
-
-        @pl.when(c != my_c)
-        def _():
-            oth_ref[at] = out
+            y, zl, c = place(src, zl_n)
+            away = jnp.where(c == my_c, 0, 1)
+            at = (pl.ds(away, 1), pl.ds(y * x_n, x_n), pl.ds(pl.multiple_of(zl * rows, rows), rows), slice(None))
+            out_ref[at] = acc.astype(BF16).reshape(1, x_n, rows, tile)
 
 
 def plane_sum_kernel(y_n, x_n, in_ref, out_ref):
@@ -163,10 +154,11 @@
     rows = in_ref.shape[1] - EXTRA
     hidden = bgrad_ref.shape[1]
     share = hidden // y_n
-    for x in range(x_n):
-        feat_ref[x * rows : (x + 1) * rows, :] = in_ref[my_y * x_n + x, :rows, :].astype(F32)
+    feat_ref[...] = jnp.concatenate(
+        [in_ref[my_y * x_n + x, :rows, :].astype(F32) for x in range(x_n)], axis=0
+    ).T
     pieces = [in_ref[y * x_n + my_x, rows:, :].astype(F32) for y in range(y_n)]
-    wgrad_ref[...] = jnp.concatenate([p[:share] for p in pieces], axis=0).T
+    wgrad_ref[...] = jnp.concatenate([p[:share] for p in pieces], axis=0)
     bgrad_ref[...] = pieces[0][8:9, :hidden]
 
 
@@ -205,7 +197,7 @@
     rows = tile // x_n
     tiles = tile_values.reshape(-1, tile, tile)
     sources = tile_block.reshape(-1)
-    my_x, my_zh = lax.axis_index("x"), lax.axis_index("zh")
+    my_x = lax.axis_index("x")
 
     b_hi = bias.astype(BF16)
     b_mid = (bias - b_hi.astype(F32)).astype(BF16)
@@ -216,32 +208,41 @@
 
     mine = lax.dynamic_slice_in_dim(features, my_x * rows, rows, 0)
     column = to_all(jnp.broadcast_to(mine[None], (zl_n, rows, feat)), "zl")
-    pair = jnp.where(my_zh == 0, jnp.stack([pack, pack_other]), jnp.stack([pack_other, pack]))
-    packs = to_all(jnp.broadcast_to(pair[None], (x_n,) + pair.shape), "x")
+    column, pack_other = lax.optimization_barrier((column, pack_other))
     plane = to_all(jnp.broadcast_to(column[None], (y_n * x_n, zl_n, rows, feat)), ("y", "x"))
     own = plane.reshape(y_n, x_n, zl_n, rows, feat)
     other = swap(own, "c")
 
-    part = call(
-        functools.partial(forward_kernel, zl_n, x_n), shape(x_n, tile, feat), sources, tiles, own, other, smem=1
-    )
-    summed = jnp.sum(to_all(part, "x").astype(F32), axis=0).astype(BF16)
+    size = pack.shape[0]
+    part = to_all(
+        call(
+            functools.partial(forward_kernel, zl_n, x_n),
+            shape(x_n, tile + 2 * size, feat),
+            sources,
+            tiles,
+            own,
+            other,
+            pack,
+            pack_other,
+            smem=1,
+        ),
+        "x",
+    )
+    summed = jnp.sum(part[:, :tile].astype(F32), axis=0).astype(BF16)
     summed_other = swap(summed, "zh")
 
-    payload = shape(y_n * x_n, zl_n * rows + EXTRA, feat)
-    activations, keep, give = call(
+    act_t, pieces = call(
         functools.partial(backward_kernel, zl_n),
-        (shape(tile, hidden), payload, payload),
+        (shape(hidden, tile), shape(2, y_n * x_n, zl_n * rows + EXTRA, feat)),
         sources,
         summed,
         summed_other,
-        packs,
+        part,
         pack,
-        bias[None],
         tiles,
         smem=1,
     )
-    both = (keep.astype(F32) + swap(give, "c").astype(F32)).astype(BF16)
+    both = (pieces[0].astype(F32) + swap(pieces[1], "c").astype(F32)).astype(BF16)
     across = to_all(both, ("y", "x"))
     up = call(
         functools.partial(plane_sum_kernel, y_n, x_n), shape(zl_n, zh_n, rows + EXTRA, feat), across
@@ -250,12 +251,12 @@
     last = call(
         functools.partial(column_sum_kernel, zl_n, zh_n), shape(y_n * x_n, rows + EXTRA, feat), down
     )
-    feature_grad, weight_grad, bias_grad = call(
+    feature_grad, wgrad_t, bias_grad = call(
         functools.partial(finish_kernel, y_n, x_n),
-        (shape(tile, feat, dtype=F32), shape(feat, hidden, dtype=F32), shape(1, hidden, dtype=F32)),
+        (shape(tile, feat, dtype=F32), shape(hidden, feat, dtype=F32), shape(1, hidden, dtype=F32)),
         to_all(last, ("y", "x")),
     )
-    return activations, feature_grad, weight_grad, bias_grad[0]
+    return act_t.T, feature_grad, wgrad_t.T, bias_grad[0]
 
 
 def split_mesh(mesh, sizes):

time: 161 us -> 152 us (0.944)
  waiting for transfers between devices: 25.4 us -> 18.4 us
  Pallas kernels: 10.6 us -> 4.39 us
  starting transfers between devices: 28.8 us -> 32.9 us
    all_to_all x3 -> x1, waiting for transfers between devices: 12 us -> 0.01 us  [to_all(): return lax.all_to_all(v, axes, 0, 0, tiled=True)]
    pallas_call x5, Pallas kernels: 10.6 us -> 4.39 us  [call(): pl.pallas_call(kernel, out_shape=out, in_specs=[SMEM] * smem + [VMEM] * (...]
    ppermute x4, waiting for transfers between devices: 13.4 us -> 18.4 us  [swap(): return lax.ppermute(v, axis, [(0, 1), (1, 0)])]
    all_to_all x3 -> x1, starting transfers between devices: 10.4 us -> 12.6 us  [to_all(): return lax.all_to_all(v, axes, 0, 0, tiled=True)]
    ppermute x4, starting transfers between devices: 18.4 us -> 20.2 us  [swap(): return lax.ppermute(v, axis, [(0, 1), (1, 0)])]
    all_to_all x4 -> x5, blocking collectives: 91.1 us -> 91.7 us  [to_all(): return lax.all_to_all(v, axes, 0, 0, tiled=True)]
  transfers between devices with their start and end apart: 7 -> 5, of which waited for: 5 -> 4; matrix products, arithmetic and copies ran while one was open for 0% -> 1% of each run, Pallas kernels for 1% -> 0%
where the time goes in v2:
time: 152 us
  blocking collectives  91.7 us (60%)
  starting transfers between devices  32.9 us (22%)
  waiting for transfers between devices  18.4 us (12%)
  Pallas kernels  4.39 us (3%)
  other arithmetic  1.78 us (1%)
  local copies, waits for them, and re-layouts  1.67 us (1%)
    all_to_all x5, blocking collectives, to_all(): return lax.all_to_all(v, axes, 0, 0, tiled=True)  91.7 us
    ppermute x4, starting transfers between devices, swap(): return lax.ppermute(v, axis, [(0, 1), (1, 0)])  20.2 us
    ppermute x4, waiting for transfers between devices, swap(): return lax.ppermute(v, axis, [(0, 1), (1, 0)])  18.4 us
    all_to_all x1, starting transfers between devices, to_all(): return lax.all_to_all(v, axes, 0, 0, tiled=True)  12.6 us
    pallas_call x5, Pallas kernels, call(): pl.pallas_call(kernel, out_shape=out, in_specs=[SMEM] * smem + [VMEM] * (...  4.39 us
  transfers between devices with their start and end apart: 5, of which 4 were waited for; matrix products, arithmetic and copies ran while one was open for 1% of the time, Pallas kernels for 0%

profile of v2, /device:TPU:32, one launch (start us, length us, event | category | flops | bytes accessed | tf_op | source)
XLA Modules:
  0.0 151.5 jit_solution(3967542620035019749)
XLA Ops:
  0.6 0.0 copy-start
  0.6 0.7 copy-done
  1.4 0.6 broadcast_in_dim.4
  2.0 12.6 %all-to-all-start = ((bf16[8,32,128]{2,1,0:T(8,128)(2,1)}), bf16[8,32,128]{2,1,0:T(8,128)(2,1)S(1)}, u32[]{:S(2)}, u32[]{:S(2)}) async-start(bf16[8,32,128]{2,1,0:T(8,128)(2,1)} %broadcast_in_dim.4), calls=%async_computation | async-start | bytes 131072 | tf_op jit(solution)/shard_map/all_to_all | solution.py:185
  14.7 0.7 convert_bitcast_fusion.2
  15.4 0.7 pad_maximum_fusion.pack_ref
  16.1 8.2 %collective-permute-start = (bf16[80,128]{1,0:T(8,128)(2,1)S(1)}, bf16[80,128]{1,0:T(8,128)(2,1)S(1)}, u32[]{:S(2)}, u32[]{:S(2)}) collective-permute-start(bf16[80,128]{1,0:T(8,128)(2,1)S(1)} %pad_maximum_fusion.pack_ref), channel_id=1, source_target_pairs={{0,1},{1,0},{2,3},{3,2},{4,5},{5,4},{6,7},{7,6},{8,9},{9,8},{10,11... | collective-permute-start | bytes 61448 | tf_op jit(solution)/shard_map/ppermute | solution.py:189
  24.4 6.4 %collective-permute-done.pack_other_ref = bf16[80,128]{1,0:T(8,128)(2,1)S(1)} collective-permute-done((bf16[80,128]{1,0:T(8,128)(2,1)S(1)}, bf16[80,128]{1,0:T(8,128)(2,1)S(1)}, u32[]{:S(2)}, u32[]{:S(2)}) %collective-permute-start) | collective-permute-done | bytes 20512 | tf_op jit(solution)/shard_map/ppermute | solution.py:189
  30.7 0.0 all-to-all-done
  30.7 0.2 broadcast_in_dim.5
  30.9 0.0 copy-start.1
  31.0 0.0 copy-start.2
  31.0 22.3 %all_to_all.30 = bf16[16,8,32,128]{3,2,1,0:T(8,128)(2,1)S(1)} all-to-all(bf16[16,8,32,128]{3,2,1,0:T(8,128)(2,1)S(1)} %broadcast_in_dim.5), channel_id=1, replica_groups=mesh['y'=4,'zl'=8,'c'=2,'x'=4,'zh'=2] {'y','x'}, dimensions={0} | all-to-all | bytes 2097152 | tf_op jit(solution)/shard_map/all_to_all | solution.py:185
  53.3 1.9 %collective-permute-start.1 = (bf16[4,4,8,32,128]{4,3,2,1,0:T(8,128)(2,1)S(1)}, bf16[4,4,8,32,128]{4,3,2,1,0:T(8,128)(2,1)S(1)}, u32[]{:S(2)}, u32[]{:S(2)}) collective-permute-start(bf16[4,4,8,32,128]{4,3,2,1,0:T(8,128)(2,1)S(1)} %bitcast.22), channel_id=1, source_target_pairs={{0,8},{8,0},{1,9},{9,1},{2,10},{10,2},{3,11},{11,3},{4,12},{12,4},... | collective-permute-start | bytes 3145736 | tf_op jit(solution)/shard_map/ppermute | solution.py:189
  55.2 2.6 %collective-permute-done.1.oth_ref = bf16[4,4,8,32,128]{4,3,2,1,0:T(8,128)(2,1)S(1)} collective-permute-done((bf16[4,4,8,32,128]{4,3,2,1,0:T(8,128)(2,1)S(1)}, bf16[4,4,8,32,128]{4,3,2,1,0:T(8,128)(2,1)S(1)}, u32[]{:S(2)}, u32[]{:S(2)}) %collective-permute-start.1) | collective-permute-done | bytes 1048608 | tf_op jit(solution)/shard_map/ppermute | solution.py:189
  57.8 0.0 copy-done.1
  57.8 0.0 copy-done.2
  57.8 1.2 shard_map.93
  59.0 10.0 %all_to_all.31.packs_ref = bf16[4,288,128]{2,1,0:T(8,128)(2,1)S(1)} all-to-all(bf16[4,288,128]{2,1,0:T(8,128)(2,1)S(1)} %shard_map.93), channel_id=1, replica_groups=mesh['y'=4,'zl'=8,'c'=2,'x'=4,'zh'=2] {'x'}, dimensions={0} | all-to-all | bytes 589824 | tf_op jit(solution)/shard_map/all_to_all | solution.py:185
  69.0 8.2 %collective-permute-start.2 = (bf16[128,128]{1,0:T(8,128)(2,1)S(1)}, bf16[128,128]{1,0:T(8,128)(2,1)S(1)}, u32[]{:S(2)}, u32[]{:S(2)}) collective-permute-start(bf16[128,128]{1,0:T(8,128)(2,1)S(1)} %slice_reduce_fusion.sum_ref), channel_id=1, source_target_pairs={{0,1},{1,0},{2,3},{3,2},{4,5},{5,4},{6,7},{7,6},{8,9},{9,8},{10,11... | collective-permute-start | bytes 98312 | tf_op jit(solution)/shard_map/ppermute | solution.py:189
  77.2 6.7 %collective-permute-done.2.other_ref = bf16[128,128]{1,0:T(8,128)(2,1)S(1)} collective-permute-done((bf16[128,128]{1,0:T(8,128)(2,1)S(1)}, bf16[128,128]{1,0:T(8,128)(2,1)S(1)}, u32[]{:S(2)}, u32[]{:S(2)}) %collective-permute-start.2) | collective-permute-done | bytes 32800 | tf_op jit(solution)/shard_map/ppermute | solution.py:189
  83.9 2.3 %shard_map.94 = (bf16[32,128]{1,0:T(8,128)(2,1)}, bf16[2,16,272,128]{3,2,1,0:T(8,128)(2,1)S(1)}) custom-call(s32[32]{0:T(128)S(1)} %bitcast.26, bf16[128,128]{1,0:T(8,128)(2,1)S(1)} %slice_reduce_fusion.sum_ref, bf16[128,128]{1,0:T(8,128)(2,1)S(1)} %collective-permute-done.2.other_ref, bf16[4,288,128]{2,1,0:T(8,128)(2,1)S(1)} %all_to_all.31.packs_ref, ...), custom_call_target="tpu_custom_call" | custom-call | tf_op jit(solution)/shard_map/pallas_call | solution.py:175
  86.1 0.1 slice_bitcast_fusion
  86.2 1.9 %collective-permute-start.3 = (bf16[16,272,128]{2,1,0:T(8,128)(2,1)S(1)}, bf16[16,272,128]{2,1,0:T(8,128)(2,1)S(1)}, u32[]{:S(2)}, u32[]{:S(2)}) collective-permute-start(bf16[16,272,128]{2,1,0:T(8,128)(2,1)S(1)} %slice_bitcast_fusion), channel_id=1, source_target_pairs={{0,8},{8,0},{1,9},{9,1},{2,10},{10,2},{3,11},{11,3},{4,12},{12,4},... | collective-permute-start | bytes 3342344 | tf_op jit(solution)/shard_map/ppermute | solution.py:189
  88.2 2.7 %collective-permute-done.3 = bf16[16,272,128]{2,1,0:T(8,128)(2,1)S(1)} collective-permute-done((bf16[16,272,128]{2,1,0:T(8,128)(2,1)S(1)}, bf16[16,272,128]{2,1,0:T(8,128)(2,1)S(1)}, u32[]{:S(2)}, u32[]{:S(2)}) %collective-permute-start.3) | collective-permute-done | bytes 1114144 | tf_op jit(solution)/shard_map/ppermute | solution.py:189
  90.9 0.3 fusion
  91.2 21.1 %all_to_all.32.in_ref = bf16[16,272,128]{2,1,0:T(8,128)(2,1)S(1)} all-to-all(bf16[16,272,128]{2,1,0:T(8,128)(2,1)S(1)} %fusion), channel_id=1, replica_groups=mesh['y'=4,'zl'=8,'c'=2,'x'=4,'zh'=2] {'y','x'}, dimensions={0} | all-to-all | bytes 2228224 | tf_op jit(solution)/shard_map/all_to_all | solution.py:185
  112.2 0.1 shard_map.95
  112.4 26.6 %all_to_all.33.in_ref = bf16[16,48,128]{2,1,0:T(8,128)(2,1)S(1)} all-to-all(bf16[16,48,128]{2,1,0:T(8,128)(2,1)S(1)} %bitcast.24), channel_id=1, replica_groups=mesh['y'=4,'zl'=8,'c'=2,'x'=4,'zh'=2] {'zl','zh'}, dimensions={0} | all-to-all | bytes 393216 | tf_op jit(solution)/shard_map/all_to_all | solution.py:185
  139.0 11.8 %all_to_all.34.in_ref = bf16[16,48,128]{2,1,0:T(8,128)(2,1)S(1)} all-to-all(bf16[16,48,128]{2,1,0:T(8,128)(2,1)S(1)} %shard_map.96), channel_id=1, replica_groups=mesh['y'=4,'zl'=8,'c'=2,'x'=4,'zh'=2] {'y','x'}, dimensions={0} | all-to-all | bytes 393216 | tf_op jit(solution)/shard_map/all_to_all | solution.py:185
  150.8 0.7 shard_map.97
  (4 shorter events, 0.1 us)
Async XLA Ops:
  0.6 0.8 copy-start
  2.0 28.7 %all-to-all-start = ((bf16[8,32,128]{2,1,0:T(8,128)(2,1)}), bf16[8,32,128]{2,1,0:T(8,128)(2,1)S(1)}, u32[]{:S(2)}, u32[]{:S(2)}) async-start(bf16[8,32,128]{2,1,0:T(8,128)(2,1)} %broadcast_in_dim.4), calls=%async_computation | async-start | bytes 131072 | tf_op jit(solution)/shard_map/all_to_all | solution.py:185
  16.1 14.6 %collective-permute-start = (bf16[80,128]{1,0:T(8,128)(2,1)S(1)}, bf16[80,128]{1,0:T(8,128)(2,1)S(1)}, u32[]{:S(2)}, u32[]{:S(2)}) collective-permute-start(bf16[80,128]{1,0:T(8,128)(2,1)S(1)} %pad_maximum_fusion.pack_ref), channel_id=1, source_target_pairs={{0,1},{1,0},{2,3},{3,2},{4,5},{5,4},{6,7},{7,6},{8,9},{9,8},{10,11... | collective-permute-start | bytes 61448 | tf_op jit(solution)/shard_map/ppermute | solution.py:189
  30.9 26.9 %copy-start.1 = (bf16[1,1,32,128,128]{4,3,2,1,0:T(8,128)(2,1)S(1)}, bf16[1,1,32,128,128]{4,3,2,1,0:T(8,128)(2,1)}, u32[]{:S(2)}) copy-start(bf16[1,1,32,128,128]{4,3,2,1,0:T(8,128)(2,1)} %param.7) | copy-start | bytes 3145732
  31.0 26.8 %copy-start.2 = (s32[1,1,32]{2,1,0:T(1,128)S(1)}, s32[1,1,32]{2,1,0:T(1,128)}, u32[]{:S(2)}) copy-start(s32[1,1,32]{2,1,0:T(1,128)} %param.8) | copy-start | bytes 388
  53.3 4.5 %collective-permute-start.1 = (bf16[4,4,8,32,128]{4,3,2,1,0:T(8,128)(2,1)S(1)}, bf16[4,4,8,32,128]{4,3,2,1,0:T(8,128)(2,1)S(1)}, u32[]{:S(2)}, u32[]{:S(2)}) collective-permute-start(bf16[4,4,8,32,128]{4,3,2,1,0:T(8,128)(2,1)S(1)} %bitcast.22), channel_id=1, source_target_pairs={{0,8},{8,0},{1,9},{9,1},{2,10},{10,2},{3,11},{11,3},{4,12},{12,4},... | collective-permute-start | bytes 3145736 | tf_op jit(solution)/shard_map/ppermute | solution.py:189
  69.0 14.9 %collective-permute-start.2 = (bf16[128,128]{1,0:T(8,128)(2,1)S(1)}, bf16[128,128]{1,0:T(8,128)(2,1)S(1)}, u32[]{:S(2)}, u32[]{:S(2)}) collective-permute-start(bf16[128,128]{1,0:T(8,128)(2,1)S(1)} %slice_reduce_fusion.sum_ref), channel_id=1, source_target_pairs={{0,1},{1,0},{2,3},{3,2},{4,5},{5,4},{6,7},{7,6},{8,9},{9,8},{10,11... | collective-permute-start | bytes 98312 | tf_op jit(solution)/shard_map/ppermute | solution.py:189
  86.2 4.6 %collective-permute-start.3 = (bf16[16,272,128]{2,1,0:T(8,128)(2,1)S(1)}, bf16[16,272,128]{2,1,0:T(8,128)(2,1)S(1)}, u32[]{:S(2)}, u32[]{:S(2)}) collective-permute-start(bf16[16,272,128]{2,1,0:T(8,128)(2,1)S(1)} %slice_bitcast_fusion), channel_id=1, source_target_pairs={{0,8},{8,0},{1,9},{9,1},{2,10},{10,2},{3,11},{11,3},{4,12},{12,4},... | collective-permute-start | bytes 3342344 | tf_op jit(solution)/shard_map/ppermute | solution.py:189

commit v3 on v2

--- a/solution.py
+++ b/solution.py
@@ -204,12 +204,12 @@
     b_lo = (bias - b_hi.astype(F32) - b_mid.astype(F32)).astype(BF16)
     terms = jnp.pad(jnp.stack([b_hi, b_mid, b_lo]), ((0, 13), (0, feat - hidden)))
     pack = jnp.concatenate([weight.T, cotangent.T, terms], axis=0)
-    pack_other = swap(pack, "zh")
-
     mine = lax.dynamic_slice_in_dim(features, my_x * rows, rows, 0)
     column = to_all(jnp.broadcast_to(mine[None], (zl_n, rows, feat)), "zl")
-    column, pack_other = lax.optimization_barrier((column, pack_other))
+    column, pack = lax.optimization_barrier((column, pack))
+    pack_other = swap(pack, "zh")
     plane = to_all(jnp.broadcast_to(column[None], (y_n * x_n, zl_n, rows, feat)), ("y", "x"))
+    plane, pack_other = lax.optimization_barrier((plane, pack_other))
     own = plane.reshape(y_n, x_n, zl_n, rows, feat)
     other = swap(own, "c")
 

time: 152 us -> 149 us (0.980)
  blocking collectives: 91.7 us -> 70.3 us
  waiting for transfers between devices: 18.4 us -> 28 us
  starting transfers between devices: 32.9 us -> 40.1 us
    all_to_all x5 -> x4, blocking collectives: 91.7 us -> 70.3 us  [to_all(): return lax.all_to_all(v, axes, 0, 0, tiled=True)]
    all_to_all x1 -> x2, waiting for transfers between devices: 0.01 us -> 9.17 us  [to_all(): return lax.all_to_all(v, axes, 0, 0, tiled=True)]
    all_to_all x1 -> x2, starting transfers between devices: 12.6 us -> 19.8 us  [to_all(): return lax.all_to_all(v, axes, 0, 0, tiled=True)]
  transfers between devices with their start and end apart: 5 -> 6, of which waited for: 4 -> 6; matrix products, arithmetic and copies ran while one was open for 1% -> 1% of each run, Pallas kernels for 0% -> 0%
where the time goes in v3:
time: 149 us; the launch traced here: 148 us
  blocking collectives  70.3 us (47%)
  starting transfers between devices  40.1 us (27%)
  waiting for transfers between devices  28 us (19%)
  Pallas kernels  4.4 us (3%)
  local copies, waits for them, and re-layouts  2.65 us (2%)
  other arithmetic  1.78 us (1%)
    all_to_all x4, blocking collectives, to_all(): return lax.all_to_all(v, axes, 0, 0, tiled=True)  70.3 us
    ppermute x4, starting transfers between devices, swap(): return lax.ppermute(v, axis, [(0, 1), (1, 0)])  20.3 us
    all_to_all x2, starting transfers between devices, to_all(): return lax.all_to_all(v, axes, 0, 0, tiled=True)  19.8 us
    ppermute x4, waiting for transfers between devices, swap(): return lax.ppermute(v, axis, [(0, 1), (1, 0)])  18.9 us
    all_to_all x2, waiting for transfers between devices, to_all(): return lax.all_to_all(v, axes, 0, 0, tiled=True)  9.17 us
    pallas_call x5, Pallas kernels, call(): pl.pallas_call(kernel, out_shape=out, in_specs=[SMEM] * smem + [VMEM] * (...  4.4 us
  transfers between devices with their start and end apart: 6, of which 6 were waited for; matrix products, arithmetic and copies ran while one was open for 1% of the time, Pallas kernels for 0%

profile of v3, /device:TPU:32, one launch (start us, length us, event | category | flops | bytes accessed | tf_op | source)
XLA Modules:
  0.0 147.9 jit_solution(40134867876350752)
XLA Ops:
  0.6 0.0 copy-start
  0.6 0.7 copy-done
  1.4 0.6 broadcast_in_dim.4
  2.0 12.6 %all-to-all-start = ((bf16[8,32,128]{2,1,0:T(8,128)(2,1)}), bf16[8,32,128]{2,1,0:T(8,128)(2,1)S(1)}, u32[]{:S(2)}, u32[]{:S(2)}) async-start(bf16[8,32,128]{2,1,0:T(8,128)(2,1)} %broadcast_in_dim.4), calls=%async_computation | async-start | bytes 131072 | tf_op jit(solution)/shard_map/all_to_all | solution.py:185
  14.7 0.7 convert_bitcast_fusion.2
  15.4 0.7 pad_maximum_fusion.pack_ref
  16.1 7.8 %all-to-all-done = bf16[8,32,128]{2,1,0:T(8,128)(2,1)S(1)} async-done(((bf16[8,32,128]{2,1,0:T(8,128)(2,1)}), bf16[8,32,128]{2,1,0:T(8,128)(2,1)S(1)}, u32[]{:S(2)}, u32[]{:S(2)}) %all-to-all-start) | async-done | bytes 65568 | tf_op jit(solution)/shard_map/all_to_all | solution.py:185
  23.9 1.2 broadcast_in_dim.5
  25.1 0.0 copy-start.1
  25.1 0.0 copy-start.2
  25.1 7.2 %all-to-all-start.1 = ((bf16[16,8,32,128]{3,2,1,0:T(8,128)(2,1)}), bf16[16,8,32,128]{3,2,1,0:T(8,128)(2,1)S(1)}, u32[]{:S(2)}, u32[]{:S(2)}) async-start(bf16[16,8,32,128]{3,2,1,0:T(8,128)(2,1)} %broadcast_in_dim.5), calls=%async_computation.1 | async-start | bytes 2097152 | tf_op jit(solution)/shard_map/all_to_all | solution.py:185
  32.3 8.2 %collective-permute-start = (bf16[80,128]{1,0:T(8,128)(2,1)S(1)}, bf16[80,128]{1,0:T(8,128)(2,1)S(1)}, u32[]{:S(2)}, u32[]{:S(2)}) collective-permute-start(bf16[80,128]{1,0:T(8,128)(2,1)S(1)} %pad_maximum_fusion.pack_ref), channel_id=1, source_target_pairs={{0,1},{1,0},{2,3},{3,2},{4,5},{5,4},{6,7},{7,6},{8,9},{9,8},{10,11... | collective-permute-start | bytes 61448 | tf_op jit(solution)/shard_map/ppermute | solution.py:189
  40.5 6.5 %collective-permute-done.pack_other_ref = bf16[80,128]{1,0:T(8,128)(2,1)S(1)} collective-permute-done((bf16[80,128]{1,0:T(8,128)(2,1)S(1)}, bf16[80,128]{1,0:T(8,128)(2,1)S(1)}, u32[]{:S(2)}, u32[]{:S(2)}) %collective-permute-start) | collective-permute-done | bytes 20512 | tf_op jit(solution)/shard_map/ppermute | solution.py:189
  47.0 1.4 all-to-all-done.1
  48.4 1.9 %collective-permute-start.1 = (bf16[4,4,8,32,128]{4,3,2,1,0:T(8,128)(2,1)S(1)}, bf16[4,4,8,32,128]{4,3,2,1,0:T(8,128)(2,1)S(1)}, u32[]{:S(2)}, u32[]{:S(2)}) collective-permute-start(bf16[4,4,8,32,128]{4,3,2,1,0:T(8,128)(2,1)S(1)} %bitcast.22), channel_id=1, source_target_pairs={{0,8},{8,0},{1,9},{9,1},{2,10},{10,2},{3,11},{11,3},{4,12},{12,4},... | collective-permute-start | bytes 3145736 | tf_op jit(solution)/shard_map/ppermute | solution.py:189
  50.3 2.6 %collective-permute-done.1.oth_ref = bf16[4,4,8,32,128]{4,3,2,1,0:T(8,128)(2,1)S(1)} collective-permute-done((bf16[4,4,8,32,128]{4,3,2,1,0:T(8,128)(2,1)S(1)}, bf16[4,4,8,32,128]{4,3,2,1,0:T(8,128)(2,1)S(1)}, u32[]{:S(2)}, u32[]{:S(2)}) %collective-permute-start.1) | collective-permute-done | bytes 1048608 | tf_op jit(solution)/shard_map/ppermute | solution.py:189
  52.9 0.0 copy-done.1
  52.9 0.0 copy-done.2
  53.0 1.2 shard_map.93
  54.2 10.4 %all_to_all.30.packs_ref = bf16[4,288,128]{2,1,0:T(8,128)(2,1)S(1)} all-to-all(bf16[4,288,128]{2,1,0:T(8,128)(2,1)S(1)} %shard_map.93), channel_id=1, replica_groups=mesh['y'=4,'zl'=8,'c'=2,'x'=4,'zh'=2] {'x'}, dimensions={0} | all-to-all | bytes 589824 | tf_op jit(solution)/shard_map/all_to_all | solution.py:185
  64.6 8.2 %collective-permute-start.2 = (bf16[128,128]{1,0:T(8,128)(2,1)S(1)}, bf16[128,128]{1,0:T(8,128)(2,1)S(1)}, u32[]{:S(2)}, u32[]{:S(2)}) collective-permute-start(bf16[128,128]{1,0:T(8,128)(2,1)S(1)} %slice_reduce_fusion.sum_ref), channel_id=1, source_target_pairs={{0,1},{1,0},{2,3},{3,2},{4,5},{5,4},{6,7},{7,6},{8,9},{9,8},{10,11... | collective-permute-start | bytes 98312 | tf_op jit(solution)/shard_map/ppermute | solution.py:189
  72.9 7.0 %collective-permute-done.2.other_ref = bf16[128,128]{1,0:T(8,128)(2,1)S(1)} collective-permute-done((bf16[128,128]{1,0:T(8,128)(2,1)S(1)}, bf16[128,128]{1,0:T(8,128)(2,1)S(1)}, u32[]{:S(2)}, u32[]{:S(2)}) %collective-permute-start.2) | collective-permute-done | bytes 32800 | tf_op jit(solution)/shard_map/ppermute | solution.py:189
  79.9 2.3 %shard_map.94 = (bf16[32,128]{1,0:T(8,128)(2,1)}, bf16[2,16,272,128]{3,2,1,0:T(8,128)(2,1)S(1)}) custom-call(s32[32]{0:T(128)S(1)} %bitcast.26, bf16[128,128]{1,0:T(8,128)(2,1)S(1)} %slice_reduce_fusion.sum_ref, bf16[128,128]{1,0:T(8,128)(2,1)S(1)} %collective-permute-done.2.other_ref, bf16[4,288,128]{2,1,0:T(8,128)(2,1)S(1)} %all_to_all.30.packs_ref, ...), custom_call_target="tpu_custom_call" | custom-call | tf_op jit(solution)/shard_map/pallas_call | solution.py:175
  82.2 0.1 slice_bitcast_fusion
  82.2 1.9 %collective-permute-start.3 = (bf16[16,272,128]{2,1,0:T(8,128)(2,1)S(1)}, bf16[16,272,128]{2,1,0:T(8,128)(2,1)S(1)}, u32[]{:S(2)}, u32[]{:S(2)}) collective-permute-start(bf16[16,272,128]{2,1,0:T(8,128)(2,1)S(1)} %slice_bitcast_fusion), channel_id=1, source_target_pairs={{0,8},{8,0},{1,9},{9,1},{2,10},{10,2},{3,11},{11,3},{4,12},{12,4},... | collective-permute-start | bytes 3342344 | tf_op jit(solution)/shard_map/ppermute | solution.py:189
  84.2 2.7 %collective-permute-done.3 = bf16[16,272,128]{2,1,0:T(8,128)(2,1)S(1)} collective-permute-done((bf16[16,272,128]{2,1,0:T(8,128)(2,1)S(1)}, bf16[16,272,128]{2,1,0:T(8,128)(2,1)S(1)}, u32[]{:S(2)}, u32[]{:S(2)}) %collective-permute-start.3) | collective-permute-done | bytes 1114144 | tf_op jit(solution)/shard_map/ppermute | solution.py:189
  86.9 0.3 fusion
  87.2 22.9 %all_to_all.31.in_ref = bf16[16,272,128]{2,1,0:T(8,128)(2,1)S(1)} all-to-all(bf16[16,272,128]{2,1,0:T(8,128)(2,1)S(1)} %fusion), channel_id=1, replica_groups=mesh['y'=4,'zl'=8,'c'=2,'x'=4,'zh'=2] {'y','x'}, dimensions={0} | all-to-all | bytes 2228224 | tf_op jit(solution)/shard_map/all_to_all | solution.py:185
  110.0 0.1 shard_map.95
  110.2 25.1 %all_to_all.32.in_ref = bf16[16,48,128]{2,1,0:T(8,128)(2,1)S(1)} all-to-all(bf16[16,48,128]{2,1,0:T(8,128)(2,1)S(1)} %bitcast.24), channel_id=1, replica_groups=mesh['y'=4,'zl'=8,'c'=2,'x'=4,'zh'=2] {'zl','zh'}, dimensions={0} | all-to-all | bytes 393216 | tf_op jit(solution)/shard_map/all_to_all | solution.py:185
  135.3 11.8 %all_to_all.33.in_ref = bf16[16,48,128]{2,1,0:T(8,128)(2,1)S(1)} all-to-all(bf16[16,48,128]{2,1,0:T(8,128)(2,1)S(1)} %shard_map.96), channel_id=1, replica_groups=mesh['y'=4,'zl'=8,'c'=2,'x'=4,'zh'=2] {'y','x'}, dimensions={0} | all-to-all | bytes 393216 | tf_op jit(solution)/shard_map/all_to_all | solution.py:185
  147.2 0.7 shard_map.97
  (4 shorter events, 0.1 us)
Async XLA Ops:
  0.6 0.8 copy-start
  2.0 21.9 %all-to-all-start = ((bf16[8,32,128]{2,1,0:T(8,128)(2,1)}), bf16[8,32,128]{2,1,0:T(8,128)(2,1)S(1)}, u32[]{:S(2)}, u32[]{:S(2)}) async-start(bf16[8,32,128]{2,1,0:T(8,128)(2,1)} %broadcast_in_dim.4), calls=%async_computation | async-start | bytes 131072 | tf_op jit(solution)/shard_map/all_to_all | solution.py:185
  25.1 27.8 %copy-start.1 = (bf16[1,1,32,128,128]{4,3,2,1,0:T(8,128)(2,1)S(1)}, bf16[1,1,32,128,128]{4,3,2,1,0:T(8,128)(2,1)}, u32[]{:S(2)}) copy-start(bf16[1,1,32,128,128]{4,3,2,1,0:T(8,128)(2,1)} %param.7) | copy-start | bytes 3145732
  25.1 27.8 %copy-start.2 = (s32[1,1,32]{2,1,0:T(1,128)S(1)}, s32[1,1,32]{2,1,0:T(1,128)}, u32[]{:S(2)}) copy-start(s32[1,1,32]{2,1,0:T(1,128)} %param.8) | copy-start | bytes 388
  25.1 23.3 %all-to-all-start.1 = ((bf16[16,8,32,128]{3,2,1,0:T(8,128)(2,1)}), bf16[16,8,32,128]{3,2,1,0:T(8,128)(2,1)S(1)}, u32[]{:S(2)}, u32[]{:S(2)}) async-start(bf16[16,8,32,128]{3,2,1,0:T(8,128)(2,1)} %broadcast_in_dim.5), calls=%async_computation.1 | async-start | bytes 2097152 | tf_op jit(solution)/shard_map/all_to_all | solution.py:185
  32.3 14.7 %collective-permute-start = (bf16[80,128]{1,0:T(8,128)(2,1)S(1)}, bf16[80,128]{1,0:T(8,128)(2,1)S(1)}, u32[]{:S(2)}, u32[]{:S(2)}) collective-permute-start(bf16[80,128]{1,0:T(8,128)(2,1)S(1)} %pad_maximum_fusion.pack_ref), channel_id=1, source_target_pairs={{0,1},{1,0},{2,3},{3,2},{4,5},{5,4},{6,7},{7,6},{8,9},{9,8},{10,11... | collective-permute-start | bytes 61448 | tf_op jit(solution)/shard_map/ppermute | solution.py:189
  48.4 4.5 %collective-permute-start.1 = (bf16[4,4,8,32,128]{4,3,2,1,0:T(8,128)(2,1)S(1)}, bf16[4,4,8,32,128]{4,3,2,1,0:T(8,128)(2,1)S(1)}, u32[]{:S(2)}, u32[]{:S(2)}) collective-permute-start(bf16[4,4,8,32,128]{4,3,2,1,0:T(8,128)(2,1)S(1)} %bitcast.22), channel_id=1, source_target_pairs={{0,8},{8,0},{1,9},{9,1},{2,10},{10,2},{3,11},{11,3},{4,12},{12,4},... | collective-permute-start | bytes 3145736 | tf_op jit(solution)/shard_map/ppermute | solution.py:189
  64.6 15.2 %collective-permute-start.2 = (bf16[128,128]{1,0:T(8,128)(2,1)S(1)}, bf16[128,128]{1,0:T(8,128)(2,1)S(1)}, u32[]{:S(2)}, u32[]{:S(2)}) collective-permute-start(bf16[128,128]{1,0:T(8,128)(2,1)S(1)} %slice_reduce_fusion.sum_ref), channel_id=1, source_target_pairs={{0,1},{1,0},{2,3},{3,2},{4,5},{5,4},{6,7},{7,6},{8,9},{9,8},{10,11... | collective-permute-start | bytes 98312 | tf_op jit(solution)/shard_map/ppermute | solution.py:189
  82.2 4.6 %collective-permute-start.3 = (bf16[16,272,128]{2,1,0:T(8,128)(2,1)S(1)}, bf16[16,272,128]{2,1,0:T(8,128)(2,1)S(1)}, u32[]{:S(2)}, u32[]{:S(2)}) collective-permute-start(bf16[16,272,128]{2,1,0:T(8,128)(2,1)S(1)} %slice_bitcast_fusion), channel_id=1, source_target_pairs={{0,8},{8,0},{1,9},{9,1},{2,10},{10,2},{3,11},{11,3},{4,12},{12,4},... | collective-permute-start | bytes 3342344 | tf_op jit(solution)/shard_map/ppermute | solution.py:189

commit v4 on v3

--- a/solution.py
+++ b/solution.py
@@ -29,41 +29,51 @@
     return 0.5 * (1.0 + t) + 0.5 * v * (1.0 - t * t) * du
 
 
-def place(src, zl_n):
-    return src // (2 * zl_n), (src // 2) % zl_n, src % 2
-
-
-def forward_kernel(zl_n, x_n, src_ref, tiles_ref, own_ref, oth_ref, pack_ref, pack_other_ref, out_ref):
-    my_c = lax.axis_index("c")
-    tile = tiles_ref.shape[-1]
+def dense_kernel(zl_n, src_ref, tiles_ref, out_ref):
+    my_c, my_x = lax.axis_index("c"), lax.axis_index("x")
+    x_n = out_ref.shape[0]
+    out_ref[...] = jnp.zeros_like(out_ref)
+    acc = None
+    for k in range(tiles_ref.shape[0]):
+        src = src_ref[k]
+        piece = tiles_ref[k].astype(F32)
+        if k:
+            piece = piece + jnp.where(src == src_ref[k - 1], acc, 0.0)
+        acc = piece
+        y, zl, c = src // (2 * zl_n), (src // 2) % zl_n, src % 2
+        at = (pl.ds((y + x_n - my_x) % x_n, 1), pl.ds(jnp.where(c == my_c, 0, 1), 1), pl.ds(zl, 1))
+        out_ref[at] = acc.astype(BF16)[None, None, None]
+
+
+def forward_kernel(d0_ref, d1_ref, d2_ref, d3_ref, own_ref, oth_ref, pack_ref, pack_other_ref, a_ref, out_ref):
+    tile = d0_ref.shape[-1]
     feat = own_ref.shape[-1]
     size = pack_ref.shape[0]
+    zl_n = d0_ref.shape[1]
     acc = jnp.zeros((tile, feat), F32)
-    n = tiles_ref.shape[0]
-    for k in range(0, n, 2):
-        blocks = []
-        for q in range(k, k + 2):
-            y, zl, c = place(src_ref[q], zl_n)
-            a = own_ref[pl.ds(y, 1), :, pl.ds(zl, 1)].reshape(tile, feat)
-            b = oth_ref[pl.ds(y, 1), :, pl.ds(zl, 1)].reshape(tile, feat)
-            blocks.append(jnp.where(c == my_c, a, b))
-        lhs = jnp.concatenate([tiles_ref[k], tiles_ref[k + 1]], axis=1)
-        acc = acc + mm(lhs, jnp.concatenate(blocks, axis=0), 1, 0)
+    for core, x_ref in ((0, own_ref), (1, oth_ref)):
+        for zl in range(zl_n):
+            total = d0_ref[core, zl].astype(F32)
+            for ref in (d1_ref, d2_ref, d3_ref)[: out_ref.shape[0] - 1]:
+                total = total + ref[core, zl].astype(F32)
+            total = total.astype(BF16)
+            a_ref[core, zl] = total
+            acc = acc + mm(total, x_ref[:, zl].reshape(tile, feat), 1, 0)
     part = acc.astype(BF16)
-    for x in range(x_n):
+    for x in range(out_ref.shape[0]):
         out_ref[x, :tile, :] = part
         out_ref[x, tile : tile + size, :] = pack_ref[...]
         out_ref[x, tile + size :, :] = pack_other_ref[...]
 
 
-def backward_kernel(zl_n, src_ref, sum_ref, other_ref, packs_ref, pack_ref, tiles_ref, act_ref, out_ref):
-    my_c = lax.axis_index("c")
+def backward_kernel(sum_ref, other_ref, packs_ref, pack_ref, a_ref, act_ref, own_ref, oth_ref):
     x_n = packs_ref.shape[0]
     hidden = act_ref.shape[0]
-    tile = tiles_ref.shape[-1]
+    tile = a_ref.shape[-1]
+    zl_n = a_ref.shape[1]
     size = pack_ref.shape[0]
-    y_n = out_ref.shape[1] // x_n
-    rows = tile // x_n
+    y_n = own_ref.shape[0]
+    rows = tile // y_n
     agg = (sum_ref[...].astype(F32) + other_ref[...].astype(F32)).astype(BF16)
     starts = [(x, tile + z * size) for x in range(x_n) for z in range(2)]
 
@@ -92,47 +102,33 @@
     body = zl_n * rows
     share = hidden // y_n
     assert share <= 8
-    out_ref[:, :, :body, :] = jnp.zeros((2, y_n * x_n, body, tile), BF16)
     for y in range(y_n):
         piece = [wgrad[y * share : (y + 1) * share], bgrad]
         if share < 8:
             piece.insert(1, jnp.zeros((8 - share, tile), F32))
         piece = jnp.concatenate(piece, axis=0).astype(BF16)
-        for x in range(x_n):
-            out_ref[0, y * x_n + x, body:, :] = piece
-            out_ref[1, y * x_n + x, body:, :] = piece
-
-    acc = None
-    for k in range(0, tiles_ref.shape[0], 2):
-        pair = mm(back_t, jnp.concatenate([tiles_ref[k], tiles_ref[k + 1]], axis=1), 1, 0)
-        for q, contrib in ((k, pair[:, :tile]), (k + 1, pair[:, tile:])):
-            src = src_ref[q]
-            if q:
-                contrib = contrib + jnp.where(src == src_ref[q - 1], acc, 0.0)
-            acc = contrib
-            y, zl, c = place(src, zl_n)
-            away = jnp.where(c == my_c, 0, 1)
-            at = (pl.ds(away, 1), pl.ds(y * x_n, x_n), pl.ds(pl.multiple_of(zl * rows, rows), rows), slice(None))
-            out_ref[at] = acc.astype(BF16).reshape(1, x_n, rows, tile)
-
-
-def plane_sum_kernel(y_n, x_n, in_ref, out_ref):
-    my_x = lax.axis_index("x")
+        own_ref[y, body:, :] = piece
+        oth_ref[y, body:, :] = piece
+    for core, out_ref in ((1, oth_ref), (0, own_ref)):
+        for zl in range(0, zl_n, 2):
+            pair = mm(back_t, jnp.concatenate([a_ref[core, zl], a_ref[core, zl + 1]], axis=1), 1, 0).astype(BF16)
+            for y in range(y_n):
+                part = pair[y * rows : (y + 1) * rows]
+                out_ref[y, zl * rows : (zl + 1) * rows, :] = part[:, :tile]
+                out_ref[y, (zl + 1) * rows : (zl + 2) * rows, :] = part[:, tile:]
+
+
+def plane_sum_kernel(in_ref, out_ref):
     zl_n, zh_n, size, _ = out_ref.shape
     rows = size - EXTRA
-    body = zl_n * rows
-    total = in_ref[0, :body, :].astype(F32)
-    for s in range(1, y_n * x_n):
-        total = total + in_ref[s, :body, :].astype(F32)
-    extra = in_ref[my_x, body:, :].astype(F32)
-    for y in range(1, y_n):
-        extra = extra + in_ref[y * x_n + my_x, body:, :].astype(F32)
+    total = in_ref[0].astype(F32)
+    for y in range(1, in_ref.shape[0]):
+        total = total + in_ref[y].astype(F32)
     total = total.astype(BF16)
-    extra = extra.astype(BF16)
     for z in range(zl_n):
         for h in range(zh_n):
             out_ref[z, h, :rows, :] = total[z * rows : (z + 1) * rows]
-            out_ref[z, h, rows:, :] = extra
+            out_ref[z, h, rows:, :] = total[zl_n * rows :]
 
 
 def column_sum_kernel(zl_n, zh_n, in_ref, out_ref):
@@ -155,7 +151,7 @@
     hidden = bgrad_ref.shape[1]
     share = hidden // y_n
     feat_ref[...] = jnp.concatenate(
-        [in_ref[my_y * x_n + x, :rows, :].astype(F32) for x in range(x_n)], axis=0
+        [in_ref[y * x_n + my_y, :rows, :].astype(F32) for y in range(y_n)], axis=0
     ).T
     pieces = [in_ref[y * x_n + my_x, rows:, :].astype(F32) for y in range(y_n)]
     wgrad_ref[...] = jnp.concatenate([p[:share] for p in pieces], axis=0)
@@ -194,7 +190,7 @@
     tile = tile_values.shape[-1]
     feat = features.shape[1]
     hidden = bias.shape[0]
-    rows = tile // x_n
+    rows = tile // y_n
     tiles = tile_values.reshape(-1, tile, tile)
     sources = tile_block.reshape(-1)
     my_x = lax.axis_index("x")
@@ -204,49 +200,58 @@
     b_lo = (bias - b_hi.astype(F32) - b_mid.astype(F32)).astype(BF16)
     terms = jnp.pad(jnp.stack([b_hi, b_mid, b_lo]), ((0, 13), (0, feat - hidden)))
     pack = jnp.concatenate([weight.T, cotangent.T, terms], axis=0)
-    mine = lax.dynamic_slice_in_dim(features, my_x * rows, rows, 0)
+    dense = call(
+        functools.partial(dense_kernel, zl_n),
+        shape(x_n, c_n, zl_n, tile, tile),
+        sources,
+        tiles,
+        smem=1,
+    )
+
+    quarters = to_all(features.reshape(y_n, rows, feat), "y")
+    mine = lax.dynamic_index_in_dim(quarters, my_x, 0, keepdims=False)
+    mine, dense = lax.optimization_barrier((mine, dense))
+    pieces = [dense[0]]
+    for step in range(1, x_n):
+        pieces.append(lax.ppermute(dense[step], "x", [(x, (x + step) % x_n) for x in range(x_n)]))
+    while len(pieces) < 4:
+        pieces.append(pieces[0])
     column = to_all(jnp.broadcast_to(mine[None], (zl_n, rows, feat)), "zl")
     column, pack = lax.optimization_barrier((column, pack))
     pack_other = swap(pack, "zh")
-    plane = to_all(jnp.broadcast_to(column[None], (y_n * x_n, zl_n, rows, feat)), ("y", "x"))
-    plane, pack_other = lax.optimization_barrier((plane, pack_other))
-    own = plane.reshape(y_n, x_n, zl_n, rows, feat)
+    own = to_all(jnp.broadcast_to(column[None], (y_n, zl_n, rows, feat)), "y")
+    own, pack_other = lax.optimization_barrier((own, pack_other))
     other = swap(own, "c")
 
     size = pack.shape[0]
-    part = to_all(
-        call(
-            functools.partial(forward_kernel, zl_n, x_n),
-            shape(x_n, tile + 2 * size, feat),
-            sources,
-            tiles,
-            own,
-            other,
-            pack,
-            pack_other,
-            smem=1,
-        ),
-        "x",
-    )
+    a_mine, part = call(
+        forward_kernel,
+        (shape(c_n, zl_n, tile, tile), shape(x_n, tile + 2 * size, feat)),
+        *pieces,
+        own,
+        other,
+        pack,
+        pack_other,
+    )
+    part = to_all(part, "x")
     summed = jnp.sum(part[:, :tile].astype(F32), axis=0).astype(BF16)
     summed_other = swap(summed, "zh")
 
-    act_t, pieces = call(
-        functools.partial(backward_kernel, zl_n),
-        (shape(hidden, tile), shape(2, y_n * x_n, zl_n * rows + EXTRA, feat)),
-        sources,
+    payload = shape(y_n, zl_n * rows + EXTRA, tile)
+    act_t, keep, give = call(
+        backward_kernel,
+        (shape(hidden, tile), payload, payload),
         summed,
         summed_other,
         part,
         pack,
-        tiles,
-        smem=1,
-    )
-    both = (pieces[0].astype(F32) + swap(pieces[1], "c").astype(F32)).astype(BF16)
-    across = to_all(both, ("y", "x"))
-    up = call(
-        functools.partial(plane_sum_kernel, y_n, x_n), shape(zl_n, zh_n, rows + EXTRA, feat), across
-    ).reshape(zl_n * zh_n, rows + EXTRA, feat)
+        a_mine,
+    )
+    both = (keep.astype(F32) + swap(give, "c").astype(F32)).astype(BF16)
+    across = to_all(both, "y")
+    up = call(plane_sum_kernel, shape(zl_n, zh_n, rows + EXTRA, feat), across).reshape(
+        zl_n * zh_n, rows + EXTRA, feat
+    )
     down = to_all(up, ("zl", "zh"))
     last = call(
         functools.partial(column_sum_kernel, zl_n, zh_n), shape(y_n * x_n, rows + EXTRA, feat), down

time: 149 us -> 139 us (0.933)
  starting transfers between devices: 40.1 us -> 52.1 us
  blocking collectives: 70.3 us -> 59.5 us
  waiting for transfers between devices: 28 us -> 17.3 us
  local copies, waits for them, and re-layouts: 2.65 us -> 4.43 us
    ppermute x0 -> x3, starting transfers between devices: none -> 11.4 us  [on_device(): lax.ppermute(dense[step], 'x', [(x, (x + step) % x_n) for x in range(x_n)])]
    all_to_all x4, blocking collectives: 70.3 us -> 59.5 us  [to_all(): return lax.all_to_all(v, axes, 0, 0, tiled=True)]
    all_to_all x2 -> x3, waiting for transfers between devices: 9.17 us -> 1.51 us  [to_all(): return lax.all_to_all(v, axes, 0, 0, tiled=True)]
    ppermute x4, waiting for transfers between devices: 18.9 us -> 15.8 us  [swap(): return lax.ppermute(v, axis, [(0, 1), (1, 0)])]
    pallas_call x5 -> x6, Pallas kernels: 4.4 us -> 3.67 us  [call(): pl.pallas_call(kernel, out_shape=out, in_specs=[SMEM] * smem + [VMEM] * (...]
    all_to_all x2 -> x3, starting transfers between devices: 19.8 us -> 20.5 us  [to_all(): return lax.all_to_all(v, axes, 0, 0, tiled=True)]
  transfers between devices with their start and end apart: 6 -> 10, of which waited for: 6 -> 5; matrix products, arithmetic and copies ran while one was open for 1% -> 2% of each run, Pallas kernels for 0% -> 1%
where the time goes in v4:
time: 139 us
  blocking collectives  59.5 us (43%)
  starting transfers between devices  52.1 us (37%)
  waiting for transfers between devices  17.3 us (12%)
  local copies, waits for them, and re-layouts  4.43 us (3%)
  Pallas kernels  3.67 us (3%)
    all_to_all x4, blocking collectives, to_all(): return lax.all_to_all(v, axes, 0, 0, tiled=True)  59.5 us
    all_to_all x3, starting transfers between devices, to_all(): return lax.all_to_all(v, axes, 0, 0, tiled=True)  20.5 us
    ppermute x4, starting transfers between devices, swap(): return lax.ppermute(v, axis, [(0, 1), (1, 0)])  20.3 us
    ppermute x4, waiting for transfers between devices, swap(): return lax.ppermute(v, axis, [(0, 1), (1, 0)])  15.8 us
    ppermute x3, starting transfers between devices, on_device(): lax.ppermute(dense[step], 'x', [(x, (x + step) % x_n) for x in range(x_n)])  11.4 us
    pallas_call x6, Pallas kernels, call(): pl.pallas_call(kernel, out_shape=out, in_specs=[SMEM] * smem + [VMEM] * (...  3.67 us
  transfers between devices with their start and end apart: 10, of which 5 were waited for; matrix products, arithmetic and copies ran while one was open for 2% of the time, Pallas kernels for 1%

profile of v4, /device:TPU:32, one launch (start us, length us, event | category | flops | bytes accessed | tf_op | source)
XLA Modules:
  0.0 138.7 jit_solution(8483410172463541595)
XLA Ops:
  0.6 4.5 %all-to-all-start = ((bf16[4,32,128]{2,1,0:T(8,128)(2,1)}), bf16[4,32,128]{2,1,0:T(8,128)(2,1)S(1)}, u32[]{:S(2)}, u32[]{:S(2)}) async-start(bf16[4,32,128]{2,1,0:T(8,128)(2,1)} %bitcast.28), calls=%async_computation | async-start | bytes 65536 | tf_op jit(solution)/shard_map/all_to_all | solution.py:181
  5.1 0.7 convert_bitcast_fusion.2
  5.9 0.0 copy-start
  5.9 1.2 copy-done
  7.1 0.7 copy-done.1
  7.7 1.3 shard_map.93
  9.1 1.5 %all-to-all-done = bf16[4,32,128]{2,1,0:T(8,128)(2,1)S(1)} async-done(((bf16[4,32,128]{2,1,0:T(8,128)(2,1)}), bf16[4,32,128]{2,1,0:T(8,128)(2,1)S(1)}, u32[]{:S(2)}, u32[]{:S(2)}) %all-to-all-start) | async-done | bytes 32800 | tf_op jit(solution)/shard_map/all_to_all | solution.py:181
  10.6 0.6 broadcast_in_dim.4
  11.2 12.6 %all-to-all-start.1 = ((bf16[8,32,128]{2,1,0:T(8,128)(2,1)}), bf16[8,32,128]{2,1,0:T(8,128)(2,1)S(1)}, u32[]{:S(2)}, u32[]{:S(2)}) async-start(bf16[8,32,128]{2,1,0:T(8,128)(2,1)} %broadcast_in_dim.4), calls=%async_computation.1 | async-start | bytes 131072 | tf_op jit(solution)/shard_map/all_to_all | solution.py:181
  23.8 1.1 slice_bitcast_fusion
  25.0 3.4 %collective-permute-start = (bf16[2,8,128,128]{3,2,1,0:T(8,128)(2,1)}, bf16[2,8,128,128]{3,2,1,0:T(8,128)(2,1)S(1)}, u32[]{:S(2)}, u32[]{:S(2)}) collective-permute-start(bf16[2,8,128,128]{3,2,1,0:T(8,128)(2,1)} %get-tuple-element.34), channel_id=1, source_target_pairs={{0,2},{2,4},{4,6},{6,0},{1,3},{3,5},{5,7},{7,1},{8,10},{10,12},{12... | collective-permute-start | bytes 1572872 | tf_op jit(solution)/shard_map/ppermute | solution.py:216
  28.4 4.6 %collective-permute-start.1 = (bf16[2,8,128,128]{3,2,1,0:T(8,128)(2,1)}, bf16[2,8,128,128]{3,2,1,0:T(8,128)(2,1)S(1)}, u32[]{:S(2)}, u32[]{:S(2)}) collective-permute-start(bf16[2,8,128,128]{3,2,1,0:T(8,128)(2,1)} %get-tuple-element.33), channel_id=1, source_target_pairs={{0,4},{2,6},{4,0},{6,2},{1,5},{3,7},{5,1},{7,3},{8,12},{10,14},{12... | collective-permute-start | bytes 1572872 | tf_op jit(solution)/shard_map/ppermute | solution.py:216
  33.0 3.3 %collective-permute-start.2 = (bf16[2,8,128,128]{3,2,1,0:T(8,128)(2,1)S(1)}, bf16[2,8,128,128]{3,2,1,0:T(8,128)(2,1)S(1)}, u32[]{:S(2)}, u32[]{:S(2)}) collective-permute-start(bf16[2,8,128,128]{3,2,1,0:T(8,128)(2,1)S(1)} %get-tuple-element.32), channel_id=1, source_target_pairs={{0,6},{2,0},{4,2},{6,4},{1,7},{3,1},{5,3},{7,5},{8,14},{10,8},{12,... | collective-permute-start | bytes 1572872 | tf_op jit(solution)/shard_map/ppermute | solution.py:216
  36.4 0.8 broadcast_in_dim.5
  37.2 3.4 %all-to-all-start.2 = ((bf16[4,8,32,128]{3,2,1,0:T(8,128)(2,1)}), bf16[4,8,32,128]{3,2,1,0:T(8,128)(2,1)S(1)}, u32[]{:S(2)}, u32[]{:S(2)}) async-start(bf16[4,8,32,128]{3,2,1,0:T(8,128)(2,1)} %broadcast_in_dim.5), calls=%async_computation.2 | async-start | bytes 524288 | tf_op jit(solution)/shard_map/all_to_all | solution.py:181
  40.6 8.2 %collective-permute-start.3 = (bf16[80,128]{1,0:T(8,128)(2,1)S(1)}, bf16[80,128]{1,0:T(8,128)(2,1)S(1)}, u32[]{:S(2)}, u32[]{:S(2)}) collective-permute-start(bf16[80,128]{1,0:T(8,128)(2,1)S(1)} %pad_maximum_fusion.pack_ref), channel_id=1, source_target_pairs={{0,1},{1,0},{2,3},{3,2},{4,5},{5,4},{6,7},{7,6},{8,9},{9,8},{10,11... | collective-permute-start | bytes 61448 | tf_op jit(solution)/shard_map/ppermute | solution.py:185
  48.8 6.2 %collective-permute-done.3.pack_other_ref = bf16[80,128]{1,0:T(8,128)(2,1)S(1)} collective-permute-done((bf16[80,128]{1,0:T(8,128)(2,1)S(1)}, bf16[80,128]{1,0:T(8,128)(2,1)S(1)}, u32[]{:S(2)}, u32[]{:S(2)}) %collective-permute-start.3) | collective-permute-done | bytes 20512 | tf_op jit(solution)/shard_map/ppermute | solution.py:185
  55.0 0.0 all-to-all-done.2.own_ref
  55.0 1.9 %collective-permute-start.4 = (bf16[4,8,32,128]{3,2,1,0:T(8,128)(2,1)S(1)}, bf16[4,8,32,128]{3,2,1,0:T(8,128)(2,1)S(1)}, u32[]{:S(2)}, u32[]{:S(2)}) collective-permute-start(bf16[4,8,32,128]{3,2,1,0:T(8,128)(2,1)S(1)} %all-to-all-done.2.own_ref), channel_id=1, source_target_pairs={{0,8},{8,0},{1,9},{9,1},{2,10},{10,2},{3,11},{11,3},{4,12},{12,4},... | collective-permute-start | bytes 786440 | tf_op jit(solution)/shard_map/ppermute | solution.py:185
  56.9 1.5 %collective-permute-done.4.oth_ref = bf16[4,8,32,128]{3,2,1,0:T(8,128)(2,1)S(1)} collective-permute-done((bf16[4,8,32,128]{3,2,1,0:T(8,128)(2,1)S(1)}, bf16[4,8,32,128]{3,2,1,0:T(8,128)(2,1)S(1)}, u32[]{:S(2)}, u32[]{:S(2)}) %collective-permute-start.4) | collective-permute-done | bytes 262176 | tf_op jit(solution)/shard_map/ppermute | solution.py:185
  58.4 0.4 shard_map.94
  58.8 10.0 %all_to_all.35.packs_ref = bf16[4,288,128]{2,1,0:T(8,128)(2,1)S(1)} all-to-all(bf16[4,288,128]{2,1,0:T(8,128)(2,1)S(1)} %get-tuple-element.24), channel_id=1, replica_groups=mesh['y'=4,'zl'=8,'c'=2,'x'=4,'zh'=2] {'x'}, dimensions={0} | all-to-all | bytes 589824 | tf_op jit(solution)/shard_map/all_to_all | solution.py:181
  68.8 8.2 %collective-permute-start.5 = (bf16[128,128]{1,0:T(8,128)(2,1)S(1)}, bf16[128,128]{1,0:T(8,128)(2,1)S(1)}, u32[]{:S(2)}, u32[]{:S(2)}) collective-permute-start(bf16[128,128]{1,0:T(8,128)(2,1)S(1)} %slice_reduce_fusion.sum_ref), channel_id=1, source_target_pairs={{0,1},{1,0},{2,3},{3,2},{4,5},{5,4},{6,7},{7,6},{8,9},{9,8},{10,11... | collective-permute-start | bytes 98312 | tf_op jit(solution)/shard_map/ppermute | solution.py:185
  77.0 6.6 %collective-permute-done.5.other_ref = bf16[128,128]{1,0:T(8,128)(2,1)S(1)} collective-permute-done((bf16[128,128]{1,0:T(8,128)(2,1)S(1)}, bf16[128,128]{1,0:T(8,128)(2,1)S(1)}, u32[]{:S(2)}, u32[]{:S(2)}) %collective-permute-start.5) | collective-permute-done | bytes 32800 | tf_op jit(solution)/shard_map/ppermute | solution.py:185
  83.6 1.2 shard_map.95
  84.8 1.9 %collective-permute-start.6 = (bf16[4,272,128]{2,1,0:T(8,128)(2,1)S(1)}, bf16[4,272,128]{2,1,0:T(8,128)(2,1)S(1)}, u32[]{:S(2)}, u32[]{:S(2)}) collective-permute-start(bf16[4,272,128]{2,1,0:T(8,128)(2,1)S(1)} %get-tuple-element.28), channel_id=1, source_target_pairs={{0,8},{8,0},{1,9},{9,1},{2,10},{10,2},{3,11},{11,3},{4,12},{12,4},... | collective-permute-start | bytes 835592 | tf_op jit(solution)/shard_map/ppermute | solution.py:185
  86.7 1.5 %collective-permute-done.6 = bf16[4,272,128]{2,1,0:T(8,128)(2,1)S(1)} collective-permute-done((bf16[4,272,128]{2,1,0:T(8,128)(2,1)S(1)}, bf16[4,272,128]{2,1,0:T(8,128)(2,1)S(1)}, u32[]{:S(2)}, u32[]{:S(2)}) %collective-permute-start.6) | collective-permute-done | bytes 278560 | tf_op jit(solution)/shard_map/ppermute | solution.py:185
  88.3 0.1 add_convert_fusion
  88.3 11.7 %all_to_all.36.in_ref = bf16[4,272,128]{2,1,0:T(8,128)(2,1)S(1)} all-to-all(bf16[4,272,128]{2,1,0:T(8,128)(2,1)S(1)} %add_convert_fusion), channel_id=1, replica_groups=mesh['y'=4,'zl'=8,'c'=2,'x'=4,'zh'=2] {'y'}, dimensions={0} | all-to-all | bytes 557056 | tf_op jit(solution)/shard_map/all_to_all | solution.py:181
  100.1 26.6 %all_to_all.37.in_ref = bf16[16,48,128]{2,1,0:T(8,128)(2,1)S(1)} all-to-all(bf16[16,48,128]{2,1,0:T(8,128)(2,1)S(1)} %bitcast.26), channel_id=1, replica_groups=mesh['y'=4,'zl'=8,'c'=2,'x'=4,'zh'=2] {'zl','zh'}, dimensions={0} | all-to-all | bytes 393216 | tf_op jit(solution)/shard_map/all_to_all | solution.py:181
  126.7 11.3 %all_to_all.38.in_ref = bf16[16,48,128]{2,1,0:T(8,128)(2,1)S(1)} all-to-all(bf16[16,48,128]{2,1,0:T(8,128)(2,1)S(1)} %shard_map.97), channel_id=1, replica_groups=mesh['y'=4,'zl'=8,'c'=2,'x'=4,'zh'=2] {'y','x'}, dimensions={0} | all-to-all | bytes 393216 | tf_op jit(solution)/shard_map/all_to_all | solution.py:181
  138.0 0.7 shard_map.98
  (15 shorter events, 0.1 us)
Async XLA Ops:
  0.6 9.9 %all-to-all-start = ((bf16[4,32,128]{2,1,0:T(8,128)(2,1)}), bf16[4,32,128]{2,1,0:T(8,128)(2,1)S(1)}, u32[]{:S(2)}, u32[]{:S(2)}) async-start(bf16[4,32,128]{2,1,0:T(8,128)(2,1)} %bitcast.28), calls=%async_computation | async-start | bytes 65536 | tf_op jit(solution)/shard_map/all_to_all | solution.py:181
  5.9 1.2 copy-start
  7.1 0.7 copy-start.1
  11.2 25.2 %all-to-all-start.1 = ((bf16[8,32,128]{2,1,0:T(8,128)(2,1)}), bf16[8,32,128]{2,1,0:T(8,128)(2,1)S(1)}, u32[]{:S(2)}, u32[]{:S(2)}) async-start(bf16[8,32,128]{2,1,0:T(8,128)(2,1)} %broadcast_in_dim.4), calls=%async_computation.1 | async-start | bytes 131072 | tf_op jit(solution)/shard_map/all_to_all | solution.py:181
  23.8 12.5 %copy-start.2 = (bf16[128,32]{0,1:T(8,128)(2,1)S(1)}, bf16[128,32]{0,1:T(8,128)(2,1)}, u32[]{:S(2)}) copy-start(bf16[128,32]{0,1:T(8,128)(2,1)} %param.11) | copy-start | bytes 24580
  23.8 12.5 %copy-start.3 = (bf16[128,32]{0,1:T(8,128)(2,1)S(1)}, bf16[128,32]{0,1:T(8,128)(2,1)}, u32[]{:S(2)}) copy-start(bf16[128,32]{0,1:T(8,128)(2,1)} %param.9) | copy-start | bytes 24580
  25.0 31.9 %collective-permute-start = (bf16[2,8,128,128]{3,2,1,0:T(8,128)(2,1)}, bf16[2,8,128,128]{3,2,1,0:T(8,128)(2,1)S(1)}, u32[]{:S(2)}, u32[]{:S(2)}) collective-permute-start(bf16[2,8,128,128]{3,2,1,0:T(8,128)(2,1)} %get-tuple-element.34), channel_id=1, source_target_pairs={{0,2},{2,4},{4,6},{6,0},{1,3},{3,5},{5,7},{7,1},{8,10},{10,12},{12... | collective-permute-start | bytes 1572872 | tf_op jit(solution)/shard_map/ppermute | solution.py:216
  28.4 28.5 %collective-permute-start.1 = (bf16[2,8,128,128]{3,2,1,0:T(8,128)(2,1)}, bf16[2,8,128,128]{3,2,1,0:T(8,128)(2,1)S(1)}, u32[]{:S(2)}, u32[]{:S(2)}) collective-permute-start(bf16[2,8,128,128]{3,2,1,0:T(8,128)(2,1)} %get-tuple-element.33), channel_id=1, source_target_pairs={{0,4},{2,6},{4,0},{6,2},{1,5},{3,7},{5,1},{7,3},{8,12},{10,14},{12... | collective-permute-start | bytes 1572872 | tf_op jit(solution)/shard_map/ppermute | solution.py:216
  33.0 23.9 %collective-permute-start.2 = (bf16[2,8,128,128]{3,2,1,0:T(8,128)(2,1)S(1)}, bf16[2,8,128,128]{3,2,1,0:T(8,128)(2,1)S(1)}, u32[]{:S(2)}, u32[]{:S(2)}) collective-permute-start(bf16[2,8,128,128]{3,2,1,0:T(8,128)(2,1)S(1)} %get-tuple-element.32), channel_id=1, source_target_pairs={{0,6},{2,0},{4,2},{6,4},{1,7},{3,1},{5,3},{7,5},{8,14},{10,8},{12,... | collective-permute-start | bytes 1572872 | tf_op jit(solution)/shard_map/ppermute | solution.py:216
  37.2 17.8 %all-to-all-start.2 = ((bf16[4,8,32,128]{3,2,1,0:T(8,128)(2,1)}), bf16[4,8,32,128]{3,2,1,0:T(8,128)(2,1)S(1)}, u32[]{:S(2)}, u32[]{:S(2)}) async-start(bf16[4,8,32,128]{3,2,1,0:T(8,128)(2,1)} %broadcast_in_dim.5), calls=%async_computation.2 | async-start | bytes 524288 | tf_op jit(solution)/shard_map/all_to_all | solution.py:181
  40.6 14.4 %collective-permute-start.3 = (bf16[80,128]{1,0:T(8,128)(2,1)S(1)}, bf16[80,128]{1,0:T(8,128)(2,1)S(1)}, u32[]{:S(2)}, u32[]{:S(2)}) collective-permute-start(bf16[80,128]{1,0:T(8,128)(2,1)S(1)} %pad_maximum_fusion.pack_ref), channel_id=1, source_target_pairs={{0,1},{1,0},{2,3},{3,2},{4,5},{5,4},{6,7},{7,6},{8,9},{9,8},{10,11... | collective-permute-start | bytes 61448 | tf_op jit(solution)/shard_map/ppermute | solution.py:185
  55.0 3.4 %collective-permute-start.4 = (bf16[4,8,32,128]{3,2,1,0:T(8,128)(2,1)S(1)}, bf16[4,8,32,128]{3,2,1,0:T(8,128)(2,1)S(1)}, u32[]{:S(2)}, u32[]{:S(2)}) collective-permute-start(bf16[4,8,32,128]{3,2,1,0:T(8,128)(2,1)S(1)} %all-to-all-done.2.own_ref), channel_id=1, source_target_pairs={{0,8},{8,0},{1,9},{9,1},{2,10},{10,2},{3,11},{11,3},{4,12},{12,4},... | collective-permute-start | bytes 786440 | tf_op jit(solution)/shard_map/ppermute | solution.py:185
  68.8 14.9 %collective-permute-start.5 = (bf16[128,128]{1,0:T(8,128)(2,1)S(1)}, bf16[128,128]{1,0:T(8,128)(2,1)S(1)}, u32[]{:S(2)}, u32[]{:S(2)}) collective-permute-start(bf16[128,128]{1,0:T(8,128)(2,1)S(1)} %slice_reduce_fusion.sum_ref), channel_id=1, source_target_pairs={{0,1},{1,0},{2,3},{3,2},{4,5},{5,4},{6,7},{7,6},{8,9},{9,8},{10,11... | collective-permute-start | bytes 98312 | tf_op jit(solution)/shard_map/ppermute | solution.py:185
  84.8 3.4 %collective-permute-start.6 = (bf16[4,272,128]{2,1,0:T(8,128)(2,1)S(1)}, bf16[4,272,128]{2,1,0:T(8,128)(2,1)S(1)}, u32[]{:S(2)}, u32[]{:S(2)}) collective-permute-start(bf16[4,272,128]{2,1,0:T(8,128)(2,1)S(1)} %get-tuple-element.28), channel_id=1, source_target_pairs={{0,8},{8,0},{1,9},{9,1},{2,10},{10,2},{3,11},{11,3},{4,12},{12,4},... | collective-permute-start | bytes 835592 | tf_op jit(solution)/shard_map/ppermute | solution.py:185

commit v5 on v4

--- a/solution.py
+++ b/solution.py
@@ -45,10 +45,9 @@
         out_ref[at] = acc.astype(BF16)[None, None, None]
 
 
-def forward_kernel(d0_ref, d1_ref, d2_ref, d3_ref, own_ref, oth_ref, pack_ref, pack_other_ref, a_ref, out_ref):
+def forward_kernel(d0_ref, d1_ref, d2_ref, d3_ref, own_ref, oth_ref, pack_ref, a_ref, out_ref):
     tile = d0_ref.shape[-1]
     feat = own_ref.shape[-1]
-    size = pack_ref.shape[0]
     zl_n = d0_ref.shape[1]
     acc = jnp.zeros((tile, feat), F32)
     for core, x_ref in ((0, own_ref), (1, oth_ref)):
@@ -62,30 +61,39 @@
     part = acc.astype(BF16)
     for x in range(out_ref.shape[0]):
         out_ref[x, :tile, :] = part
-        out_ref[x, tile : tile + size, :] = pack_ref[...]
-        out_ref[x, tile + size :, :] = pack_other_ref[...]
-
-
-def backward_kernel(sum_ref, other_ref, packs_ref, pack_ref, a_ref, act_ref, own_ref, oth_ref):
-    x_n = packs_ref.shape[0]
+        out_ref[x, tile:, :] = pack_ref[...]
+
+
+def row_sum_kernel(in_ref, out_ref):
+    tile = in_ref.shape[2]
+    size = in_ref.shape[1] - tile
+    total = in_ref[0, :tile, :].astype(F32)
+    for x in range(1, in_ref.shape[0]):
+        total = total + in_ref[x, :tile, :].astype(F32)
+    out_ref[:tile, :] = total.astype(BF16)
+    for x in range(in_ref.shape[0]):
+        out_ref[tile + x * size : tile + (x + 1) * size, :] = in_ref[x, tile:, :]
+
+
+def backward_kernel(sum_ref, other_ref, pack_ref, a_ref, act_ref, own_ref, oth_ref):
     hidden = act_ref.shape[0]
     tile = a_ref.shape[-1]
     zl_n = a_ref.shape[1]
     size = pack_ref.shape[0]
     y_n = own_ref.shape[0]
     rows = tile // y_n
-    agg = (sum_ref[...].astype(F32) + other_ref[...].astype(F32)).astype(BF16)
-    starts = [(x, tile + z * size) for x in range(x_n) for z in range(2)]
+    agg = (sum_ref[:tile, :].astype(F32) + other_ref[:tile, :].astype(F32)).astype(BF16)
+    starts = [(ref, at) for at in range(tile, sum_ref.shape[0], size) for ref in (sum_ref, other_ref)]
 
     def gather(start, count):
-        return jnp.concatenate([packs_ref[x, at + start : at + start + count, :] for x, at in starts], axis=0)
+        return jnp.concatenate([ref[at + start : at + start + count, :] for ref, at in starts], axis=0)
 
     def bias_of(three):
         return mm(three, jnp.ones((three.shape[0], tile), BF16), 0, 0)[:hidden]
 
     w_t = gather(0, hidden)
     cot_t = gather(hidden, hidden)
-    bias_t = jnp.concatenate([bias_of(packs_ref[x, at + 2 * hidden : at + size, :]) for x, at in starts], axis=0)
+    bias_t = jnp.concatenate([bias_of(ref[at + 2 * hidden : at + size, :]) for ref, at in starts], axis=0)
     pre_t = mm(w_t, agg, 1, 1) + bias_t
     grad_t = (cot_t.astype(F32) * slope(pre_t)).astype(BF16)
     back_t = mm(w_t, grad_t, 0, 0).astype(BF16)
@@ -208,33 +216,32 @@
         smem=1,
     )
 
+    def along_x(v, step):
+        return lax.ppermute(v, "x", [(x, (x + step) % x_n) for x in range(x_n)])
+
+    shares = [dense[0], along_x(dense[1], 1)]
     quarters = to_all(features.reshape(y_n, rows, feat), "y")
     mine = lax.dynamic_index_in_dim(quarters, my_x, 0, keepdims=False)
-    mine, dense = lax.optimization_barrier((mine, dense))
-    pieces = [dense[0]]
-    for step in range(1, x_n):
-        pieces.append(lax.ppermute(dense[step], "x", [(x, (x + step) % x_n) for x in range(x_n)]))
-    while len(pieces) < 4:
-        pieces.append(pieces[0])
+    if x_n > 2:
+        mine, second = lax.optimization_barrier((mine, dense[2]))
+        shares.append(along_x(second, 2))
     column = to_all(jnp.broadcast_to(mine[None], (zl_n, rows, feat)), "zl")
-    column, pack = lax.optimization_barrier((column, pack))
-    pack_other = swap(pack, "zh")
+    if x_n > 3:
+        column, third, *shares = lax.optimization_barrier((column, dense[3], *shares))
+        shares.append(along_x(third, 3))
     own = to_all(jnp.broadcast_to(column[None], (y_n, zl_n, rows, feat)), "y")
-    own, pack_other = lax.optimization_barrier((own, pack_other))
     other = swap(own, "c")
 
     size = pack.shape[0]
     a_mine, part = call(
         forward_kernel,
-        (shape(c_n, zl_n, tile, tile), shape(x_n, tile + 2 * size, feat)),
-        *pieces,
+        (shape(c_n, zl_n, tile, tile), shape(x_n, tile + size, feat)),
+        *(shares + shares)[:4],
         own,
         other,
         pack,
-        pack_other,
-    )
-    part = to_all(part, "x")
-    summed = jnp.sum(part[:, :tile].astype(F32), axis=0).astype(BF16)
+    )
+    summed = call(row_sum_kernel, shape(tile + x_n * size, feat), to_all(part, "x"))
     summed_other = swap(summed, "zh")
 
     payload = shape(y_n, zl_n * rows + EXTRA, tile)
@@ -243,7 +250,6 @@
         (shape(hidden, tile), payload, payload),
         summed,
         summed_other,
-        part,
         pack,
         a_mine,
     )

time: 139 us -> 145 us (1.043)
  blocking collectives: 59.5 us -> 83.5 us
  starting transfers between devices: 52.1 us -> 37.8 us
  waiting for transfers between devices: 17.3 us -> 15.1 us
  local copies, waits for them, and re-layouts: 4.43 us -> 2.83 us
    all_to_all x4 -> x5, blocking collectives: 59.5 us -> 83.5 us  [to_all(): return lax.all_to_all(v, axes, 0, 0, tiled=True)]
    all_to_all x3 -> x2, starting transfers between devices: 20.5 us -> 9.27 us  [to_all(): return lax.all_to_all(v, axes, 0, 0, tiled=True)]
    ppermute x4 -> x3, waiting for transfers between devices: 15.8 us -> 9.11 us  [swap(): return lax.ppermute(v, axis, [(0, 1), (1, 0)])]
    ppermute x4 -> x3, starting transfers between devices: 20.3 us -> 17.2 us  [swap(): return lax.ppermute(v, axis, [(0, 1), (1, 0)])]
    ppermute x3, waiting for transfers between devices: 0.01 us -> 2.64 us  [along_x(): return lax.ppermute(v, 'x', [(x, (x + step) % x_n) for x in range(x_n)])]
    all_to_all x3 -> x2, waiting for transfers between devices: 1.51 us -> 3.34 us  [to_all(): return lax.all_to_all(v, axes, 0, 0, tiled=True)]
    pallas_call x6 -> x7, Pallas kernels: 3.67 us -> 3.68 us  [call(): pl.pallas_call(kernel, out_shape=out, in_specs=[SMEM] * smem + [VMEM] * (...]
  transfers between devices with their start and end apart: 10 -> 8, of which waited for: 5 -> 5; matrix products, arithmetic and copies ran while one was open for 2% -> 0% of each run, Pallas kernels for 1% -> 1%
where the time goes in v5:
time: 145 us; the launch traced here: 144 us
  blocking collectives  83.5 us (58%)
  starting transfers between devices  37.8 us (26%)
  waiting for transfers between devices  15.1 us (10%)
  Pallas kernels  3.68 us (3%)
  local copies, waits for them, and re-layouts  2.83 us (2%)
    all_to_all x5, blocking collectives, to_all(): return lax.all_to_all(v, axes, 0, 0, tiled=True)  83.5 us
    ppermute x3, starting transfers between devices, swap(): return lax.ppermute(v, axis, [(0, 1), (1, 0)])  17.2 us
    ppermute x3, starting transfers between devices, along_x(): return lax.ppermute(v, 'x', [(x, (x + step) % x_n) for x in range(x_n)])  11.4 us
    all_to_all x2, starting transfers between devices, to_all(): return lax.all_to_all(v, axes, 0, 0, tiled=True)  9.27 us
    ppermute x3, waiting for transfers between devices, swap(): return lax.ppermute(v, axis, [(0, 1), (1, 0)])  9.11 us
    pallas_call x7, Pallas kernels, call(): pl.pallas_call(kernel, out_shape=out, in_specs=[SMEM] * smem + [VMEM] * (...  3.68 us
    all_to_all x2, waiting for transfers between devices, to_all(): return lax.all_to_all(v, axes, 0, 0, tiled=True)  3.34 us
  transfers between devices with their start and end apart: 8, of which 5 were waited for; matrix products, arithmetic and copies ran while one was open for 0% of the time, Pallas kernels for 1%

profile of v5, /device:TPU:32, one launch (start us, length us, event | category | flops | bytes accessed | tf_op | source)
XLA Modules:
  0.0 143.9 jit_solution(16712913399576511342)
XLA Ops:
  0.6 4.5 %all-to-all-start = ((bf16[4,32,128]{2,1,0:T(8,128)(2,1)}), bf16[4,32,128]{2,1,0:T(8,128)(2,1)S(1)}, u32[]{:S(2)}, u32[]{:S(2)}) async-start(bf16[4,32,128]{2,1,0:T(8,128)(2,1)} %bitcast.28), calls=%async_computation | async-start | bytes 65536 | tf_op jit(solution)/shard_map/all_to_all | solution.py:189
  5.1 1.2 copy-done
  6.3 0.7 copy-done.1
  7.0 1.3 shard_map.93
  8.3 0.0 copy-start.4
  8.3 0.0 copy-start.2
  8.3 0.0 copy-start.3
  8.3 0.2 slice_bitcast_fusion
  8.5 3.4 %collective-permute-start = (bf16[2,8,128,128]{3,2,1,0:T(8,128)(2,1)S(1)}, bf16[2,8,128,128]{3,2,1,0:T(8,128)(2,1)S(1)}, u32[]{:S(2)}, u32[]{:S(2)}) collective-permute-start(bf16[2,8,128,128]{3,2,1,0:T(8,128)(2,1)S(1)} %get-tuple-element.34), channel_id=1, source_target_pairs={{0,2},{2,4},{4,6},{6,0},{1,3},{3,5},{5,7},{7,1},{8,10},{10,12},{12... | collective-permute-start | bytes 1572872 | tf_op jit(solution)/shard_map/ppermute | solution.py:220
  12.0 4.6 %collective-permute-start.1 = (bf16[2,8,128,128]{3,2,1,0:T(8,128)(2,1)S(1)}, bf16[2,8,128,128]{3,2,1,0:T(8,128)(2,1)S(1)}, u32[]{:S(2)}, u32[]{:S(2)}) collective-permute-start(bf16[2,8,128,128]{3,2,1,0:T(8,128)(2,1)S(1)} %get-tuple-element.20), channel_id=1, source_target_pairs={{0,4},{2,6},{4,0},{6,2},{1,5},{3,7},{5,1},{7,3},{8,12},{10,14},{12... | collective-permute-start | bytes 1572872 | tf_op jit(solution)/shard_map/ppermute | solution.py:220
  16.6 21.7 %all_to_all.35 = bf16[8,32,128]{2,1,0:T(8,128)(2,1)S(1)} all-to-all(bf16[8,32,128]{2,1,0:T(8,128)(2,1)S(1)} %broadcast_in_dim.4), channel_id=1, replica_groups=mesh['y'=4,'zl'=8,'c'=2,'x'=4,'zh'=2] {'zl'}, dimensions={0} | all-to-all | bytes 131072 | tf_op jit(solution)/shard_map/all_to_all | solution.py:189
  38.3 0.0 collective-permute-done.d1_ref
  38.3 0.0 collective-permute-done.1.d2_ref
  38.3 0.7 broadcast_in_dim.5
  39.1 4.8 %all-to-all-start.2 = ((bf16[4,8,32,128]{3,2,1,0:T(8,128)(2,1)}), bf16[4,8,32,128]{3,2,1,0:T(8,128)(2,1)S(1)}, u32[]{:S(2)}, u32[]{:S(2)}) async-start(bf16[4,8,32,128]{3,2,1,0:T(8,128)(2,1)} %broadcast_in_dim.5), calls=%async_computation.2 | async-start | bytes 524288 | tf_op jit(solution)/shard_map/all_to_all | solution.py:189
  43.9 3.3 %collective-permute-start.2 = (bf16[2,8,128,128]{3,2,1,0:T(8,128)(2,1)S(1)}, bf16[2,8,128,128]{3,2,1,0:T(8,128)(2,1)S(1)}, u32[]{:S(2)}, u32[]{:S(2)}) collective-permute-start(bf16[2,8,128,128]{3,2,1,0:T(8,128)(2,1)S(1)} %get-tuple-element.24), channel_id=1, source_target_pairs={{0,6},{2,0},{4,2},{6,4},{1,7},{3,1},{5,3},{7,5},{8,14},{10,8},{12,... | collective-permute-start | bytes 1572872 | tf_op jit(solution)/shard_map/ppermute | solution.py:220
  47.2 3.3 %all-to-all-done.2.own_ref = bf16[4,8,32,128]{3,2,1,0:T(8,128)(2,1)S(1)} async-done(((bf16[4,8,32,128]{3,2,1,0:T(8,128)(2,1)}), bf16[4,8,32,128]{3,2,1,0:T(8,128)(2,1)S(1)}, u32[]{:S(2)}, u32[]{:S(2)}) %all-to-all-start.2) | async-done | bytes 262176 | tf_op jit(solution)/shard_map/all_to_all | solution.py:189
  50.5 1.9 %collective-permute-start.3 = (bf16[4,8,32,128]{3,2,1,0:T(8,128)(2,1)S(1)}, bf16[4,8,32,128]{3,2,1,0:T(8,128)(2,1)S(1)}, u32[]{:S(2)}, u32[]{:S(2)}) collective-permute-start(bf16[4,8,32,128]{3,2,1,0:T(8,128)(2,1)S(1)} %all-to-all-done.2.own_ref), channel_id=1, source_target_pairs={{0,8},{8,0},{1,9},{9,1},{2,10},{10,2},{3,11},{11,3},{4,12},{12,4},... | collective-permute-start | bytes 786440 | tf_op jit(solution)/shard_map/ppermute | solution.py:193
  52.5 1.4 collective-permute-done.3.oth_ref
  54.0 2.6 %collective-permute-done.2.d3_ref = bf16[2,8,128,128]{3,2,1,0:T(8,128)(2,1)S(1)} collective-permute-done((bf16[2,8,128,128]{3,2,1,0:T(8,128)(2,1)S(1)}, bf16[2,8,128,128]{3,2,1,0:T(8,128)(2,1)S(1)}, u32[]{:S(2)}, u32[]{:S(2)}) %collective-permute-start.2) | collective-permute-done | bytes 524320 | tf_op jit(solution)/shard_map/ppermute | solution.py:220
  56.6 0.4 shard_map.94
  57.0 10.1 %all_to_all.36.in_ref = bf16[4,208,128]{2,1,0:T(8,128)(2,1)S(1)} all-to-all(bf16[4,208,128]{2,1,0:T(8,128)(2,1)S(1)} %get-tuple-element.26), channel_id=1, replica_groups=mesh['y'=4,'zl'=8,'c'=2,'x'=4,'zh'=2] {'x'}, dimensions={0} | all-to-all | bytes 425984 | tf_op jit(solution)/shard_map/all_to_all | solution.py:189
  67.1 13.4 %collective-permute-start.4 = (bf16[448,128]{1,0:T(8,128)(2,1)S(1)}, bf16[448,128]{1,0:T(8,128)(2,1)S(1)}, u32[]{:S(2)}, u32[]{:S(2)}) collective-permute-start(bf16[448,128]{1,0:T(8,128)(2,1)S(1)} %shard_map.95.sum_ref), channel_id=1, source_target_pairs={{0,1},{1,0},{2,3},{3,2},{4,5},{5,4},{6,7},{7,6},{8,9},{9,8},{10,11... | collective-permute-start | bytes 344072 | tf_op jit(solution)/shard_map/ppermute | solution.py:193
  80.5 6.2 %collective-permute-done.4.other_ref = bf16[448,128]{1,0:T(8,128)(2,1)S(1)} collective-permute-done((bf16[448,128]{1,0:T(8,128)(2,1)S(1)}, bf16[448,128]{1,0:T(8,128)(2,1)S(1)}, u32[]{:S(2)}, u32[]{:S(2)}) %collective-permute-start.4) | collective-permute-done | bytes 114720 | tf_op jit(solution)/shard_map/ppermute | solution.py:193
  86.7 1.2 shard_map.96
  87.8 1.9 %collective-permute-start.5 = (bf16[4,272,128]{2,1,0:T(8,128)(2,1)S(1)}, bf16[4,272,128]{2,1,0:T(8,128)(2,1)S(1)}, u32[]{:S(2)}, u32[]{:S(2)}) collective-permute-start(bf16[4,272,128]{2,1,0:T(8,128)(2,1)S(1)} %get-tuple-element.30), channel_id=1, source_target_pairs={{0,8},{8,0},{1,9},{9,1},{2,10},{10,2},{3,11},{11,3},{4,12},{12,4},... | collective-permute-start | bytes 835592 | tf_op jit(solution)/shard_map/ppermute | solution.py:193
  89.7 1.5 %collective-permute-done.5 = bf16[4,272,128]{2,1,0:T(8,128)(2,1)S(1)} collective-permute-done((bf16[4,272,128]{2,1,0:T(8,128)(2,1)S(1)}, bf16[4,272,128]{2,1,0:T(8,128)(2,1)S(1)}, u32[]{:S(2)}, u32[]{:S(2)}) %collective-permute-start.5) | collective-permute-done | bytes 278560 | tf_op jit(solution)/shard_map/ppermute | solution.py:193
  91.3 0.1 add_convert_fusion
  91.4 11.2 %all_to_all.37.in_ref = bf16[4,272,128]{2,1,0:T(8,128)(2,1)S(1)} all-to-all(bf16[4,272,128]{2,1,0:T(8,128)(2,1)S(1)} %add_convert_fusion), channel_id=1, replica_groups=mesh['y'=4,'zl'=8,'c'=2,'x'=4,'zh'=2] {'y'}, dimensions={0} | all-to-all | bytes 557056 | tf_op jit(solution)/shard_map/all_to_all | solution.py:189
  102.6 29.2 %all_to_all.38.in_ref = bf16[16,48,128]{2,1,0:T(8,128)(2,1)S(1)} all-to-all(bf16[16,48,128]{2,1,0:T(8,128)(2,1)S(1)} %bitcast.26), channel_id=1, replica_groups=mesh['y'=4,'zl'=8,'c'=2,'x'=4,'zh'=2] {'zl','zh'}, dimensions={0} | all-to-all | bytes 393216 | tf_op jit(solution)/shard_map/all_to_all | solution.py:189
  131.8 11.3 %all_to_all.39.in_ref = bf16[16,48,128]{2,1,0:T(8,128)(2,1)S(1)} all-to-all(bf16[16,48,128]{2,1,0:T(8,128)(2,1)S(1)} %shard_map.98), channel_id=1, replica_groups=mesh['y'=4,'zl'=8,'c'=2,'x'=4,'zh'=2] {'y','x'}, dimensions={0} | all-to-all | bytes 393216 | tf_op jit(solution)/shard_map/all_to_all | solution.py:189
  143.1 0.7 shard_map.99
  (14 shorter events, 0.1 us)
Async XLA Ops:
  0.6 11.3 %all-to-all-start = ((bf16[4,32,128]{2,1,0:T(8,128)(2,1)}), bf16[4,32,128]{2,1,0:T(8,128)(2,1)S(1)}, u32[]{:S(2)}, u32[]{:S(2)}) async-start(bf16[4,32,128]{2,1,0:T(8,128)(2,1)} %bitcast.28), calls=%async_computation | async-start | bytes 65536 | tf_op jit(solution)/shard_map/all_to_all | solution.py:189
  5.1 1.2 copy-start
  6.3 0.7 copy-start.1
  8.3 44.2 %copy-start.4 = (f32[32]{0:T(128)S(1)}, f32[32]{0:T(128)}, u32[]{:S(2)}) copy-start(f32[32]{0:T(128)} %param.10) | copy-start | bytes 388
  8.3 44.2 %copy-start.2 = (bf16[128,32]{0,1:T(8,128)(2,1)S(1)}, bf16[128,32]{0,1:T(8,128)(2,1)}, u32[]{:S(2)}) copy-start(bf16[128,32]{0,1:T(8,128)(2,1)} %param.11) | copy-start | bytes 24580
  8.3 44.2 %copy-start.3 = (bf16[128,32]{0,1:T(8,128)(2,1)S(1)}, bf16[128,32]{0,1:T(8,128)(2,1)}, u32[]{:S(2)}) copy-start(bf16[128,32]{0,1:T(8,128)(2,1)} %param.9) | copy-start | bytes 24580
  8.5 29.8 %collective-permute-start = (bf16[2,8,128,128]{3,2,1,0:T(8,128)(2,1)S(1)}, bf16[2,8,128,128]{3,2,1,0:T(8,128)(2,1)S(1)}, u32[]{:S(2)}, u32[]{:S(2)}) collective-permute-start(bf16[2,8,128,128]{3,2,1,0:T(8,128)(2,1)S(1)} %get-tuple-element.34), channel_id=1, source_target_pairs={{0,2},{2,4},{4,6},{6,0},{1,3},{3,5},{5,7},{7,1},{8,10},{10,12},{12... | collective-permute-start | bytes 1572872 | tf_op jit(solution)/shard_map/ppermute | solution.py:220
  12.0 26.4 %collective-permute-start.1 = (bf16[2,8,128,128]{3,2,1,0:T(8,128)(2,1)S(1)}, bf16[2,8,128,128]{3,2,1,0:T(8,128)(2,1)S(1)}, u32[]{:S(2)}, u32[]{:S(2)}) collective-permute-start(bf16[2,8,128,128]{3,2,1,0:T(8,128)(2,1)S(1)} %get-tuple-element.20), channel_id=1, source_target_pairs={{0,4},{2,6},{4,0},{6,2},{1,5},{3,7},{5,1},{7,3},{8,12},{10,14},{12... | collective-permute-start | bytes 1572872 | tf_op jit(solution)/shard_map/ppermute | solution.py:220
  39.1 11.5 %all-to-all-start.2 = ((bf16[4,8,32,128]{3,2,1,0:T(8,128)(2,1)}), bf16[4,8,32,128]{3,2,1,0:T(8,128)(2,1)S(1)}, u32[]{:S(2)}, u32[]{:S(2)}) async-start(bf16[4,8,32,128]{3,2,1,0:T(8,128)(2,1)} %broadcast_in_dim.5), calls=%async_computation.2 | async-start | bytes 524288 | tf_op jit(solution)/shard_map/all_to_all | solution.py:189
  43.9 12.7 %collective-permute-start.2 = (bf16[2,8,128,128]{3,2,1,0:T(8,128)(2,1)S(1)}, bf16[2,8,128,128]{3,2,1,0:T(8,128)(2,1)S(1)}, u32[]{:S(2)}, u32[]{:S(2)}) collective-permute-start(bf16[2,8,128,128]{3,2,1,0:T(8,128)(2,1)S(1)} %get-tuple-element.24), channel_id=1, source_target_pairs={{0,6},{2,0},{4,2},{6,4},{1,7},{3,1},{5,3},{7,5},{8,14},{10,8},{12,... | collective-permute-start | bytes 1572872 | tf_op jit(solution)/shard_map/ppermute | solution.py:220
  50.5 3.4 %collective-permute-start.3 = (bf16[4,8,32,128]{3,2,1,0:T(8,128)(2,1)S(1)}, bf16[4,8,32,128]{3,2,1,0:T(8,128)(2,1)S(1)}, u32[]{:S(2)}, u32[]{:S(2)}) collective-permute-start(bf16[4,8,32,128]{3,2,1,0:T(8,128)(2,1)S(1)} %all-to-all-done.2.own_ref), channel_id=1, source_target_pairs={{0,8},{8,0},{1,9},{9,1},{2,10},{10,2},{3,11},{11,3},{4,12},{12,4},... | collective-permute-start | bytes 786440 | tf_op jit(solution)/shard_map/ppermute | solution.py:193
  67.1 19.5 %collective-permute-start.4 = (bf16[448,128]{1,0:T(8,128)(2,1)S(1)}, bf16[448,128]{1,0:T(8,128)(2,1)S(1)}, u32[]{:S(2)}, u32[]{:S(2)}) collective-permute-start(bf16[448,128]{1,0:T(8,128)(2,1)S(1)} %shard_map.95.sum_ref), channel_id=1, source_target_pairs={{0,1},{1,0},{2,3},{3,2},{4,5},{5,4},{6,7},{7,6},{8,9},{9,8},{10,11... | collective-permute-start | bytes 344072 | tf_op jit(solution)/shard_map/ppermute | solution.py:193
  87.8 3.4 %collective-permute-start.5 = (bf16[4,272,128]{2,1,0:T(8,128)(2,1)S(1)}, bf16[4,272,128]{2,1,0:T(8,128)(2,1)S(1)}, u32[]{:S(2)}, u32[]{:S(2)}) collective-permute-start(bf16[4,272,128]{2,1,0:T(8,128)(2,1)S(1)} %get-tuple-element.30), channel_id=1, source_target_pairs={{0,8},{8,0},{1,9},{9,1},{2,10},{10,2},{3,11},{11,3},{4,12},{12,4},... | collective-permute-start | bytes 835592 | tf_op jit(solution)/shard_map/ppermute | solution.py:193

commit v6 on v4

--- a/solution.py
+++ b/solution.py
@@ -45,20 +45,22 @@
         out_ref[at] = acc.astype(BF16)[None, None, None]
 
 
-def forward_kernel(d0_ref, d1_ref, d2_ref, d3_ref, own_ref, oth_ref, pack_ref, pack_other_ref, a_ref, out_ref):
+def forward_kernel(d0_ref, d1_ref, d2_ref, d3_ref, feat_ref, pack_ref, pack_other_ref, a_ref, out_ref):
+    my_c = lax.axis_index("c")
     tile = d0_ref.shape[-1]
-    feat = own_ref.shape[-1]
+    feat = feat_ref.shape[-1]
     size = pack_ref.shape[0]
     zl_n = d0_ref.shape[1]
     acc = jnp.zeros((tile, feat), F32)
-    for core, x_ref in ((0, own_ref), (1, oth_ref)):
+    for core in range(2):
         for zl in range(zl_n):
             total = d0_ref[core, zl].astype(F32)
             for ref in (d1_ref, d2_ref, d3_ref)[: out_ref.shape[0] - 1]:
                 total = total + ref[core, zl].astype(F32)
             total = total.astype(BF16)
             a_ref[core, zl] = total
-            acc = acc + mm(total, x_ref[:, zl].reshape(tile, feat), 1, 0)
+            at = (slice(None), pl.ds(my_c if core == 0 else 1 - my_c, 1), slice(zl, zl + 1))
+            acc = acc + mm(total, feat_ref[at].reshape(tile, feat), 1, 0)
     part = acc.astype(BF16)
     for x in range(out_ref.shape[0]):
         out_ref[x, :tile, :] = part
@@ -217,19 +219,17 @@
     while len(pieces) < 4:
         pieces.append(pieces[0])
     column = to_all(jnp.broadcast_to(mine[None], (zl_n, rows, feat)), "zl")
+    column = lax.all_gather(column, "c")
     column, pack = lax.optimization_barrier((column, pack))
     pack_other = swap(pack, "zh")
-    own = to_all(jnp.broadcast_to(column[None], (y_n, zl_n, rows, feat)), "y")
-    own, pack_other = lax.optimization_barrier((own, pack_other))
-    other = swap(own, "c")
+    blocks = to_all(jnp.broadcast_to(column[None], (y_n,) + column.shape), "y")
 
     size = pack.shape[0]
     a_mine, part = call(
         forward_kernel,
         (shape(c_n, zl_n, tile, tile), shape(x_n, tile + 2 * size, feat)),
         *pieces,
-        own,
-        other,
+        blocks,
         pack,
         pack_other,
     )

time: 139 us -> 137 us (0.986)
  starting transfers between devices: 52.1 us -> 50.3 us
  waiting for transfers between devices: 17.3 us -> 15.6 us
  blocking collectives: 59.5 us -> 61 us
    all_gather x0 -> x1, blocking collectives: none -> 1.9 us  [on_device(): column = lax.all_gather(column, 'c')]
    ppermute x4 -> x3, starting transfers between devices: 20.3 us -> 18.4 us  [swap(): return lax.ppermute(v, axis, [(0, 1), (1, 0)])]
    ppermute x4 -> x3, waiting for transfers between devices: 15.8 us -> 14 us  [swap(): return lax.ppermute(v, axis, [(0, 1), (1, 0)])]
  transfers between devices with their start and end apart: 10 -> 9, of which waited for: 5 -> 4; matrix products, arithmetic and copies ran while one was open for 2% -> 2% of each run, Pallas kernels for 1% -> 1%
where the time goes in v6:
time: 137 us
  blocking collectives  61 us (45%)
  starting transfers between devices  50.3 us (37%)
  waiting for transfers between devices  15.6 us (11%)
  local copies, waits for them, and re-layouts  4.58 us (3%)
  Pallas kernels  3.67 us (3%)
    all_to_all x4, blocking collectives, to_all(): return lax.all_to_all(v, axes, 0, 0, tiled=True)  59.1 us
    all_to_all x3, starting transfers between devices, to_all(): return lax.all_to_all(v, axes, 0, 0, tiled=True)  20.6 us
    ppermute x3, starting transfers between devices, swap(): return lax.ppermute(v, axis, [(0, 1), (1, 0)])  18.4 us
    ppermute x3, waiting for transfers between devices, swap(): return lax.ppermute(v, axis, [(0, 1), (1, 0)])  14 us
    ppermute x3, starting transfers between devices, on_device(): lax.ppermute(dense[step], 'x', [(x, (x + step) % x_n) for x in range(x_n)])  11.4 us
    pallas_call x6, Pallas kernels, call(): pl.pallas_call(kernel, out_shape=out, in_specs=[SMEM] * smem + [VMEM] * (...  3.67 us
  transfers between devices with their start and end apart: 9, of which 4 were waited for; matrix products, arithmetic and copies ran while one was open for 2% of the time, Pallas kernels for 1%

profile of v6, /device:TPU:32, one launch (start us, length us, event | category | flops | bytes accessed | tf_op | source)
XLA Modules:
  0.0 136.7 jit_solution(15768227319602149157)
XLA Ops:
  0.6 4.5 %all-to-all-start = ((bf16[4,32,128]{2,1,0:T(8,128)(2,1)}), bf16[4,32,128]{2,1,0:T(8,128)(2,1)S(1)}, u32[]{:S(2)}, u32[]{:S(2)}) async-start(bf16[4,32,128]{2,1,0:T(8,128)(2,1)} %bitcast.30), calls=%async_computation | async-start | bytes 65536 | tf_op jit(solution)/shard_map/all_to_all | solution.py:183
  5.1 0.7 convert_bitcast_fusion.2
  5.9 0.0 copy-start
  5.9 1.2 copy-done
  7.1 0.7 copy-done.1
  7.7 1.3 shard_map.93
  9.1 1.5 %all-to-all-done = bf16[4,32,128]{2,1,0:T(8,128)(2,1)S(1)} async-done(((bf16[4,32,128]{2,1,0:T(8,128)(2,1)}), bf16[4,32,128]{2,1,0:T(8,128)(2,1)S(1)}, u32[]{:S(2)}, u32[]{:S(2)}) %all-to-all-start) | async-done | bytes 32800 | tf_op jit(solution)/shard_map/all_to_all | solution.py:183
  10.6 0.6 broadcast_in_dim.4
  11.2 12.6 %all-to-all-start.1 = ((bf16[8,32,128]{2,1,0:T(8,128)(2,1)}), bf16[8,32,128]{2,1,0:T(8,128)(2,1)S(1)}, u32[]{:S(2)}, u32[]{:S(2)}) async-start(bf16[8,32,128]{2,1,0:T(8,128)(2,1)} %broadcast_in_dim.4), calls=%async_computation.1 | async-start | bytes 131072 | tf_op jit(solution)/shard_map/all_to_all | solution.py:183
  23.8 1.1 slice_bitcast_fusion
  25.0 3.4 %collective-permute-start = (bf16[2,8,128,128]{3,2,1,0:T(8,128)(2,1)}, bf16[2,8,128,128]{3,2,1,0:T(8,128)(2,1)S(1)}, u32[]{:S(2)}, u32[]{:S(2)}) collective-permute-start(bf16[2,8,128,128]{3,2,1,0:T(8,128)(2,1)} %get-tuple-element.30), channel_id=1, source_target_pairs={{0,2},{2,4},{4,6},{6,0},{1,3},{3,5},{5,7},{7,1},{8,10},{10,12},{12... | collective-permute-start | bytes 1572872 | tf_op jit(solution)/shard_map/ppermute | solution.py:218
  28.4 4.6 %collective-permute-start.1 = (bf16[2,8,128,128]{3,2,1,0:T(8,128)(2,1)}, bf16[2,8,128,128]{3,2,1,0:T(8,128)(2,1)S(1)}, u32[]{:S(2)}, u32[]{:S(2)}) collective-permute-start(bf16[2,8,128,128]{3,2,1,0:T(8,128)(2,1)} %get-tuple-element.29), channel_id=1, source_target_pairs={{0,4},{2,6},{4,0},{6,2},{1,5},{3,7},{5,1},{7,3},{8,12},{10,14},{12... | collective-permute-start | bytes 1572872 | tf_op jit(solution)/shard_map/ppermute | solution.py:218
  33.0 3.3 %collective-permute-start.2 = (bf16[2,8,128,128]{3,2,1,0:T(8,128)(2,1)S(1)}, bf16[2,8,128,128]{3,2,1,0:T(8,128)(2,1)S(1)}, u32[]{:S(2)}, u32[]{:S(2)}) collective-permute-start(bf16[2,8,128,128]{3,2,1,0:T(8,128)(2,1)S(1)} %get-tuple-element.28), channel_id=1, source_target_pairs={{0,6},{2,0},{4,2},{6,4},{1,7},{3,1},{5,3},{7,5},{8,14},{10,8},{12,... | collective-permute-start | bytes 1572872 | tf_op jit(solution)/shard_map/ppermute | solution.py:218
  36.4 1.9 %all-gather = bf16[16,32,128]{2,1,0:T(8,128)(2,1)S(1)} all-gather(bf16[8,32,128]{2,1,0:T(8,128)(2,1)S(1)} %all-to-all-done.1), channel_id=2, replica_groups=mesh['y'=4,'zl'=8,'c'=2,'x'=4,'zh'=2] {'c'}, dimensions={0}, use_global_device_ids=true | all-gather | bytes 196608 | tf_op jit(solution)/shard_map/all_gather | solution.py:222
  38.3 0.9 broadcast_in_dim.5
  39.2 3.5 %all-to-all-start.2 = ((bf16[4,2,8,32,128]{4,3,2,1,0:T(8,128)(2,1)}), bf16[4,2,8,32,128]{4,3,2,1,0:T(8,128)(2,1)S(1)}, u32[]{:S(2)}, u32[]{:S(2)}) async-start(bf16[4,2,8,32,128]{4,3,2,1,0:T(8,128)(2,1)} %broadcast_in_dim.5), calls=%async_computation.2 | async-start | bytes 1048576 | tf_op jit(solution)/shard_map/all_to_all | solution.py:183
  42.7 8.2 %collective-permute-start.3 = (bf16[80,128]{1,0:T(8,128)(2,1)S(1)}, bf16[80,128]{1,0:T(8,128)(2,1)S(1)}, u32[]{:S(2)}, u32[]{:S(2)}) collective-permute-start(bf16[80,128]{1,0:T(8,128)(2,1)S(1)} %pad_maximum_fusion.pack_ref), channel_id=1, source_target_pairs={{0,1},{1,0},{2,3},{3,2},{4,5},{5,4},{6,7},{7,6},{8,9},{9,8},{10,11... | collective-permute-start | bytes 61448 | tf_op jit(solution)/shard_map/ppermute | solution.py:187
  50.9 6.2 %collective-permute-done.3.pack_other_ref = bf16[80,128]{1,0:T(8,128)(2,1)S(1)} collective-permute-done((bf16[80,128]{1,0:T(8,128)(2,1)S(1)}, bf16[80,128]{1,0:T(8,128)(2,1)S(1)}, u32[]{:S(2)}, u32[]{:S(2)}) %collective-permute-start.3) | collective-permute-done | bytes 20512 | tf_op jit(solution)/shard_map/ppermute | solution.py:187
  57.1 0.0 collective-permute-done.d1_ref
  57.1 0.0 collective-permute-done.1.d2_ref
  57.1 0.4 shard_map.94
  57.5 9.2 %all_to_all.35.packs_ref = bf16[4,288,128]{2,1,0:T(8,128)(2,1)S(1)} all-to-all(bf16[4,288,128]{2,1,0:T(8,128)(2,1)S(1)} %get-tuple-element.20), channel_id=1, replica_groups=mesh['y'=4,'zl'=8,'c'=2,'x'=4,'zh'=2] {'x'}, dimensions={0} | all-to-all | bytes 589824 | tf_op jit(solution)/shard_map/all_to_all | solution.py:183
  66.8 8.2 %collective-permute-start.4 = (bf16[128,128]{1,0:T(8,128)(2,1)S(1)}, bf16[128,128]{1,0:T(8,128)(2,1)S(1)}, u32[]{:S(2)}, u32[]{:S(2)}) collective-permute-start(bf16[128,128]{1,0:T(8,128)(2,1)S(1)} %slice_reduce_fusion.sum_ref), channel_id=1, source_target_pairs={{0,1},{1,0},{2,3},{3,2},{4,5},{5,4},{6,7},{7,6},{8,9},{9,8},{10,11... | collective-permute-start | bytes 98312 | tf_op jit(solution)/shard_map/ppermute | solution.py:187
  75.0 6.3 %collective-permute-done.4.other_ref = bf16[128,128]{1,0:T(8,128)(2,1)S(1)} collective-permute-done((bf16[128,128]{1,0:T(8,128)(2,1)S(1)}, bf16[128,128]{1,0:T(8,128)(2,1)S(1)}, u32[]{:S(2)}, u32[]{:S(2)}) %collective-permute-start.4) | collective-permute-done | bytes 32800 | tf_op jit(solution)/shard_map/ppermute | solution.py:187
  81.3 1.2 shard_map.95
  82.5 1.9 %collective-permute-start.5 = (bf16[4,272,128]{2,1,0:T(8,128)(2,1)S(1)}, bf16[4,272,128]{2,1,0:T(8,128)(2,1)S(1)}, u32[]{:S(2)}, u32[]{:S(2)}) collective-permute-start(bf16[4,272,128]{2,1,0:T(8,128)(2,1)S(1)} %get-tuple-element.24), channel_id=1, source_target_pairs={{0,8},{8,0},{1,9},{9,1},{2,10},{10,2},{3,11},{11,3},{4,12},{12,4},... | collective-permute-start | bytes 835592 | tf_op jit(solution)/shard_map/ppermute | solution.py:187
  84.4 1.5 %collective-permute-done.5 = bf16[4,272,128]{2,1,0:T(8,128)(2,1)S(1)} collective-permute-done((bf16[4,272,128]{2,1,0:T(8,128)(2,1)S(1)}, bf16[4,272,128]{2,1,0:T(8,128)(2,1)S(1)}, u32[]{:S(2)}, u32[]{:S(2)}) %collective-permute-start.5) | collective-permute-done | bytes 278560 | tf_op jit(solution)/shard_map/ppermute | solution.py:187
  86.0 0.1 add_convert_fusion
  86.0 11.7 %all_to_all.36.in_ref = bf16[4,272,128]{2,1,0:T(8,128)(2,1)S(1)} all-to-all(bf16[4,272,128]{2,1,0:T(8,128)(2,1)S(1)} %add_convert_fusion), channel_id=1, replica_groups=mesh['y'=4,'zl'=8,'c'=2,'x'=4,'zh'=2] {'y'}, dimensions={0} | all-to-all | bytes 557056 | tf_op jit(solution)/shard_map/all_to_all | solution.py:183
  97.8 26.9 %all_to_all.37.in_ref = bf16[16,48,128]{2,1,0:T(8,128)(2,1)S(1)} all-to-all(bf16[16,48,128]{2,1,0:T(8,128)(2,1)S(1)} %bitcast.27), channel_id=1, replica_groups=mesh['y'=4,'zl'=8,'c'=2,'x'=4,'zh'=2] {'zl','zh'}, dimensions={0} | all-to-all | bytes 393216 | tf_op jit(solution)/shard_map/all_to_all | solution.py:183
  124.7 11.3 %all_to_all.38.in_ref = bf16[16,48,128]{2,1,0:T(8,128)(2,1)S(1)} all-to-all(bf16[16,48,128]{2,1,0:T(8,128)(2,1)S(1)} %shard_map.97), channel_id=1, replica_groups=mesh['y'=4,'zl'=8,'c'=2,'x'=4,'zh'=2] {'y','x'}, dimensions={0} | all-to-all | bytes 393216 | tf_op jit(solution)/shard_map/all_to_all | solution.py:183
  136.0 0.7 shard_map.98
  (14 shorter events, 0.1 us)
Async XLA Ops:
  0.6 9.9 %all-to-all-start = ((bf16[4,32,128]{2,1,0:T(8,128)(2,1)}), bf16[4,32,128]{2,1,0:T(8,128)(2,1)S(1)}, u32[]{:S(2)}, u32[]{:S(2)}) async-start(bf16[4,32,128]{2,1,0:T(8,128)(2,1)} %bitcast.30), calls=%async_computation | async-start | bytes 65536 | tf_op jit(solution)/shard_map/all_to_all | solution.py:183
  5.9 1.2 copy-start
  7.1 0.7 copy-start.1
  11.2 25.2 %all-to-all-start.1 = ((bf16[8,32,128]{2,1,0:T(8,128)(2,1)}), bf16[8,32,128]{2,1,0:T(8,128)(2,1)S(1)}, u32[]{:S(2)}, u32[]{:S(2)}) async-start(bf16[8,32,128]{2,1,0:T(8,128)(2,1)} %broadcast_in_dim.4), calls=%async_computation.1 | async-start | bytes 131072 | tf_op jit(solution)/shard_map/all_to_all | solution.py:183
  23.8 12.5 %copy-start.2 = (bf16[128,32]{0,1:T(8,128)(2,1)S(1)}, bf16[128,32]{0,1:T(8,128)(2,1)}, u32[]{:S(2)}) copy-start(bf16[128,32]{0,1:T(8,128)(2,1)} %param.11) | copy-start | bytes 24580
  23.8 12.5 %copy-start.3 = (bf16[128,32]{0,1:T(8,128)(2,1)S(1)}, bf16[128,32]{0,1:T(8,128)(2,1)}, u32[]{:S(2)}) copy-start(bf16[128,32]{0,1:T(8,128)(2,1)} %param.9) | copy-start | bytes 24580
  25.0 32.1 %collective-permute-start = (bf16[2,8,128,128]{3,2,1,0:T(8,128)(2,1)}, bf16[2,8,128,128]{3,2,1,0:T(8,128)(2,1)S(1)}, u32[]{:S(2)}, u32[]{:S(2)}) collective-permute-start(bf16[2,8,128,128]{3,2,1,0:T(8,128)(2,1)} %get-tuple-element.30), channel_id=1, source_target_pairs={{0,2},{2,4},{4,6},{6,0},{1,3},{3,5},{5,7},{7,1},{8,10},{10,12},{12... | collective-permute-start | bytes 1572872 | tf_op jit(solution)/shard_map/ppermute | solution.py:218
  28.4 28.7 %collective-permute-start.1 = (bf16[2,8,128,128]{3,2,1,0:T(8,128)(2,1)}, bf16[2,8,128,128]{3,2,1,0:T(8,128)(2,1)S(1)}, u32[]{:S(2)}, u32[]{:S(2)}) collective-permute-start(bf16[2,8,128,128]{3,2,1,0:T(8,128)(2,1)} %get-tuple-element.29), channel_id=1, source_target_pairs={{0,4},{2,6},{4,0},{6,2},{1,5},{3,7},{5,1},{7,3},{8,12},{10,14},{12... | collective-permute-start | bytes 1572872 | tf_op jit(solution)/shard_map/ppermute | solution.py:218
  33.0 24.1 %collective-permute-start.2 = (bf16[2,8,128,128]{3,2,1,0:T(8,128)(2,1)S(1)}, bf16[2,8,128,128]{3,2,1,0:T(8,128)(2,1)S(1)}, u32[]{:S(2)}, u32[]{:S(2)}) collective-permute-start(bf16[2,8,128,128]{3,2,1,0:T(8,128)(2,1)S(1)} %get-tuple-element.28), channel_id=1, source_target_pairs={{0,6},{2,0},{4,2},{6,4},{1,7},{3,1},{5,3},{7,5},{8,14},{10,8},{12,... | collective-permute-start | bytes 1572872 | tf_op jit(solution)/shard_map/ppermute | solution.py:218
  39.2 17.9 %all-to-all-start.2 = ((bf16[4,2,8,32,128]{4,3,2,1,0:T(8,128)(2,1)}), bf16[4,2,8,32,128]{4,3,2,1,0:T(8,128)(2,1)S(1)}, u32[]{:S(2)}, u32[]{:S(2)}) async-start(bf16[4,2,8,32,128]{4,3,2,1,0:T(8,128)(2,1)} %broadcast_in_dim.5), calls=%async_computation.2 | async-start | bytes 1048576 | tf_op jit(solution)/shard_map/all_to_all | solution.py:183
  42.7 14.4 %collective-permute-start.3 = (bf16[80,128]{1,0:T(8,128)(2,1)S(1)}, bf16[80,128]{1,0:T(8,128)(2,1)S(1)}, u32[]{:S(2)}, u32[]{:S(2)}) collective-permute-start(bf16[80,128]{1,0:T(8,128)(2,1)S(1)} %pad_maximum_fusion.pack_ref), channel_id=1, source_target_pairs={{0,1},{1,0},{2,3},{3,2},{4,5},{5,4},{6,7},{7,6},{8,9},{9,8},{10,11... | collective-permute-start | bytes 61448 | tf_op jit(solution)/shard_map/ppermute | solution.py:187
  66.8 14.6 %collective-permute-start.4 = (bf16[128,128]{1,0:T(8,128)(2,1)S(1)}, bf16[128,128]{1,0:T(8,128)(2,1)S(1)}, u32[]{:S(2)}, u32[]{:S(2)}) collective-permute-start(bf16[128,128]{1,0:T(8,128)(2,1)S(1)} %slice_reduce_fusion.sum_ref), channel_id=1, source_target_pairs={{0,1},{1,0},{2,3},{3,2},{4,5},{5,4},{6,7},{7,6},{8,9},{9,8},{10,11... | collective-permute-start | bytes 98312 | tf_op jit(solution)/shard_map/ppermute | solution.py:187
  82.5 3.4 %collective-permute-start.5 = (bf16[4,272,128]{2,1,0:T(8,128)(2,1)S(1)}, bf16[4,272,128]{2,1,0:T(8,128)(2,1)S(1)}, u32[]{:S(2)}, u32[]{:S(2)}) collective-permute-start(bf16[4,272,128]{2,1,0:T(8,128)(2,1)S(1)} %get-tuple-element.24), channel_id=1, source_target_pairs={{0,8},{8,0},{1,9},{9,1},{2,10},{10,2},{3,11},{11,3},{4,12},{12,4},... | collective-permute-start | bytes 835592 | tf_op jit(solution)/shard_map/ppermute | solution.py:187

commit v7 on v6

--- a/solution.py
+++ b/solution.py
@@ -45,11 +45,10 @@
         out_ref[at] = acc.astype(BF16)[None, None, None]
 
 
-def forward_kernel(d0_ref, d1_ref, d2_ref, d3_ref, feat_ref, pack_ref, pack_other_ref, a_ref, out_ref):
+def forward_kernel(d0_ref, d1_ref, d2_ref, d3_ref, feat_ref, pack_ref, a_ref, out_ref):
     my_c = lax.axis_index("c")
     tile = d0_ref.shape[-1]
     feat = feat_ref.shape[-1]
-    size = pack_ref.shape[0]
     zl_n = d0_ref.shape[1]
     acc = jnp.zeros((tile, feat), F32)
     for core in range(2):
@@ -64,30 +63,50 @@
     part = acc.astype(BF16)
     for x in range(out_ref.shape[0]):
         out_ref[x, :tile, :] = part
-        out_ref[x, tile : tile + size, :] = pack_ref[...]
-        out_ref[x, tile + size :, :] = pack_other_ref[...]
-
-
-def backward_kernel(sum_ref, other_ref, packs_ref, pack_ref, a_ref, act_ref, own_ref, oth_ref):
-    x_n = packs_ref.shape[0]
+        out_ref[x, tile:, :] = pack_ref[...]
+
+
+def row_sum_kernel(hidden, in_ref, out_ref):
+    tile = in_ref.shape[2]
+    x_n = in_ref.shape[0]
+    size = 2 * hidden
+    total = in_ref[0, :tile, :].astype(F32)
+    for x in range(1, x_n):
+        total = total + in_ref[x, :tile, :].astype(F32)
+    out_ref[:tile, :] = total.astype(BF16)
+    for x in range(x_n):
+        out_ref[tile + x * size : tile + (x + 1) * size, :] = in_ref[x, tile : tile + size, :]
+    terms = [in_ref[x, tile + size :, :].astype(F32)[:4] for x in range(x_n)]
+    terms = jnp.concatenate(terms + [jnp.zeros((16 - 4 * x_n, tile), F32)] * (x_n < 4), axis=0)
+    out_ref[tile + x_n * size :, :] = terms.astype(BF16)
+
+
+def backward_kernel(x_n, sum_ref, other_ref, pack_ref, a_ref, act_ref, own_ref, oth_ref):
     hidden = act_ref.shape[0]
     tile = a_ref.shape[-1]
     zl_n = a_ref.shape[1]
-    size = pack_ref.shape[0]
     y_n = own_ref.shape[0]
     rows = tile // y_n
-    agg = (sum_ref[...].astype(F32) + other_ref[...].astype(F32)).astype(BF16)
-    starts = [(x, tile + z * size) for x in range(x_n) for z in range(2)]
+    agg = (sum_ref[:tile, :].astype(F32) + other_ref[:tile, :].astype(F32)).astype(BF16)
 
     def gather(start, count):
-        return jnp.concatenate([packs_ref[x, at + start : at + start + count, :] for x, at in starts], axis=0)
+        parts = [
+            ref[tile + x * 2 * hidden + start : tile + x * 2 * hidden + start + count, :]
+            for ref in (sum_ref, other_ref)
+            for x in range(x_n)
+        ]
+        return jnp.concatenate(parts, axis=0)
 
     def bias_of(three):
         return mm(three, jnp.ones((three.shape[0], tile), BF16), 0, 0)[:hidden]
 
+    def biases(ref):
+        terms = ref[tile + x_n * 2 * hidden :, :].astype(F32)
+        return [bias_of(terms[4 * x : 4 * x + 4].astype(BF16)) for x in range(x_n)]
+
     w_t = gather(0, hidden)
     cot_t = gather(hidden, hidden)
-    bias_t = jnp.concatenate([bias_of(packs_ref[x, at + 2 * hidden : at + size, :]) for x, at in starts], axis=0)
+    bias_t = jnp.concatenate(biases(sum_ref) + biases(other_ref), axis=0)
     pre_t = mm(w_t, agg, 1, 1) + bias_t
     grad_t = (cot_t.astype(F32) * slope(pre_t)).astype(BF16)
     back_t = mm(w_t, grad_t, 0, 0).astype(BF16)
@@ -220,30 +239,28 @@
         pieces.append(pieces[0])
     column = to_all(jnp.broadcast_to(mine[None], (zl_n, rows, feat)), "zl")
     column = lax.all_gather(column, "c")
-    column, pack = lax.optimization_barrier((column, pack))
-    pack_other = swap(pack, "zh")
     blocks = to_all(jnp.broadcast_to(column[None], (y_n,) + column.shape), "y")
 
-    size = pack.shape[0]
     a_mine, part = call(
         forward_kernel,
-        (shape(c_n, zl_n, tile, tile), shape(x_n, tile + 2 * size, feat)),
+        (shape(c_n, zl_n, tile, tile), shape(x_n, tile + pack.shape[0], feat)),
         *pieces,
         blocks,
         pack,
-        pack_other,
-    )
-    part = to_all(part, "x")
-    summed = jnp.sum(part[:, :tile].astype(F32), axis=0).astype(BF16)
+    )
+    summed = call(
+        functools.partial(row_sum_kernel, hidden),
+        shape(tile + x_n * 2 * hidden + 16, feat),
+        to_all(part, "x"),
+    )
     summed_other = swap(summed, "zh")
 
     payload = shape(y_n, zl_n * rows + EXTRA, tile)
     act_t, keep, give = call(
-        backward_kernel,
+        functools.partial(backward_kernel, x_n),
         (shape(hidden, tile), payload, payload),
         summed,
         summed_other,
-        part,
         pack,
         a_mine,
     )

time: 137 us -> 138 us (level)
  starting transfers between devices: 50.3 us -> 42.1 us
  waiting for transfers between devices: 15.6 us -> 22.1 us
  blocking collectives: 61 us -> 64.5 us
    ppermute x3, waiting for transfers between devices: 0.01 us -> 11 us  [on_device(): lax.ppermute(dense[step], 'x', [(x, (x + step) % x_n) for x in range(x_n)])]
    ppermute x3 -> x2, starting transfers between devices: 18.4 us -> 10.1 us  [swap(): return lax.ppermute(v, axis, [(0, 1), (1, 0)])]
    ppermute x3 -> x2, waiting for transfers between devices: 14 us -> 8.88 us  [swap(): return lax.ppermute(v, axis, [(0, 1), (1, 0)])]
    all_to_all x4, blocking collectives: 59.1 us -> 62.6 us  [to_all(): return lax.all_to_all(v, axes, 0, 0, tiled=True)]
    pallas_call x6 -> x7, Pallas kernels: 3.67 us -> 3.69 us  [call(): pl.pallas_call(kernel, out_shape=out, in_specs=[SMEM] * smem + [VMEM] * (...]
  transfers between devices with their start and end apart: 9 -> 8, of which waited for: 4 -> 5; matrix products, arithmetic and copies ran while one was open for 2% -> 2% of each run, Pallas kernels for 1% -> 1%
where the time goes in v7:
time: 138 us
  blocking collectives  64.5 us (47%)
  starting transfers between devices  42.1 us (31%)
  waiting for transfers between devices  22.1 us (16%)
  local copies, waits for them, and re-layouts  4.59 us (3%)
  Pallas kernels  3.69 us (3%)
    all_to_all x4, blocking collectives, to_all(): return lax.all_to_all(v, axes, 0, 0, tiled=True)  62.6 us
    all_to_all x3, starting transfers between devices, to_all(): return lax.all_to_all(v, axes, 0, 0, tiled=True)  20.6 us
    ppermute x3, starting transfers between devices, on_device(): lax.ppermute(dense[step], 'x', [(x, (x + step) % x_n) for x in range(x_n)])  11.4 us
    ppermute x3, waiting for transfers between devices, on_device(): lax.ppermute(dense[step], 'x', [(x, (x + step) % x_n) for x in range(x_n)])  11 us
    ppermute x2, starting transfers between devices, swap(): return lax.ppermute(v, axis, [(0, 1), (1, 0)])  10.1 us
    ppermute x2, waiting for transfers between devices, swap(): return lax.ppermute(v, axis, [(0, 1), (1, 0)])  8.88 us
    pallas_call x7, Pallas kernels, call(): pl.pallas_call(kernel, out_shape=out, in_specs=[SMEM] * smem + [VMEM] * (...  3.69 us
  transfers between devices with their start and end apart: 8, of which 5 were waited for; matrix products, arithmetic and copies ran while one was open for 2% of the time, Pallas kernels for 1%

profile of v7, /device:TPU:32, one launch (start us, length us, event | category | flops | bytes accessed | tf_op | source)
XLA Modules:
  0.0 137.9 jit_solution(16515667607150744814)
XLA Ops:
  0.6 4.5 %all-to-all-start = ((bf16[4,32,128]{2,1,0:T(8,128)(2,1)}), bf16[4,32,128]{2,1,0:T(8,128)(2,1)S(1)}, u32[]{:S(2)}, u32[]{:S(2)}) async-start(bf16[4,32,128]{2,1,0:T(8,128)(2,1)} %bitcast.30), calls=%async_computation | async-start | bytes 65536 | tf_op jit(solution)/shard_map/all_to_all | solution.py:202
  5.1 1.2 copy-done
  6.3 0.7 copy-done.1
  7.0 1.3 shard_map.93
  8.3 2.3 %all-to-all-done = bf16[4,32,128]{2,1,0:T(8,128)(2,1)S(1)} async-done(((bf16[4,32,128]{2,1,0:T(8,128)(2,1)}), bf16[4,32,128]{2,1,0:T(8,128)(2,1)S(1)}, u32[]{:S(2)}, u32[]{:S(2)}) %all-to-all-start) | async-done | bytes 32800 | tf_op jit(solution)/shard_map/all_to_all | solution.py:202
  10.6 0.6 broadcast_in_dim.4
  11.2 12.6 %all-to-all-start.1 = ((bf16[8,32,128]{2,1,0:T(8,128)(2,1)}), bf16[8,32,128]{2,1,0:T(8,128)(2,1)S(1)}, u32[]{:S(2)}, u32[]{:S(2)}) async-start(bf16[8,32,128]{2,1,0:T(8,128)(2,1)} %broadcast_in_dim.4), calls=%async_computation.1 | async-start | bytes 131072 | tf_op jit(solution)/shard_map/all_to_all | solution.py:202
  23.8 1.2 slice_bitcast_fusion
  25.0 3.4 %collective-permute-start = (bf16[2,8,128,128]{3,2,1,0:T(8,128)(2,1)}, bf16[2,8,128,128]{3,2,1,0:T(8,128)(2,1)S(1)}, u32[]{:S(2)}, u32[]{:S(2)}) collective-permute-start(bf16[2,8,128,128]{3,2,1,0:T(8,128)(2,1)} %get-tuple-element.26), channel_id=1, source_target_pairs={{0,2},{2,4},{4,6},{6,0},{1,3},{3,5},{5,7},{7,1},{8,10},{10,12},{12... | collective-permute-start | bytes 1572872 | tf_op jit(solution)/shard_map/ppermute | solution.py:237
  28.4 4.6 %collective-permute-start.1 = (bf16[2,8,128,128]{3,2,1,0:T(8,128)(2,1)}, bf16[2,8,128,128]{3,2,1,0:T(8,128)(2,1)S(1)}, u32[]{:S(2)}, u32[]{:S(2)}) collective-permute-start(bf16[2,8,128,128]{3,2,1,0:T(8,128)(2,1)} %get-tuple-element.25), channel_id=1, source_target_pairs={{0,4},{2,6},{4,0},{6,2},{1,5},{3,7},{5,1},{7,3},{8,12},{10,14},{12... | collective-permute-start | bytes 1572872 | tf_op jit(solution)/shard_map/ppermute | solution.py:237
  33.0 3.3 %collective-permute-start.2 = (bf16[2,8,128,128]{3,2,1,0:T(8,128)(2,1)S(1)}, bf16[2,8,128,128]{3,2,1,0:T(8,128)(2,1)S(1)}, u32[]{:S(2)}, u32[]{:S(2)}) collective-permute-start(bf16[2,8,128,128]{3,2,1,0:T(8,128)(2,1)S(1)} %get-tuple-element.24), channel_id=1, source_target_pairs={{0,6},{2,0},{4,2},{6,4},{1,7},{3,1},{5,3},{7,5},{8,14},{10,8},{12,... | collective-permute-start | bytes 1572872 | tf_op jit(solution)/shard_map/ppermute | solution.py:237
  36.4 0.0 all-to-all-done.1
  36.4 1.9 %all-gather = bf16[16,32,128]{2,1,0:T(8,128)(2,1)S(1)} all-gather(bf16[8,32,128]{2,1,0:T(8,128)(2,1)S(1)} %all-to-all-done.1), channel_id=2, replica_groups=mesh['y'=4,'zl'=8,'c'=2,'x'=4,'zh'=2] {'c'}, dimensions={0}, use_global_device_ids=true | all-gather | bytes 196608 | tf_op jit(solution)/shard_map/all_gather | solution.py:241
  38.3 0.9 broadcast_in_dim.5
  39.2 3.5 %all-to-all-start.2 = ((bf16[4,2,8,32,128]{4,3,2,1,0:T(8,128)(2,1)}), bf16[4,2,8,32,128]{4,3,2,1,0:T(8,128)(2,1)S(1)}, u32[]{:S(2)}, u32[]{:S(2)}) async-start(bf16[4,2,8,32,128]{4,3,2,1,0:T(8,128)(2,1)} %broadcast_in_dim.5), calls=%async_computation.2 | async-start | bytes 1048576 | tf_op jit(solution)/shard_map/all_to_all | solution.py:202
  42.7 0.0 copy-done.4
  42.8 0.0 collective-permute-done.d1_ref
  42.8 9.4 %collective-permute-done.1.d2_ref = bf16[2,8,128,128]{3,2,1,0:T(8,128)(2,1)S(1)} collective-permute-done((bf16[2,8,128,128]{3,2,1,0:T(8,128)(2,1)}, bf16[2,8,128,128]{3,2,1,0:T(8,128)(2,1)S(1)}, u32[]{:S(2)}, u32[]{:S(2)}) %collective-permute-start.1) | collective-permute-done | bytes 524320 | tf_op jit(solution)/shard_map/ppermute | solution.py:237
  52.2 1.6 %collective-permute-done.2.d3_ref = bf16[2,8,128,128]{3,2,1,0:T(8,128)(2,1)S(1)} collective-permute-done((bf16[2,8,128,128]{3,2,1,0:T(8,128)(2,1)S(1)}, bf16[2,8,128,128]{3,2,1,0:T(8,128)(2,1)S(1)}, u32[]{:S(2)}, u32[]{:S(2)}) %collective-permute-start.2) | collective-permute-done | bytes 524320 | tf_op jit(solution)/shard_map/ppermute | solution.py:237
  53.7 0.0 all-to-all-done.2.feat_ref
  53.8 0.4 shard_map.94
  54.1 10.5 %all_to_all.35.in_ref = bf16[4,208,128]{2,1,0:T(8,128)(2,1)S(1)} all-to-all(bf16[4,208,128]{2,1,0:T(8,128)(2,1)S(1)} %get-tuple-element.16), channel_id=1, replica_groups=mesh['y'=4,'zl'=8,'c'=2,'x'=4,'zh'=2] {'x'}, dimensions={0} | all-to-all | bytes 425984 | tf_op jit(solution)/shard_map/all_to_all | solution.py:202
  64.7 8.2 %collective-permute-start.3 = (bf16[400,128]{1,0:T(8,128)(2,1)S(1)}, bf16[400,128]{1,0:T(8,128)(2,1)S(1)}, u32[]{:S(2)}, u32[]{:S(2)}) collective-permute-start(bf16[400,128]{1,0:T(8,128)(2,1)S(1)} %shard_map.95.sum_ref), channel_id=1, source_target_pairs={{0,1},{1,0},{2,3},{3,2},{4,5},{5,4},{6,7},{7,6},{8,9},{9,8},{10,11... | collective-permute-start | bytes 307208 | tf_op jit(solution)/shard_map/ppermute | solution.py:206
  72.9 7.4 %collective-permute-done.3.other_ref = bf16[400,128]{1,0:T(8,128)(2,1)S(1)} collective-permute-done((bf16[400,128]{1,0:T(8,128)(2,1)S(1)}, bf16[400,128]{1,0:T(8,128)(2,1)S(1)}, u32[]{:S(2)}, u32[]{:S(2)}) %collective-permute-start.3) | collective-permute-done | bytes 102432 | tf_op jit(solution)/shard_map/ppermute | solution.py:206
  80.3 1.2 shard_map.96
  81.5 1.9 %collective-permute-start.4 = (bf16[4,272,128]{2,1,0:T(8,128)(2,1)S(1)}, bf16[4,272,128]{2,1,0:T(8,128)(2,1)S(1)}, u32[]{:S(2)}, u32[]{:S(2)}) collective-permute-start(bf16[4,272,128]{2,1,0:T(8,128)(2,1)S(1)} %get-tuple-element.20), channel_id=1, source_target_pairs={{0,8},{8,0},{1,9},{9,1},{2,10},{10,2},{3,11},{11,3},{4,12},{12,4},... | collective-permute-start | bytes 835592 | tf_op jit(solution)/shard_map/ppermute | solution.py:206
  83.4 1.5 %collective-permute-done.4 = bf16[4,272,128]{2,1,0:T(8,128)(2,1)S(1)} collective-permute-done((bf16[4,272,128]{2,1,0:T(8,128)(2,1)S(1)}, bf16[4,272,128]{2,1,0:T(8,128)(2,1)S(1)}, u32[]{:S(2)}, u32[]{:S(2)}) %collective-permute-start.4) | collective-permute-done | bytes 278560 | tf_op jit(solution)/shard_map/ppermute | solution.py:206
  84.9 0.1 add_convert_fusion
  85.0 10.4 %all_to_all.36.in_ref = bf16[4,272,128]{2,1,0:T(8,128)(2,1)S(1)} all-to-all(bf16[4,272,128]{2,1,0:T(8,128)(2,1)S(1)} %add_convert_fusion), channel_id=1, replica_groups=mesh['y'=4,'zl'=8,'c'=2,'x'=4,'zh'=2] {'y'}, dimensions={0} | all-to-all | bytes 557056 | tf_op jit(solution)/shard_map/all_to_all | solution.py:202
  95.4 30.3 %all_to_all.37.in_ref = bf16[16,48,128]{2,1,0:T(8,128)(2,1)S(1)} all-to-all(bf16[16,48,128]{2,1,0:T(8,128)(2,1)S(1)} %bitcast.27), channel_id=1, replica_groups=mesh['y'=4,'zl'=8,'c'=2,'x'=4,'zh'=2] {'zl','zh'}, dimensions={0} | all-to-all | bytes 393216 | tf_op jit(solution)/shard_map/all_to_all | solution.py:202
  125.7 11.4 %all_to_all.38.in_ref = bf16[16,48,128]{2,1,0:T(8,128)(2,1)S(1)} all-to-all(bf16[16,48,128]{2,1,0:T(8,128)(2,1)S(1)} %shard_map.98), channel_id=1, replica_groups=mesh['y'=4,'zl'=8,'c'=2,'x'=4,'zh'=2] {'y','x'}, dimensions={0} | all-to-all | bytes 393216 | tf_op jit(solution)/shard_map/all_to_all | solution.py:202
  137.1 0.7 shard_map.99
  (14 shorter events, 0.1 us)
Async XLA Ops:
  0.6 9.9 %all-to-all-start = ((bf16[4,32,128]{2,1,0:T(8,128)(2,1)}), bf16[4,32,128]{2,1,0:T(8,128)(2,1)S(1)}, u32[]{:S(2)}, u32[]{:S(2)}) async-start(bf16[4,32,128]{2,1,0:T(8,128)(2,1)} %bitcast.30), calls=%async_computation | async-start | bytes 65536 | tf_op jit(solution)/shard_map/all_to_all | solution.py:202
  5.1 1.2 copy-start
  6.3 0.7 copy-start.1
  11.2 25.2 %all-to-all-start.1 = ((bf16[8,32,128]{2,1,0:T(8,128)(2,1)}), bf16[8,32,128]{2,1,0:T(8,128)(2,1)S(1)}, u32[]{:S(2)}, u32[]{:S(2)}) async-start(bf16[8,32,128]{2,1,0:T(8,128)(2,1)} %broadcast_in_dim.4), calls=%async_computation.1 | async-start | bytes 131072 | tf_op jit(solution)/shard_map/all_to_all | solution.py:202
  23.8 18.9 %copy-start.4 = (f32[32]{0:T(128)S(1)}, f32[32]{0:T(128)}, u32[]{:S(2)}) copy-start(f32[32]{0:T(128)} %param.10) | copy-start | bytes 388
  23.8 18.9 %copy-start.2 = (bf16[128,32]{0,1:T(8,128)(2,1)S(1)}, bf16[128,32]{0,1:T(8,128)(2,1)}, u32[]{:S(2)}) copy-start(bf16[128,32]{0,1:T(8,128)(2,1)} %param.11) | copy-start | bytes 24580
  23.8 18.9 %copy-start.3 = (bf16[128,32]{0,1:T(8,128)(2,1)S(1)}, bf16[128,32]{0,1:T(8,128)(2,1)}, u32[]{:S(2)}) copy-start(bf16[128,32]{0,1:T(8,128)(2,1)} %param.9) | copy-start | bytes 24580
  25.0 17.8 %collective-permute-start = (bf16[2,8,128,128]{3,2,1,0:T(8,128)(2,1)}, bf16[2,8,128,128]{3,2,1,0:T(8,128)(2,1)S(1)}, u32[]{:S(2)}, u32[]{:S(2)}) collective-permute-start(bf16[2,8,128,128]{3,2,1,0:T(8,128)(2,1)} %get-tuple-element.26), channel_id=1, source_target_pairs={{0,2},{2,4},{4,6},{6,0},{1,3},{3,5},{5,7},{7,1},{8,10},{10,12},{12... | collective-permute-start | bytes 1572872 | tf_op jit(solution)/shard_map/ppermute | solution.py:237
  28.4 23.8 %collective-permute-start.1 = (bf16[2,8,128,128]{3,2,1,0:T(8,128)(2,1)}, bf16[2,8,128,128]{3,2,1,0:T(8,128)(2,1)S(1)}, u32[]{:S(2)}, u32[]{:S(2)}) collective-permute-start(bf16[2,8,128,128]{3,2,1,0:T(8,128)(2,1)} %get-tuple-element.25), channel_id=1, source_target_pairs={{0,4},{2,6},{4,0},{6,2},{1,5},{3,7},{5,1},{7,3},{8,12},{10,14},{12... | collective-permute-start | bytes 1572872 | tf_op jit(solution)/shard_map/ppermute | solution.py:237
  33.0 20.7 %collective-permute-start.2 = (bf16[2,8,128,128]{3,2,1,0:T(8,128)(2,1)S(1)}, bf16[2,8,128,128]{3,2,1,0:T(8,128)(2,1)S(1)}, u32[]{:S(2)}, u32[]{:S(2)}) collective-permute-start(bf16[2,8,128,128]{3,2,1,0:T(8,128)(2,1)S(1)} %get-tuple-element.24), channel_id=1, source_target_pairs={{0,6},{2,0},{4,2},{6,4},{1,7},{3,1},{5,3},{7,5},{8,14},{10,8},{12,... | collective-permute-start | bytes 1572872 | tf_op jit(solution)/shard_map/ppermute | solution.py:237
  39.2 14.5 %all-to-all-start.2 = ((bf16[4,2,8,32,128]{4,3,2,1,0:T(8,128)(2,1)}), bf16[4,2,8,32,128]{4,3,2,1,0:T(8,128)(2,1)S(1)}, u32[]{:S(2)}, u32[]{:S(2)}) async-start(bf16[4,2,8,32,128]{4,3,2,1,0:T(8,128)(2,1)} %broadcast_in_dim.5), calls=%async_computation.2 | async-start | bytes 1048576 | tf_op jit(solution)/shard_map/all_to_all | solution.py:202
  64.7 15.6 %collective-permute-start.3 = (bf16[400,128]{1,0:T(8,128)(2,1)S(1)}, bf16[400,128]{1,0:T(8,128)(2,1)S(1)}, u32[]{:S(2)}, u32[]{:S(2)}) collective-permute-start(bf16[400,128]{1,0:T(8,128)(2,1)S(1)} %shard_map.95.sum_ref), channel_id=1, source_target_pairs={{0,1},{1,0},{2,3},{3,2},{4,5},{5,4},{6,7},{7,6},{8,9},{9,8},{10,11... | collective-permute-start | bytes 307208 | tf_op jit(solution)/shard_map/ppermute | solution.py:206
  81.5 3.4 %collective-permute-start.4 = (bf16[4,272,128]{2,1,0:T(8,128)(2,1)S(1)}, bf16[4,272,128]{2,1,0:T(8,128)(2,1)S(1)}, u32[]{:S(2)}, u32[]{:S(2)}) collective-permute-start(bf16[4,272,128]{2,1,0:T(8,128)(2,1)S(1)} %get-tuple-element.20), channel_id=1, source_target_pairs={{0,8},{8,0},{1,9},{9,1},{2,10},{10,2},{3,11},{11,3},{4,12},{12,4},... | collective-permute-start | bytes 835592 | tf_op jit(solution)/shard_map/ppermute | solution.py:206

commit v8 on v7

--- a/solution.py
+++ b/solution.py
@@ -231,14 +231,16 @@
 
     quarters = to_all(features.reshape(y_n, rows, feat), "y")
     mine = lax.dynamic_index_in_dim(quarters, my_x, 0, keepdims=False)
+    def along_x(v, step):
+        return lax.ppermute(v, "x", [(x, (x + step) % x_n) for x in range(x_n)])
+
     mine, dense = lax.optimization_barrier((mine, dense))
-    pieces = [dense[0]]
-    for step in range(1, x_n):
-        pieces.append(lax.ppermute(dense[step], "x", [(x, (x + step) % x_n) for x in range(x_n)]))
-    while len(pieces) < 4:
-        pieces.append(pieces[0])
+    shares = [along_x(dense[step], step) for step in range(1, x_n)]
     column = to_all(jnp.broadcast_to(mine[None], (zl_n, rows, feat)), "zl")
     column = lax.all_gather(column, "c")
+    if x_n > 2:
+        column, shares[1] = lax.optimization_barrier((column, shares[1]))
+    pieces = ([dense[0]] + shares + [dense[0]] * 2)[:4]
     blocks = to_all(jnp.broadcast_to(column[None], (y_n,) + column.shape), "y")
 
     a_mine, part = call(

time: 138 us -> 139 us (level)
  blocking collectives: 64.5 us -> 59.8 us
  waiting for transfers between devices: 22.1 us -> 26.4 us
    all_to_all x3, waiting for transfers between devices: 2.26 us -> 14.4 us  [to_all(): return lax.all_to_all(v, axes, 0, 0, tiled=True)]
    ppermute x3, waiting for transfers between devices: 11 us -> 0.07 us  [along_x(): return lax.ppermute(v, 'x', [(x, (x + step) % x_n) for x in range(x_n)])]
    all_to_all x4, blocking collectives: 62.6 us -> 57.9 us  [to_all(): return lax.all_to_all(v, axes, 0, 0, tiled=True)]
    ppermute x2, waiting for transfers between devices: 8.88 us -> 12 us  [swap(): return lax.ppermute(v, axis, [(0, 1), (1, 0)])]
  transfers between devices with their start and end apart: 8 -> 8, of which waited for: 5 -> 6; matrix products, arithmetic and copies ran while one was open for 2% -> 1% of each run, Pallas kernels for 1% -> 1%
where the time goes in v8:
time: 139 us; the launch traced here: 138 us
  blocking collectives  59.8 us (43%)
  starting transfers between devices  42.8 us (31%)
  waiting for transfers between devices  26.4 us (19%)
  local copies, waits for them, and re-layouts  4.55 us (3%)
  Pallas kernels  3.69 us (3%)
    all_to_all x4, blocking collectives, to_all(): return lax.all_to_all(v, axes, 0, 0, tiled=True)  57.9 us
    all_to_all x3, starting transfers between devices, to_all(): return lax.all_to_all(v, axes, 0, 0, tiled=True)  20.6 us
    all_to_all x3, waiting for transfers between devices, to_all(): return lax.all_to_all(v, axes, 0, 0, tiled=True)  14.4 us
    ppermute x3, starting transfers between devices, along_x(): return lax.ppermute(v, 'x', [(x, (x + step) % x_n) for x in range(x_n)])  12.1 us
    ppermute x2, waiting for transfers between devices, swap(): return lax.ppermute(v, axis, [(0, 1), (1, 0)])  12 us
    ppermute x2, starting transfers between devices, swap(): return lax.ppermute(v, axis, [(0, 1), (1, 0)])  10.1 us
    pallas_call x7, Pallas kernels, call(): pl.pallas_call(kernel, out_shape=out, in_specs=[SMEM] * smem + [VMEM] * (...  3.69 us
  transfers between devices with their start and end apart: 8, of which 6 were waited for; matrix products, arithmetic and copies ran while one was open for 1% of the time, Pallas kernels for 1%

profile of v8, /device:TPU:32, one launch (start us, length us, event | category | flops | bytes accessed | tf_op | source)
XLA Modules:
  0.0 138.2 jit_solution(4173924557478632342)
XLA Ops:
  0.6 4.5 %all-to-all-start = ((bf16[4,32,128]{2,1,0:T(8,128)(2,1)}), bf16[4,32,128]{2,1,0:T(8,128)(2,1)S(1)}, u32[]{:S(2)}, u32[]{:S(2)}) async-start(bf16[4,32,128]{2,1,0:T(8,128)(2,1)} %bitcast.30), calls=%async_computation | async-start | bytes 65536 | tf_op jit(solution)/shard_map/all_to_all | solution.py:202
  5.1 1.2 copy-done
  6.3 0.7 copy-done.1
  7.0 1.3 shard_map.93
  8.3 2.3 %all-to-all-done = bf16[4,32,128]{2,1,0:T(8,128)(2,1)S(1)} async-done(((bf16[4,32,128]{2,1,0:T(8,128)(2,1)}), bf16[4,32,128]{2,1,0:T(8,128)(2,1)S(1)}, u32[]{:S(2)}, u32[]{:S(2)}) %all-to-all-start) | async-done | bytes 32800 | tf_op jit(solution)/shard_map/all_to_all | solution.py:202
  10.6 1.1 slice_bitcast_fusion
  11.7 5.1 %collective-permute-start.1 = (bf16[2,8,128,128]{3,2,1,0:T(8,128)(2,1)}, bf16[2,8,128,128]{3,2,1,0:T(8,128)(2,1)S(1)}, u32[]{:S(2)}, u32[]{:S(2)}) collective-permute-start(bf16[2,8,128,128]{3,2,1,0:T(8,128)(2,1)} %get-tuple-element.29), channel_id=1, source_target_pairs={{0,4},{2,6},{4,0},{6,2},{1,5},{3,7},{5,1},{7,3},{8,12},{10,14},{12... | collective-permute-start | bytes 1572872 | tf_op jit(solution)/shard_map/ppermute | solution.py:235
  16.8 0.6 broadcast_in_dim.4
  17.4 12.6 %all-to-all-start.1 = ((bf16[8,32,128]{2,1,0:T(8,128)(2,1)}), bf16[8,32,128]{2,1,0:T(8,128)(2,1)S(1)}, u32[]{:S(2)}, u32[]{:S(2)}) async-start(bf16[8,32,128]{2,1,0:T(8,128)(2,1)} %broadcast_in_dim.4), calls=%async_computation.1 | async-start | bytes 131072 | tf_op jit(solution)/shard_map/all_to_all | solution.py:202
  30.0 2.5 %collective-permute-start = (bf16[2,8,128,128]{3,2,1,0:T(8,128)(2,1)}, bf16[2,8,128,128]{3,2,1,0:T(8,128)(2,1)S(1)}, u32[]{:S(2)}, u32[]{:S(2)}) collective-permute-start(bf16[2,8,128,128]{3,2,1,0:T(8,128)(2,1)} %get-tuple-element.30), channel_id=1, source_target_pairs={{0,2},{2,4},{4,6},{6,0},{1,3},{3,5},{5,7},{7,1},{8,10},{10,12},{12... | collective-permute-start | bytes 1572872 | tf_op jit(solution)/shard_map/ppermute | solution.py:235
  32.5 4.6 %collective-permute-start.2 = (bf16[2,8,128,128]{3,2,1,0:T(8,128)(2,1)S(1)}, bf16[2,8,128,128]{3,2,1,0:T(8,128)(2,1)S(1)}, u32[]{:S(2)}, u32[]{:S(2)}) collective-permute-start(bf16[2,8,128,128]{3,2,1,0:T(8,128)(2,1)S(1)} %get-tuple-element.28), channel_id=1, source_target_pairs={{0,6},{2,0},{4,2},{6,4},{1,7},{3,1},{5,3},{7,5},{8,14},{10,8},{12,... | collective-permute-start | bytes 1572872 | tf_op jit(solution)/shard_map/ppermute | solution.py:235
  37.1 2.2 %all-to-all-done.1 = bf16[8,32,128]{2,1,0:T(8,128)(2,1)S(1)} async-done(((bf16[8,32,128]{2,1,0:T(8,128)(2,1)}), bf16[8,32,128]{2,1,0:T(8,128)(2,1)S(1)}, u32[]{:S(2)}, u32[]{:S(2)}) %all-to-all-start.1) | async-done | bytes 65568 | tf_op jit(solution)/shard_map/all_to_all | solution.py:202
  39.3 1.9 %all-gather = bf16[16,32,128]{2,1,0:T(8,128)(2,1)S(1)} all-gather(bf16[8,32,128]{2,1,0:T(8,128)(2,1)S(1)} %all-to-all-done.1), channel_id=2, replica_groups=mesh['y'=4,'zl'=8,'c'=2,'x'=4,'zh'=2] {'c'}, dimensions={0}, use_global_device_ids=true | all-gather | bytes 196608 | tf_op jit(solution)/shard_map/all_gather | solution.py:240
  41.2 0.0 collective-permute-done.1.d2_ref
  41.2 0.9 broadcast_in_dim.5
  42.1 3.5 %all-to-all-start.2 = ((bf16[4,2,8,32,128]{4,3,2,1,0:T(8,128)(2,1)}), bf16[4,2,8,32,128]{4,3,2,1,0:T(8,128)(2,1)S(1)}, u32[]{:S(2)}, u32[]{:S(2)}) async-start(bf16[4,2,8,32,128]{4,3,2,1,0:T(8,128)(2,1)} %broadcast_in_dim.5), calls=%async_computation.2 | async-start | bytes 1048576 | tf_op jit(solution)/shard_map/all_to_all | solution.py:202
  45.6 0.0 copy-done.4
  45.6 0.0 collective-permute-done.d1_ref
  45.6 0.1 collective-permute-done.2.d3_ref
  45.7 9.9 %all-to-all-done.2.feat_ref = bf16[4,2,8,32,128]{4,3,2,1,0:T(8,128)(2,1)S(1)} async-done(((bf16[4,2,8,32,128]{4,3,2,1,0:T(8,128)(2,1)}), bf16[4,2,8,32,128]{4,3,2,1,0:T(8,128)(2,1)S(1)}, u32[]{:S(2)}, u32[]{:S(2)}) %all-to-all-start.2) | async-done | bytes 524320 | tf_op jit(solution)/shard_map/all_to_all | solution.py:202
  55.6 0.4 shard_map.94
  56.0 8.8 %all_to_all.35.in_ref = bf16[4,208,128]{2,1,0:T(8,128)(2,1)S(1)} all-to-all(bf16[4,208,128]{2,1,0:T(8,128)(2,1)S(1)} %get-tuple-element.20), channel_id=1, replica_groups=mesh['y'=4,'zl'=8,'c'=2,'x'=4,'zh'=2] {'x'}, dimensions={0} | all-to-all | bytes 425984 | tf_op jit(solution)/shard_map/all_to_all | solution.py:202
  64.8 8.2 %collective-permute-start.3 = (bf16[400,128]{1,0:T(8,128)(2,1)S(1)}, bf16[400,128]{1,0:T(8,128)(2,1)S(1)}, u32[]{:S(2)}, u32[]{:S(2)}) collective-permute-start(bf16[400,128]{1,0:T(8,128)(2,1)S(1)} %shard_map.95.sum_ref), channel_id=1, source_target_pairs={{0,1},{1,0},{2,3},{3,2},{4,5},{5,4},{6,7},{7,6},{8,9},{9,8},{10,11... | collective-permute-start | bytes 307208 | tf_op jit(solution)/shard_map/ppermute | solution.py:206
  73.0 10.5 %collective-permute-done.3.other_ref = bf16[400,128]{1,0:T(8,128)(2,1)S(1)} collective-permute-done((bf16[400,128]{1,0:T(8,128)(2,1)S(1)}, bf16[400,128]{1,0:T(8,128)(2,1)S(1)}, u32[]{:S(2)}, u32[]{:S(2)}) %collective-permute-start.3) | collective-permute-done | bytes 102432 | tf_op jit(solution)/shard_map/ppermute | solution.py:206
  83.5 1.2 shard_map.96
  84.7 1.9 %collective-permute-start.4 = (bf16[4,272,128]{2,1,0:T(8,128)(2,1)S(1)}, bf16[4,272,128]{2,1,0:T(8,128)(2,1)S(1)}, u32[]{:S(2)}, u32[]{:S(2)}) collective-permute-start(bf16[4,272,128]{2,1,0:T(8,128)(2,1)S(1)} %get-tuple-element.24), channel_id=1, source_target_pairs={{0,8},{8,0},{1,9},{9,1},{2,10},{10,2},{3,11},{11,3},{4,12},{12,4},... | collective-permute-start | bytes 835592 | tf_op jit(solution)/shard_map/ppermute | solution.py:206
  86.6 1.5 %collective-permute-done.4 = bf16[4,272,128]{2,1,0:T(8,128)(2,1)S(1)} collective-permute-done((bf16[4,272,128]{2,1,0:T(8,128)(2,1)S(1)}, bf16[4,272,128]{2,1,0:T(8,128)(2,1)S(1)}, u32[]{:S(2)}, u32[]{:S(2)}) %collective-permute-start.4) | collective-permute-done | bytes 278560 | tf_op jit(solution)/shard_map/ppermute | solution.py:206
  88.1 0.1 add_convert_fusion
  88.2 9.8 %all_to_all.36.in_ref = bf16[4,272,128]{2,1,0:T(8,128)(2,1)S(1)} all-to-all(bf16[4,272,128]{2,1,0:T(8,128)(2,1)S(1)} %add_convert_fusion), channel_id=1, replica_groups=mesh['y'=4,'zl'=8,'c'=2,'x'=4,'zh'=2] {'y'}, dimensions={0} | all-to-all | bytes 557056 | tf_op jit(solution)/shard_map/all_to_all | solution.py:202
  98.0 28.0 %all_to_all.37.in_ref = bf16[16,48,128]{2,1,0:T(8,128)(2,1)S(1)} all-to-all(bf16[16,48,128]{2,1,0:T(8,128)(2,1)S(1)} %bitcast.27), channel_id=1, replica_groups=mesh['y'=4,'zl'=8,'c'=2,'x'=4,'zh'=2] {'zl','zh'}, dimensions={0} | all-to-all | bytes 393216 | tf_op jit(solution)/shard_map/all_to_all | solution.py:202
  126.1 11.4 %all_to_all.38.in_ref = bf16[16,48,128]{2,1,0:T(8,128)(2,1)S(1)} all-to-all(bf16[16,48,128]{2,1,0:T(8,128)(2,1)S(1)} %shard_map.98), channel_id=1, replica_groups=mesh['y'=4,'zl'=8,'c'=2,'x'=4,'zh'=2] {'y','x'}, dimensions={0} | all-to-all | bytes 393216 | tf_op jit(solution)/shard_map/all_to_all | solution.py:202
  137.4 0.7 shard_map.99
  (14 shorter events, 0.1 us)
Async XLA Ops:
  0.6 9.9 %all-to-all-start = ((bf16[4,32,128]{2,1,0:T(8,128)(2,1)}), bf16[4,32,128]{2,1,0:T(8,128)(2,1)S(1)}, u32[]{:S(2)}, u32[]{:S(2)}) async-start(bf16[4,32,128]{2,1,0:T(8,128)(2,1)} %bitcast.30), calls=%async_computation | async-start | bytes 65536 | tf_op jit(solution)/shard_map/all_to_all | solution.py:202
  5.1 1.2 copy-start
  6.3 0.7 copy-start.1
  11.7 33.9 %copy-start.4 = (f32[32]{0:T(128)S(1)}, f32[32]{0:T(128)}, u32[]{:S(2)}) copy-start(f32[32]{0:T(128)} %param.10) | copy-start | bytes 388
  11.7 33.9 %copy-start.2 = (bf16[128,32]{0,1:T(8,128)(2,1)S(1)}, bf16[128,32]{0,1:T(8,128)(2,1)}, u32[]{:S(2)}) copy-start(bf16[128,32]{0,1:T(8,128)(2,1)} %param.11) | copy-start | bytes 24580
  11.7 33.9 %copy-start.3 = (bf16[128,32]{0,1:T(8,128)(2,1)S(1)}, bf16[128,32]{0,1:T(8,128)(2,1)}, u32[]{:S(2)}) copy-start(bf16[128,32]{0,1:T(8,128)(2,1)} %param.9) | copy-start | bytes 24580
  11.7 29.5 %collective-permute-start.1 = (bf16[2,8,128,128]{3,2,1,0:T(8,128)(2,1)}, bf16[2,8,128,128]{3,2,1,0:T(8,128)(2,1)S(1)}, u32[]{:S(2)}, u32[]{:S(2)}) collective-permute-start(bf16[2,8,128,128]{3,2,1,0:T(8,128)(2,1)} %get-tuple-element.29), channel_id=1, source_target_pairs={{0,4},{2,6},{4,0},{6,2},{1,5},{3,7},{5,1},{7,3},{8,12},{10,14},{12... | collective-permute-start | bytes 1572872 | tf_op jit(solution)/shard_map/ppermute | solution.py:235
  17.4 21.9 %all-to-all-start.1 = ((bf16[8,32,128]{2,1,0:T(8,128)(2,1)}), bf16[8,32,128]{2,1,0:T(8,128)(2,1)S(1)}, u32[]{:S(2)}, u32[]{:S(2)}) async-start(bf16[8,32,128]{2,1,0:T(8,128)(2,1)} %broadcast_in_dim.4), calls=%async_computation.1 | async-start | bytes 131072 | tf_op jit(solution)/shard_map/all_to_all | solution.py:202
  30.0 15.6 %collective-permute-start = (bf16[2,8,128,128]{3,2,1,0:T(8,128)(2,1)}, bf16[2,8,128,128]{3,2,1,0:T(8,128)(2,1)S(1)}, u32[]{:S(2)}, u32[]{:S(2)}) collective-permute-start(bf16[2,8,128,128]{3,2,1,0:T(8,128)(2,1)} %get-tuple-element.30), channel_id=1, source_target_pairs={{0,2},{2,4},{4,6},{6,0},{1,3},{3,5},{5,7},{7,1},{8,10},{10,12},{12... | collective-permute-start | bytes 1572872 | tf_op jit(solution)/shard_map/ppermute | solution.py:235
  32.5 13.2 %collective-permute-start.2 = (bf16[2,8,128,128]{3,2,1,0:T(8,128)(2,1)S(1)}, bf16[2,8,128,128]{3,2,1,0:T(8,128)(2,1)S(1)}, u32[]{:S(2)}, u32[]{:S(2)}) collective-permute-start(bf16[2,8,128,128]{3,2,1,0:T(8,128)(2,1)S(1)} %get-tuple-element.28), channel_id=1, source_target_pairs={{0,6},{2,0},{4,2},{6,4},{1,7},{3,1},{5,3},{7,5},{8,14},{10,8},{12,... | collective-permute-start | bytes 1572872 | tf_op jit(solution)/shard_map/ppermute | solution.py:235
  42.1 13.5 %all-to-all-start.2 = ((bf16[4,2,8,32,128]{4,3,2,1,0:T(8,128)(2,1)}), bf16[4,2,8,32,128]{4,3,2,1,0:T(8,128)(2,1)S(1)}, u32[]{:S(2)}, u32[]{:S(2)}) async-start(bf16[4,2,8,32,128]{4,3,2,1,0:T(8,128)(2,1)} %broadcast_in_dim.5), calls=%async_computation.2 | async-start | bytes 1048576 | tf_op jit(solution)/shard_map/all_to_all | solution.py:202
  64.8 18.7 %collective-permute-start.3 = (bf16[400,128]{1,0:T(8,128)(2,1)S(1)}, bf16[400,128]{1,0:T(8,128)(2,1)S(1)}, u32[]{:S(2)}, u32[]{:S(2)}) collective-permute-start(bf16[400,128]{1,0:T(8,128)(2,1)S(1)} %shard_map.95.sum_ref), channel_id=1, source_target_pairs={{0,1},{1,0},{2,3},{3,2},{4,5},{5,4},{6,7},{7,6},{8,9},{9,8},{10,11... | collective-permute-start | bytes 307208 | tf_op jit(solution)/shard_map/ppermute | solution.py:206
  84.7 3.4 %collective-permute-start.4 = (bf16[4,272,128]{2,1,0:T(8,128)(2,1)S(1)}, bf16[4,272,128]{2,1,0:T(8,128)(2,1)S(1)}, u32[]{:S(2)}, u32[]{:S(2)}) collective-permute-start(bf16[4,272,128]{2,1,0:T(8,128)(2,1)S(1)} %get-tuple-element.24), channel_id=1, source_target_pairs={{0,8},{8,0},{1,9},{9,1},{2,10},{10,2},{3,11},{11,3},{4,12},{12,4},... | collective-permute-start | bytes 835592 | tf_op jit(solution)/shard_map/ppermute | solution.py:206

commit v9 on v6

--- a/solution.py
+++ b/solution.py
@@ -68,13 +68,14 @@
         out_ref[x, tile + size :, :] = pack_other_ref[...]
 
 
-def backward_kernel(sum_ref, other_ref, packs_ref, pack_ref, a_ref, act_ref, own_ref, oth_ref):
+def backward_kernel(sum_ref, other_ref, packs_ref, pack_ref, a_ref, act_ref, out_ref):
+    my_c = lax.axis_index("c")
     x_n = packs_ref.shape[0]
     hidden = act_ref.shape[0]
     tile = a_ref.shape[-1]
     zl_n = a_ref.shape[1]
     size = pack_ref.shape[0]
-    y_n = own_ref.shape[0]
+    y_n = out_ref.shape[0]
     rows = tile // y_n
     agg = (sum_ref[...].astype(F32) + other_ref[...].astype(F32)).astype(BF16)
     starts = [(x, tile + z * size) for x in range(x_n) for z in range(2)]
@@ -109,15 +110,16 @@
         if share < 8:
             piece.insert(1, jnp.zeros((8 - share, tile), F32))
         piece = jnp.concatenate(piece, axis=0).astype(BF16)
-        own_ref[y, body:, :] = piece
-        oth_ref[y, body:, :] = piece
-    for core, out_ref in ((1, oth_ref), (0, own_ref)):
+        out_ref[y, 0, body:, :] = piece
+        out_ref[y, 1, body:, :] = piece
+    for core in range(2):
+        to = pl.ds(my_c if core == 0 else 1 - my_c, 1)
         for zl in range(0, zl_n, 2):
             pair = mm(back_t, jnp.concatenate([a_ref[core, zl], a_ref[core, zl + 1]], axis=1), 1, 0).astype(BF16)
             for y in range(y_n):
                 part = pair[y * rows : (y + 1) * rows]
-                out_ref[y, zl * rows : (zl + 1) * rows, :] = part[:, :tile]
-                out_ref[y, (zl + 1) * rows : (zl + 2) * rows, :] = part[:, tile:]
+                out_ref[y, to, zl * rows : (zl + 1) * rows, :] = part[None, :, :tile]
+                out_ref[y, to, (zl + 1) * rows : (zl + 2) * rows, :] = part[None, :, tile:]
 
 
 def plane_sum_kernel(in_ref, out_ref):
@@ -219,10 +221,10 @@
     while len(pieces) < 4:
         pieces.append(pieces[0])
     column = to_all(jnp.broadcast_to(mine[None], (zl_n, rows, feat)), "zl")
-    column = lax.all_gather(column, "c")
     column, pack = lax.optimization_barrier((column, pack))
     pack_other = swap(pack, "zh")
-    blocks = to_all(jnp.broadcast_to(column[None], (y_n,) + column.shape), "y")
+    blocks = to_all(jnp.broadcast_to(column[None], (y_n * c_n,) + column.shape), ("y", "c"))
+    blocks = blocks.reshape((y_n, c_n) + column.shape)
 
     size = pack.shape[0]
     a_mine, part = call(
@@ -237,18 +239,16 @@
     summed = jnp.sum(part[:, :tile].astype(F32), axis=0).astype(BF16)
     summed_other = swap(summed, "zh")
 
-    payload = shape(y_n, zl_n * rows + EXTRA, tile)
-    act_t, keep, give = call(
+    act_t, sent = call(
         backward_kernel,
-        (shape(hidden, tile), payload, payload),
+        (shape(hidden, tile), shape(y_n, c_n, zl_n * rows + EXTRA, tile)),
         summed,
         summed_other,
         part,
         pack,
         a_mine,
     )
-    both = (keep.astype(F32) + swap(give, "c").astype(F32)).astype(BF16)
-    across = to_all(both, "y")
+    across = to_all(sent.reshape(y_n * c_n, zl_n * rows + EXTRA, tile), ("y", "c"))
     up = call(plane_sum_kernel, shape(zl_n, zh_n, rows + EXTRA, feat), across).reshape(
         zl_n * zh_n, rows + EXTRA, feat
     )

time: 137 us -> 137 us (level)
  blocking collectives: 61 us -> 63.6 us
  starting transfers between devices: 50.3 us -> 48.4 us
  waiting for transfers between devices: 15.6 us -> 14.1 us
    all_to_all x4, blocking collectives: 59.1 us -> 63.6 us  [to_all(): return lax.all_to_all(v, axes, 0, 0, tiled=True)]
    all_gather x1 -> x0, blocking collectives: 1.9 us -> none  [on_device(): column = lax.all_gather(column, 'c')]
    ppermute x3 -> x2, starting transfers between devices: 18.4 us -> 16.5 us  [swap(): return lax.ppermute(v, axis, [(0, 1), (1, 0)])]
    ppermute x3 -> x2, waiting for transfers between devices: 14 us -> 12.6 us  [swap(): return lax.ppermute(v, axis, [(0, 1), (1, 0)])]
  transfers between devices with their start and end apart: 9 -> 8, of which waited for: 4 -> 3; matrix products, arithmetic and copies ran while one was open for 2% -> 2% of each run, Pallas kernels for 1% -> 1%
where the time goes in v9:
time: 137 us; the launch traced here: 136 us
  blocking collectives  63.6 us (46%)
  starting transfers between devices  48.4 us (35%)
  waiting for transfers between devices  14.1 us (10%)
  local copies, waits for them, and re-layouts  4.58 us (3%)
  Pallas kernels  3.84 us (3%)
    all_to_all x4, blocking collectives, to_all(): return lax.all_to_all(v, axes, 0, 0, tiled=True)  63.6 us
    all_to_all x3, starting transfers between devices, to_all(): return lax.all_to_all(v, axes, 0, 0, tiled=True)  20.6 us
    ppermute x2, starting transfers between devices, swap(): return lax.ppermute(v, axis, [(0, 1), (1, 0)])  16.5 us
    ppermute x2, waiting for transfers between devices, swap(): return lax.ppermute(v, axis, [(0, 1), (1, 0)])  12.6 us
    ppermute x3, starting transfers between devices, on_device(): lax.ppermute(dense[step], 'x', [(x, (x + step) % x_n) for x in range(x_n)])  11.4 us
    pallas_call x6, Pallas kernels, call(): pl.pallas_call(kernel, out_shape=out, in_specs=[SMEM] * smem + [VMEM] * (...  3.84 us
  transfers between devices with their start and end apart: 8, of which 3 were waited for; matrix products, arithmetic and copies ran while one was open for 2% of the time, Pallas kernels for 1%

profile of v9, /device:TPU:32, one launch (start us, length us, event | category | flops | bytes accessed | tf_op | source)
XLA Modules:
  0.0 136.1 jit_solution(17052769925243278007)
XLA Ops:
  0.6 4.5 %all-to-all-start = ((bf16[4,32,128]{2,1,0:T(8,128)(2,1)}), bf16[4,32,128]{2,1,0:T(8,128)(2,1)S(1)}, u32[]{:S(2)}, u32[]{:S(2)}) async-start(bf16[4,32,128]{2,1,0:T(8,128)(2,1)} %bitcast.32), calls=%async_computation | async-start | bytes 65536 | tf_op jit(solution)/shard_map/all_to_all | solution.py:185
  5.1 0.7 convert_bitcast_fusion.2
  5.9 0.0 copy-start
  5.9 1.2 copy-done
  7.1 0.7 copy-done.1
  7.7 1.3 shard_map.93
  9.1 1.5 %all-to-all-done = bf16[4,32,128]{2,1,0:T(8,128)(2,1)S(1)} async-done(((bf16[4,32,128]{2,1,0:T(8,128)(2,1)}), bf16[4,32,128]{2,1,0:T(8,128)(2,1)S(1)}, u32[]{:S(2)}, u32[]{:S(2)}) %all-to-all-start) | async-done | bytes 32800 | tf_op jit(solution)/shard_map/all_to_all | solution.py:185
  10.6 0.6 broadcast_in_dim.4
  11.2 12.6 %all-to-all-start.1 = ((bf16[8,32,128]{2,1,0:T(8,128)(2,1)}), bf16[8,32,128]{2,1,0:T(8,128)(2,1)S(1)}, u32[]{:S(2)}, u32[]{:S(2)}) async-start(bf16[8,32,128]{2,1,0:T(8,128)(2,1)} %broadcast_in_dim.4), calls=%async_computation.1 | async-start | bytes 131072 | tf_op jit(solution)/shard_map/all_to_all | solution.py:185
  23.8 1.1 slice_bitcast_fusion
  25.0 3.4 %collective-permute-start = (bf16[2,8,128,128]{3,2,1,0:T(8,128)(2,1)}, bf16[2,8,128,128]{3,2,1,0:T(8,128)(2,1)S(1)}, u32[]{:S(2)}, u32[]{:S(2)}) collective-permute-start(bf16[2,8,128,128]{3,2,1,0:T(8,128)(2,1)} %get-tuple-element.28), channel_id=1, source_target_pairs={{0,2},{2,4},{4,6},{6,0},{1,3},{3,5},{5,7},{7,1},{8,10},{10,12},{12... | collective-permute-start | bytes 1572872 | tf_op jit(solution)/shard_map/ppermute | solution.py:220
  28.4 4.6 %collective-permute-start.1 = (bf16[2,8,128,128]{3,2,1,0:T(8,128)(2,1)}, bf16[2,8,128,128]{3,2,1,0:T(8,128)(2,1)S(1)}, u32[]{:S(2)}, u32[]{:S(2)}) collective-permute-start(bf16[2,8,128,128]{3,2,1,0:T(8,128)(2,1)} %get-tuple-element.27), channel_id=1, source_target_pairs={{0,4},{2,6},{4,0},{6,2},{1,5},{3,7},{5,1},{7,3},{8,12},{10,14},{12... | collective-permute-start | bytes 1572872 | tf_op jit(solution)/shard_map/ppermute | solution.py:220
  33.0 3.3 %collective-permute-start.2 = (bf16[2,8,128,128]{3,2,1,0:T(8,128)(2,1)S(1)}, bf16[2,8,128,128]{3,2,1,0:T(8,128)(2,1)S(1)}, u32[]{:S(2)}, u32[]{:S(2)}) collective-permute-start(bf16[2,8,128,128]{3,2,1,0:T(8,128)(2,1)S(1)} %get-tuple-element.26), channel_id=1, source_target_pairs={{0,6},{2,0},{4,2},{6,4},{1,7},{3,1},{5,3},{7,5},{8,14},{10,8},{12,... | collective-permute-start | bytes 1572872 | tf_op jit(solution)/shard_map/ppermute | solution.py:220
  36.4 0.0 all-to-all-done.1
  36.4 0.9 broadcast_in_dim.5
  37.3 3.5 %all-to-all-start.2 = ((bf16[8,8,32,128]{3,2,1,0:T(8,128)(2,1)}), bf16[8,8,32,128]{3,2,1,0:T(8,128)(2,1)S(1)}, u32[]{:S(2)}, u32[]{:S(2)}) async-start(bf16[8,8,32,128]{3,2,1,0:T(8,128)(2,1)} %broadcast_in_dim.5), calls=%async_computation.2 | async-start | bytes 1048576 | tf_op jit(solution)/shard_map/all_to_all | solution.py:185
  40.8 8.2 %collective-permute-start.3 = (bf16[80,128]{1,0:T(8,128)(2,1)S(1)}, bf16[80,128]{1,0:T(8,128)(2,1)S(1)}, u32[]{:S(2)}, u32[]{:S(2)}) collective-permute-start(bf16[80,128]{1,0:T(8,128)(2,1)S(1)} %pad_maximum_fusion.pack_ref), channel_id=1, source_target_pairs={{0,1},{1,0},{2,3},{3,2},{4,5},{5,4},{6,7},{7,6},{8,9},{9,8},{10,11... | collective-permute-start | bytes 61448 | tf_op jit(solution)/shard_map/ppermute | solution.py:189
  49.1 6.2 %collective-permute-done.3.pack_other_ref = bf16[80,128]{1,0:T(8,128)(2,1)S(1)} collective-permute-done((bf16[80,128]{1,0:T(8,128)(2,1)S(1)}, bf16[80,128]{1,0:T(8,128)(2,1)S(1)}, u32[]{:S(2)}, u32[]{:S(2)}) %collective-permute-start.3) | collective-permute-done | bytes 20512 | tf_op jit(solution)/shard_map/ppermute | solution.py:189
  55.2 0.0 collective-permute-done.d1_ref
  55.2 0.0 collective-permute-done.1.d2_ref
  55.2 0.0 collective-permute-done.2.d3_ref
  55.3 0.0 all-to-all-done.2
  55.3 0.4 shard_map.94
  55.7 9.4 %all_to_all.35.packs_ref = bf16[4,288,128]{2,1,0:T(8,128)(2,1)S(1)} all-to-all(bf16[4,288,128]{2,1,0:T(8,128)(2,1)S(1)} %get-tuple-element.19), channel_id=1, replica_groups=mesh['y'=4,'zl'=8,'c'=2,'x'=4,'zh'=2] {'x'}, dimensions={0} | all-to-all | bytes 589824 | tf_op jit(solution)/shard_map/all_to_all | solution.py:185
  65.1 8.2 %collective-permute-start.4 = (bf16[128,128]{1,0:T(8,128)(2,1)S(1)}, bf16[128,128]{1,0:T(8,128)(2,1)S(1)}, u32[]{:S(2)}, u32[]{:S(2)}) collective-permute-start(bf16[128,128]{1,0:T(8,128)(2,1)S(1)} %slice_reduce_fusion.sum_ref), channel_id=1, source_target_pairs={{0,1},{1,0},{2,3},{3,2},{4,5},{5,4},{6,7},{7,6},{8,9},{9,8},{10,11... | collective-permute-start | bytes 98312 | tf_op jit(solution)/shard_map/ppermute | solution.py:189
  73.3 6.4 %collective-permute-done.4.other_ref = bf16[128,128]{1,0:T(8,128)(2,1)S(1)} collective-permute-done((bf16[128,128]{1,0:T(8,128)(2,1)S(1)}, bf16[128,128]{1,0:T(8,128)(2,1)S(1)}, u32[]{:S(2)}, u32[]{:S(2)}) %collective-permute-start.4) | collective-permute-done | bytes 32800 | tf_op jit(solution)/shard_map/ppermute | solution.py:189
  79.7 1.3 shard_map.95
  81.0 15.0 %all_to_all.36.in_ref = bf16[8,272,128]{2,1,0:T(8,128)(2,1)S(1)} all-to-all(bf16[8,272,128]{2,1,0:T(8,128)(2,1)S(1)} %bitcast.30), channel_id=1, replica_groups=mesh['y'=4,'zl'=8,'c'=2,'x'=4,'zh'=2] {'y','c'}, dimensions={0} | all-to-all | bytes 1114112 | tf_op jit(solution)/shard_map/all_to_all | solution.py:185
  96.0 0.1 shard_map.96
  96.1 27.9 %all_to_all.37.in_ref = bf16[16,48,128]{2,1,0:T(8,128)(2,1)S(1)} all-to-all(bf16[16,48,128]{2,1,0:T(8,128)(2,1)S(1)} %bitcast.29), channel_id=1, replica_groups=mesh['y'=4,'zl'=8,'c'=2,'x'=4,'zh'=2] {'zl','zh'}, dimensions={0} | all-to-all | bytes 393216 | tf_op jit(solution)/shard_map/all_to_all | solution.py:185
  124.1 11.3 %all_to_all.38.in_ref = bf16[16,48,128]{2,1,0:T(8,128)(2,1)S(1)} all-to-all(bf16[16,48,128]{2,1,0:T(8,128)(2,1)S(1)} %shard_map.97), channel_id=1, replica_groups=mesh['y'=4,'zl'=8,'c'=2,'x'=4,'zh'=2] {'y','x'}, dimensions={0} | all-to-all | bytes 393216 | tf_op jit(solution)/shard_map/all_to_all | solution.py:185
  135.3 0.7 shard_map.98
  (10 shorter events, 0.1 us)
Async XLA Ops:
  0.6 9.9 %all-to-all-start = ((bf16[4,32,128]{2,1,0:T(8,128)(2,1)}), bf16[4,32,128]{2,1,0:T(8,128)(2,1)S(1)}, u32[]{:S(2)}, u32[]{:S(2)}) async-start(bf16[4,32,128]{2,1,0:T(8,128)(2,1)} %bitcast.32), calls=%async_computation | async-start | bytes 65536 | tf_op jit(solution)/shard_map/all_to_all | solution.py:185
  5.9 1.2 copy-start
  7.1 0.7 copy-start.1
  11.2 25.2 %all-to-all-start.1 = ((bf16[8,32,128]{2,1,0:T(8,128)(2,1)}), bf16[8,32,128]{2,1,0:T(8,128)(2,1)S(1)}, u32[]{:S(2)}, u32[]{:S(2)}) async-start(bf16[8,32,128]{2,1,0:T(8,128)(2,1)} %broadcast_in_dim.4), calls=%async_computation.1 | async-start | bytes 131072 | tf_op jit(solution)/shard_map/all_to_all | solution.py:185
  23.8 12.5 %copy-start.2 = (bf16[128,32]{0,1:T(8,128)(2,1)S(1)}, bf16[128,32]{0,1:T(8,128)(2,1)}, u32[]{:S(2)}) copy-start(bf16[128,32]{0,1:T(8,128)(2,1)} %param.11) | copy-start | bytes 24580
  23.8 12.6 %copy-start.3 = (bf16[128,32]{0,1:T(8,128)(2,1)S(1)}, bf16[128,32]{0,1:T(8,128)(2,1)}, u32[]{:S(2)}) copy-start(bf16[128,32]{0,1:T(8,128)(2,1)} %param.9) | copy-start | bytes 24580
  25.0 30.3 %collective-permute-start = (bf16[2,8,128,128]{3,2,1,0:T(8,128)(2,1)}, bf16[2,8,128,128]{3,2,1,0:T(8,128)(2,1)S(1)}, u32[]{:S(2)}, u32[]{:S(2)}) collective-permute-start(bf16[2,8,128,128]{3,2,1,0:T(8,128)(2,1)} %get-tuple-element.28), channel_id=1, source_target_pairs={{0,2},{2,4},{4,6},{6,0},{1,3},{3,5},{5,7},{7,1},{8,10},{10,12},{12... | collective-permute-start | bytes 1572872 | tf_op jit(solution)/shard_map/ppermute | solution.py:220
  28.4 26.9 %collective-permute-start.1 = (bf16[2,8,128,128]{3,2,1,0:T(8,128)(2,1)}, bf16[2,8,128,128]{3,2,1,0:T(8,128)(2,1)S(1)}, u32[]{:S(2)}, u32[]{:S(2)}) collective-permute-start(bf16[2,8,128,128]{3,2,1,0:T(8,128)(2,1)} %get-tuple-element.27), channel_id=1, source_target_pairs={{0,4},{2,6},{4,0},{6,2},{1,5},{3,7},{5,1},{7,3},{8,12},{10,14},{12... | collective-permute-start | bytes 1572872 | tf_op jit(solution)/shard_map/ppermute | solution.py:220
  33.0 22.2 %collective-permute-start.2 = (bf16[2,8,128,128]{3,2,1,0:T(8,128)(2,1)S(1)}, bf16[2,8,128,128]{3,2,1,0:T(8,128)(2,1)S(1)}, u32[]{:S(2)}, u32[]{:S(2)}) collective-permute-start(bf16[2,8,128,128]{3,2,1,0:T(8,128)(2,1)S(1)} %get-tuple-element.26), channel_id=1, source_target_pairs={{0,6},{2,0},{4,2},{6,4},{1,7},{3,1},{5,3},{7,5},{8,14},{10,8},{12,... | collective-permute-start | bytes 1572872 | tf_op jit(solution)/shard_map/ppermute | solution.py:220
  37.3 17.9 %all-to-all-start.2 = ((bf16[8,8,32,128]{3,2,1,0:T(8,128)(2,1)}), bf16[8,8,32,128]{3,2,1,0:T(8,128)(2,1)S(1)}, u32[]{:S(2)}, u32[]{:S(2)}) async-start(bf16[8,8,32,128]{3,2,1,0:T(8,128)(2,1)} %broadcast_in_dim.5), calls=%async_computation.2 | async-start | bytes 1048576 | tf_op jit(solution)/shard_map/all_to_all | solution.py:185
  40.8 14.4 %collective-permute-start.3 = (bf16[80,128]{1,0:T(8,128)(2,1)S(1)}, bf16[80,128]{1,0:T(8,128)(2,1)S(1)}, u32[]{:S(2)}, u32[]{:S(2)}) collective-permute-start(bf16[80,128]{1,0:T(8,128)(2,1)S(1)} %pad_maximum_fusion.pack_ref), channel_id=1, source_target_pairs={{0,1},{1,0},{2,3},{3,2},{4,5},{5,4},{6,7},{7,6},{8,9},{9,8},{10,11... | collective-permute-start | bytes 61448 | tf_op jit(solution)/shard_map/ppermute | solution.py:189
  65.1 14.6 %collective-permute-start.4 = (bf16[128,128]{1,0:T(8,128)(2,1)S(1)}, bf16[128,128]{1,0:T(8,128)(2,1)S(1)}, u32[]{:S(2)}, u32[]{:S(2)}) collective-permute-start(bf16[128,128]{1,0:T(8,128)(2,1)S(1)} %slice_reduce_fusion.sum_ref), channel_id=1, source_target_pairs={{0,1},{1,0},{2,3},{3,2},{4,5},{5,4},{6,7},{7,6},{8,9},{9,8},{10,11... | collective-permute-start | bytes 98312 | tf_op jit(solution)/shard_map/ppermute | solution.py:189

commit v10 on v9

--- a/solution.py
+++ b/solution.py
@@ -31,7 +31,6 @@
 
 def dense_kernel(zl_n, src_ref, tiles_ref, out_ref):
     my_c, my_x = lax.axis_index("c"), lax.axis_index("x")
-    x_n = out_ref.shape[0]
     out_ref[...] = jnp.zeros_like(out_ref)
     acc = None
     for k in range(tiles_ref.shape[0]):
@@ -41,23 +40,27 @@
             piece = piece + jnp.where(src == src_ref[k - 1], acc, 0.0)
         acc = piece
         y, zl, c = src // (2 * zl_n), (src // 2) % zl_n, src % 2
-        at = (pl.ds((y + x_n - my_x) % x_n, 1), pl.ds(jnp.where(c == my_c, 0, 1), 1), pl.ds(zl, 1))
+        apart = y ^ my_x
+        slot = jnp.where(apart == 0, 0, jnp.where(apart == 3, 1, apart + 1))
+        at = (pl.ds(slot, 1), pl.ds(jnp.where(c == my_c, 0, 1), 1), pl.ds(zl, 1))
         out_ref[at] = acc.astype(BF16)[None, None, None]
 
 
-def forward_kernel(d0_ref, d1_ref, d2_ref, d3_ref, feat_ref, pack_ref, pack_other_ref, a_ref, out_ref):
+def relay_kernel(mine_ref, other_ref, out_ref):
+    out_ref[...] = (mine_ref[1].astype(F32) + other_ref[1].astype(F32)).astype(BF16)
+
+
+def forward_kernel(d0_ref, d1_ref, d2_ref, feat_ref, pack_ref, pack_other_ref, a_ref, out_ref):
     my_c = lax.axis_index("c")
-    tile = d0_ref.shape[-1]
+    tile = a_ref.shape[-1]
     feat = feat_ref.shape[-1]
     size = pack_ref.shape[0]
-    zl_n = d0_ref.shape[1]
+    zl_n = a_ref.shape[1]
     acc = jnp.zeros((tile, feat), F32)
     for core in range(2):
         for zl in range(zl_n):
-            total = d0_ref[core, zl].astype(F32)
-            for ref in (d1_ref, d2_ref, d3_ref)[: out_ref.shape[0] - 1]:
-                total = total + ref[core, zl].astype(F32)
-            total = total.astype(BF16)
+            total = d0_ref[0, core, zl].astype(F32) + d1_ref[0, core, zl].astype(F32)
+            total = (total + d2_ref[core, zl].astype(F32)).astype(BF16)
             a_ref[core, zl] = total
             at = (slice(None), pl.ds(my_c if core == 0 else 1 - my_c, 1), slice(zl, zl + 1))
             acc = acc + mm(total, feat_ref[at].reshape(tile, feat), 1, 0)
@@ -214,15 +217,14 @@
 
     quarters = to_all(features.reshape(y_n, rows, feat), "y")
     mine = lax.dynamic_index_in_dim(quarters, my_x, 0, keepdims=False)
-    mine, dense = lax.optimization_barrier((mine, dense))
-    pieces = [dense[0]]
-    for step in range(1, x_n):
-        pieces.append(lax.ppermute(dense[step], "x", [(x, (x + step) % x_n) for x in range(x_n)]))
-    while len(pieces) < 4:
-        pieces.append(pieces[0])
+    mine, dense, pack = lax.optimization_barrier((mine, dense, pack))
+    near = lax.ppermute(dense[2:], "x", [(x, x ^ 1) for x in range(x_n)])
+    pack_other = swap(pack, "zh")
     column = to_all(jnp.broadcast_to(mine[None], (zl_n, rows, feat)), "zl")
-    column, pack = lax.optimization_barrier((column, pack))
-    pack_other = swap(pack, "zh")
+    near, pack_other = lax.optimization_barrier((near, pack_other))
+    relay = call(relay_kernel, shape(c_n, zl_n, tile, tile), dense[:2], near)
+    far = lax.ppermute(relay, "x", [(x, x_n - 1 - x) for x in range(x_n)])
+    column, relay = lax.optimization_barrier((column, relay))
     blocks = to_all(jnp.broadcast_to(column[None], (y_n * c_n,) + column.shape), ("y", "c"))
     blocks = blocks.reshape((y_n, c_n) + column.shape)
 
@@ -230,7 +232,9 @@
     a_mine, part = call(
         forward_kernel,
         (shape(c_n, zl_n, tile, tile), shape(x_n, tile + 2 * size, feat)),
-        *pieces,
+        dense[:2],
+        near,
+        far,
         blocks,
         pack,
         pack_other,

time: 137 us -> 142 us (1.036)
  blocking collectives: 63.6 us -> 77 us
  starting transfers between devices: 48.4 us -> 43.6 us
  waiting for transfers between devices: 14.1 us -> 10.7 us
    all_to_all x4 -> x5, blocking collectives: 63.6 us -> 77 us  [to_all(): return lax.all_to_all(v, axes, 0, 0, tiled=True)]
    ppermute x3 -> x2, starting transfers between devices: 11.4 us -> 7.39 us  [the longest x1 4 us: on_device(): far = lax.ppermute(relay, 'x', [(x, x_n - 1 - x) for x in range(x_n)])]
    all_to_all x3 -> x2, starting transfers between devices: 20.6 us -> 17.1 us  [to_all(): return lax.all_to_all(v, axes, 0, 0, tiled=True)]
    ppermute x2, waiting for transfers between devices: 12.6 us -> 9.88 us  [swap(): return lax.ppermute(v, axis, [(0, 1), (1, 0)])]
    ppermute x2, starting transfers between devices: 16.5 us -> 19.1 us  [swap(): return lax.ppermute(v, axis, [(0, 1), (1, 0)])]
    pallas_call x6 -> x7, Pallas kernels: 3.84 us -> 3.88 us  [call(): pl.pallas_call(kernel, out_shape=out, in_specs=[SMEM] * smem + [VMEM] * (...]
  transfers between devices with their start and end apart: 8 -> 6, of which waited for: 3 -> 3; matrix products, arithmetic and copies ran while one was open for 2% -> 2% of each run, Pallas kernels for 1% -> 1%
where the time goes in v10:
time: 142 us; the launch traced here: 141 us
  blocking collectives  77 us (54%)
  starting transfers between devices  43.6 us (31%)
  waiting for transfers between devices  10.7 us (8%)
  Pallas kernels  3.88 us (3%)
  local copies, waits for them, and re-layouts  3.77 us (3%)
  other arithmetic  1.49 us (1%)
    all_to_all x5, blocking collectives, to_all(): return lax.all_to_all(v, axes, 0, 0, tiled=True)  77 us
    ppermute x2, starting transfers between devices, swap(): return lax.ppermute(v, axis, [(0, 1), (1, 0)])  19.1 us
    all_to_all x2, starting transfers between devices, to_all(): return lax.all_to_all(v, axes, 0, 0, tiled=True)  17.1 us
    ppermute x2, waiting for transfers between devices, swap(): return lax.ppermute(v, axis, [(0, 1), (1, 0)])  9.88 us
    ppermute x1, starting transfers between devices, on_device(): far = lax.ppermute(relay, 'x', [(x, x_n - 1 - x) for x in range(x_n)])  4 us
    pallas_call x7, Pallas kernels, call(): pl.pallas_call(kernel, out_shape=out, in_specs=[SMEM] * smem + [VMEM] * (...  3.88 us
    ppermute x1, starting transfers between devices, on_device(): near = lax.ppermute(dense[2:], 'x', [(x, x ^ 1) for x in range(x_n)])  3.39 us
  transfers between devices with their start and end apart: 6, of which 3 were waited for; matrix products, arithmetic and copies ran while one was open for 2% of the time, Pallas kernels for 1%

profile of v10, /device:TPU:32, one launch (start us, length us, event | category | flops | bytes accessed | tf_op | source)
XLA Modules:
  0.0 141.1 jit_solution(5380970273269727763)
XLA Ops:
  0.6 4.5 %all-to-all-start = ((bf16[4,32,128]{2,1,0:T(8,128)(2,1)}), bf16[4,32,128]{2,1,0:T(8,128)(2,1)S(1)}, u32[]{:S(2)}, u32[]{:S(2)}) async-start(bf16[4,32,128]{2,1,0:T(8,128)(2,1)} %bitcast.24), calls=%async_computation | async-start | bytes 65536 | tf_op jit(solution)/shard_map/all_to_all | solution.py:188
  5.1 0.7 convert_bitcast_fusion.2
  5.9 0.7 pad_maximum_fusion.pack_ref
  6.6 0.0 copy-start
  6.6 1.2 copy-done
  7.8 0.0 copy-start.1
  7.8 0.7 copy-done.1
  8.5 1.3 shard_map.93
  9.7 0.8 all-to-all-done
  10.6 1.2 fusion.9
  11.7 3.4 %collective-permute-start = (bf16[2,2,8,128,128]{4,3,2,1,0:T(8,128)(2,1)}, bf16[2,2,8,128,128]{4,3,2,1,0:T(8,128)(2,1)S(1)}, u32[]{:S(2)}, u32[]{:S(2)}) collective-permute-start(bf16[2,2,8,128,128]{4,3,2,1,0:T(8,128)(2,1)} %get-tuple-element.30), channel_id=1, source_target_pairs={{0,2},{2,0},{4,6},{6,4},{1,3},{3,1},{5,7},{7,5},{8,10},{10,8},{12,... | collective-permute-start | bytes 3145736 | tf_op jit(solution)/shard_map/ppermute | solution.py:221
  15.1 0.6 broadcast_in_dim.4
  15.8 12.6 %all-to-all-start.1 = ((bf16[8,32,128]{2,1,0:T(8,128)(2,1)}), bf16[8,32,128]{2,1,0:T(8,128)(2,1)S(1)}, u32[]{:S(2)}, u32[]{:S(2)}) async-start(bf16[8,32,128]{2,1,0:T(8,128)(2,1)} %broadcast_in_dim.4), calls=%async_computation.1 | async-start | bytes 131072 | tf_op jit(solution)/shard_map/all_to_all | solution.py:188
  28.4 8.2 %collective-permute-start.1 = (bf16[80,128]{1,0:T(8,128)(2,1)S(1)}, bf16[80,128]{1,0:T(8,128)(2,1)S(1)}, u32[]{:S(2)}, u32[]{:S(2)}) collective-permute-start(bf16[80,128]{1,0:T(8,128)(2,1)S(1)} %pad_maximum_fusion.pack_ref), channel_id=1, source_target_pairs={{0,1},{1,0},{2,3},{3,2},{4,5},{5,4},{6,7},{7,6},{8,9},{9,8},{10,11... | collective-permute-start | bytes 61448 | tf_op jit(solution)/shard_map/ppermute | solution.py:192
  36.6 6.2 %collective-permute-done.1.pack_other_ref = bf16[80,128]{1,0:T(8,128)(2,1)S(1)} collective-permute-done((bf16[80,128]{1,0:T(8,128)(2,1)S(1)}, bf16[80,128]{1,0:T(8,128)(2,1)S(1)}, u32[]{:S(2)}, u32[]{:S(2)}) %collective-permute-start.1) | collective-permute-done | bytes 20512 | tf_op jit(solution)/shard_map/ppermute | solution.py:192
  42.8 0.0 collective-permute-done.other_ref.d1_ref
  42.8 0.1 shard_map.94
  42.9 4.0 %collective-permute-start.2 = (bf16[2,8,128,128]{3,2,1,0:T(8,128)(2,1)S(1)}, bf16[2,8,128,128]{3,2,1,0:T(8,128)(2,1)S(1)}, u32[]{:S(2)}, u32[]{:S(2)}) collective-permute-start(bf16[2,8,128,128]{3,2,1,0:T(8,128)(2,1)S(1)} %shard_map.94), channel_id=1, source_target_pairs={{0,6},{2,4},{4,2},{6,0},{1,7},{3,5},{5,3},{7,1},{8,14},{10,12},{12... | collective-permute-start | bytes 1572872 | tf_op jit(solution)/shard_map/ppermute | solution.py:226
  46.9 0.0 all-to-all-done.1
  46.9 0.1 broadcast_in_dim.5
  47.0 14.2 %all_to_all.35 = bf16[8,8,32,128]{3,2,1,0:T(8,128)(2,1)S(1)} all-to-all(bf16[8,8,32,128]{3,2,1,0:T(8,128)(2,1)S(1)} %broadcast_in_dim.5), channel_id=1, replica_groups=mesh['y'=4,'zl'=8,'c'=2,'x'=4,'zh'=2] {'y','c'}, dimensions={0} | all-to-all | bytes 1048576 | tf_op jit(solution)/shard_map/all_to_all | solution.py:188
  61.2 0.0 collective-permute-done.2.d2_ref
  61.2 0.4 shard_map.95
  61.6 9.3 %all_to_all.36.packs_ref = bf16[4,288,128]{2,1,0:T(8,128)(2,1)S(1)} all-to-all(bf16[4,288,128]{2,1,0:T(8,128)(2,1)S(1)} %get-tuple-element.23), channel_id=1, replica_groups=mesh['y'=4,'zl'=8,'c'=2,'x'=4,'zh'=2] {'x'}, dimensions={0} | all-to-all | bytes 589824 | tf_op jit(solution)/shard_map/all_to_all | solution.py:188
  70.9 10.9 %collective-permute-start.3 = (bf16[128,128]{1,0:T(8,128)(2,1)S(1)}, bf16[128,128]{1,0:T(8,128)(2,1)S(1)}, u32[]{:S(2)}, u32[]{:S(2)}) collective-permute-start(bf16[128,128]{1,0:T(8,128)(2,1)S(1)} %slice_reduce_fusion.sum_ref), channel_id=1, source_target_pairs={{0,1},{1,0},{2,3},{3,2},{4,5},{5,4},{6,7},{7,6},{8,9},{9,8},{10,11... | collective-permute-start | bytes 98312 | tf_op jit(solution)/shard_map/ppermute | solution.py:192
  81.8 3.7 %collective-permute-done.3.other_ref = bf16[128,128]{1,0:T(8,128)(2,1)S(1)} collective-permute-done((bf16[128,128]{1,0:T(8,128)(2,1)S(1)}, bf16[128,128]{1,0:T(8,128)(2,1)S(1)}, u32[]{:S(2)}, u32[]{:S(2)}) %collective-permute-start.3) | collective-permute-done | bytes 32800 | tf_op jit(solution)/shard_map/ppermute | solution.py:192
  85.5 1.3 shard_map.96
  86.8 13.1 %all_to_all.37.in_ref = bf16[8,272,128]{2,1,0:T(8,128)(2,1)S(1)} all-to-all(bf16[8,272,128]{2,1,0:T(8,128)(2,1)S(1)} %bitcast.22), channel_id=1, replica_groups=mesh['y'=4,'zl'=8,'c'=2,'x'=4,'zh'=2] {'y','c'}, dimensions={0} | all-to-all | bytes 1114112 | tf_op jit(solution)/shard_map/all_to_all | solution.py:188
  99.9 0.1 shard_map.97
  100.0 29.1 %all_to_all.38.in_ref = bf16[16,48,128]{2,1,0:T(8,128)(2,1)S(1)} all-to-all(bf16[16,48,128]{2,1,0:T(8,128)(2,1)S(1)} %bitcast.21), channel_id=1, replica_groups=mesh['y'=4,'zl'=8,'c'=2,'x'=4,'zh'=2] {'zl','zh'}, dimensions={0} | all-to-all | bytes 393216 | tf_op jit(solution)/shard_map/all_to_all | solution.py:188
  129.1 11.3 %all_to_all.39.in_ref = bf16[16,48,128]{2,1,0:T(8,128)(2,1)S(1)} all-to-all(bf16[16,48,128]{2,1,0:T(8,128)(2,1)S(1)} %shard_map.98), channel_id=1, replica_groups=mesh['y'=4,'zl'=8,'c'=2,'x'=4,'zh'=2] {'y','x'}, dimensions={0} | all-to-all | bytes 393216 | tf_op jit(solution)/shard_map/all_to_all | solution.py:188
  140.4 0.7 shard_map.99
  (4 shorter events, 0.1 us)
Async XLA Ops:
  0.6 9.9 %all-to-all-start = ((bf16[4,32,128]{2,1,0:T(8,128)(2,1)}), bf16[4,32,128]{2,1,0:T(8,128)(2,1)S(1)}, u32[]{:S(2)}, u32[]{:S(2)}) async-start(bf16[4,32,128]{2,1,0:T(8,128)(2,1)} %bitcast.24), calls=%async_computation | async-start | bytes 65536 | tf_op jit(solution)/shard_map/all_to_all | solution.py:188
  6.6 1.2 copy-start
  7.8 0.7 copy-start.1
  11.7 31.0 %collective-permute-start = (bf16[2,2,8,128,128]{4,3,2,1,0:T(8,128)(2,1)}, bf16[2,2,8,128,128]{4,3,2,1,0:T(8,128)(2,1)S(1)}, u32[]{:S(2)}, u32[]{:S(2)}) collective-permute-start(bf16[2,2,8,128,128]{4,3,2,1,0:T(8,128)(2,1)} %get-tuple-element.30), channel_id=1, source_target_pairs={{0,2},{2,0},{4,6},{6,4},{1,3},{3,1},{5,7},{7,5},{8,10},{10,8},{12,... | collective-permute-start | bytes 3145736 | tf_op jit(solution)/shard_map/ppermute | solution.py:221
  15.8 31.2 %all-to-all-start.1 = ((bf16[8,32,128]{2,1,0:T(8,128)(2,1)}), bf16[8,32,128]{2,1,0:T(8,128)(2,1)S(1)}, u32[]{:S(2)}, u32[]{:S(2)}) async-start(bf16[8,32,128]{2,1,0:T(8,128)(2,1)} %broadcast_in_dim.4), calls=%async_computation.1 | async-start | bytes 131072 | tf_op jit(solution)/shard_map/all_to_all | solution.py:188
  28.4 14.4 %collective-permute-start.1 = (bf16[80,128]{1,0:T(8,128)(2,1)S(1)}, bf16[80,128]{1,0:T(8,128)(2,1)S(1)}, u32[]{:S(2)}, u32[]{:S(2)}) collective-permute-start(bf16[80,128]{1,0:T(8,128)(2,1)S(1)} %pad_maximum_fusion.pack_ref), channel_id=1, source_target_pairs={{0,1},{1,0},{2,3},{3,2},{4,5},{5,4},{6,7},{7,6},{8,9},{9,8},{10,11... | collective-permute-start | bytes 61448 | tf_op jit(solution)/shard_map/ppermute | solution.py:192
  42.9 18.3 %collective-permute-start.2 = (bf16[2,8,128,128]{3,2,1,0:T(8,128)(2,1)S(1)}, bf16[2,8,128,128]{3,2,1,0:T(8,128)(2,1)S(1)}, u32[]{:S(2)}, u32[]{:S(2)}) collective-permute-start(bf16[2,8,128,128]{3,2,1,0:T(8,128)(2,1)S(1)} %shard_map.94), channel_id=1, source_target_pairs={{0,6},{2,4},{4,2},{6,0},{1,7},{3,5},{5,3},{7,1},{8,14},{10,12},{12... | collective-permute-start | bytes 1572872 | tf_op jit(solution)/shard_map/ppermute | solution.py:226
  70.9 14.6 %collective-permute-start.3 = (bf16[128,128]{1,0:T(8,128)(2,1)S(1)}, bf16[128,128]{1,0:T(8,128)(2,1)S(1)}, u32[]{:S(2)}, u32[]{:S(2)}) collective-permute-start(bf16[128,128]{1,0:T(8,128)(2,1)S(1)} %slice_reduce_fusion.sum_ref), channel_id=1, source_target_pairs={{0,1},{1,0},{2,3},{3,2},{4,5},{5,4},{6,7},{7,6},{8,9},{9,8},{10,11... | collective-permute-start | bytes 98312 | tf_op jit(solution)/shard_map/ppermute | solution.py:192

commit v11 on v9

--- a/solution.py
+++ b/solution.py
@@ -29,7 +29,13 @@
     return 0.5 * (1.0 + t) + 0.5 * v * (1.0 - t * t) * du
 
 
-def dense_kernel(zl_n, src_ref, tiles_ref, out_ref):
+def dense_kernel(zl_n, src_ref, tiles_ref, bias_ref, out_ref, terms_ref):
+    bias = bias_ref[...]
+    high = bias.astype(BF16).astype(F32)
+    middle = (bias - high).astype(BF16).astype(F32)
+    rows = jnp.concatenate([high, middle, bias - high - middle, jnp.zeros((13, bias.shape[1]), F32)], axis=0)
+    fill = jnp.zeros((16, terms_ref.shape[1] - bias.shape[1]), F32)
+    terms_ref[...] = jnp.concatenate([rows, fill], axis=1).astype(BF16)
     my_c, my_x = lax.axis_index("c"), lax.axis_index("x")
     x_n = out_ref.shape[0]
     out_ref[...] = jnp.zeros_like(out_ref)
@@ -199,18 +205,15 @@
     sources = tile_block.reshape(-1)
     my_x = lax.axis_index("x")
 
-    b_hi = bias.astype(BF16)
-    b_mid = (bias - b_hi.astype(F32)).astype(BF16)
-    b_lo = (bias - b_hi.astype(F32) - b_mid.astype(F32)).astype(BF16)
-    terms = jnp.pad(jnp.stack([b_hi, b_mid, b_lo]), ((0, 13), (0, feat - hidden)))
-    pack = jnp.concatenate([weight.T, cotangent.T, terms], axis=0)
-    dense = call(
+    dense, terms = call(
         functools.partial(dense_kernel, zl_n),
-        shape(x_n, c_n, zl_n, tile, tile),
+        (shape(x_n, c_n, zl_n, tile, tile), shape(16, feat)),
         sources,
         tiles,
+        bias[None],
         smem=1,
     )
+    pack = jnp.concatenate([weight.T, cotangent.T, terms], axis=0)
 
     quarters = to_all(features.reshape(y_n, rows, feat), "y")
     mine = lax.dynamic_index_in_dim(quarters, my_x, 0, keepdims=False)

time: 137 us -> 137 us (level)
  waiting for transfers between devices: 14.1 us -> 16.3 us
    ppermute x3, waiting for transfers between devices: 0.01 us -> 1.85 us  [on_device(): lax.ppermute(dense[step], 'x', [(x, (x + step) % x_n) for x in range(x_n)])]
  transfers between devices with their start and end apart: 8 -> 8, of which waited for: 3 -> 4; matrix products, arithmetic and copies ran while one was open for 2% -> 2% of each run, Pallas kernels for 1% -> 1%
where the time goes in v11:
time: 137 us
  blocking collectives  63.3 us (46%)
  starting transfers between devices  47.2 us (34%)
  waiting for transfers between devices  16.3 us (12%)
  local copies, waits for them, and re-layouts  5.24 us (4%)
  Pallas kernels  3.84 us (3%)
    all_to_all x4, blocking collectives, to_all(): return lax.all_to_all(v, axes, 0, 0, tiled=True)  63.3 us
    all_to_all x3, starting transfers between devices, to_all(): return lax.all_to_all(v, axes, 0, 0, tiled=True)  20.6 us
    ppermute x2, starting transfers between devices, swap(): return lax.ppermute(v, axis, [(0, 1), (1, 0)])  16.5 us
    ppermute x2, waiting for transfers between devices, swap(): return lax.ppermute(v, axis, [(0, 1), (1, 0)])  12.8 us
    ppermute x3, starting transfers between devices, on_device(): lax.ppermute(dense[step], 'x', [(x, (x + step) % x_n) for x in range(x_n)])  10.2 us
    pallas_call x6, Pallas kernels, call(): pl.pallas_call(kernel, out_shape=out, in_specs=[SMEM] * smem + [VMEM] * (...  3.84 us
  transfers between devices with their start and end apart: 8, of which 4 were waited for; matrix products, arithmetic and copies ran while one was open for 2% of the time, Pallas kernels for 1%

profile of v11, /device:TPU:32, one launch (start us, length us, event | category | flops | bytes accessed | tf_op | source)
XLA Modules:
  0.0 136.6 jit_solution(7319036594679175614)
XLA Ops:
  0.6 4.5 %all-to-all-start = ((bf16[4,32,128]{2,1,0:T(8,128)(2,1)}), bf16[4,32,128]{2,1,0:T(8,128)(2,1)S(1)}, u32[]{:S(2)}, u32[]{:S(2)}) async-start(bf16[4,32,128]{2,1,0:T(8,128)(2,1)} %bitcast.28), calls=%async_computation | async-start | bytes 65536 | tf_op jit(solution)/shard_map/all_to_all | solution.py:191
  5.1 1.2 copy-done
  6.3 0.7 copy-done.1
  7.0 0.7 copy-done.2
  7.6 1.3 shard_map.93
  9.0 1.6 %all-to-all-done = bf16[4,32,128]{2,1,0:T(8,128)(2,1)S(1)} async-done(((bf16[4,32,128]{2,1,0:T(8,128)(2,1)}), bf16[4,32,128]{2,1,0:T(8,128)(2,1)S(1)}, u32[]{:S(2)}, u32[]{:S(2)}) %all-to-all-start) | async-done | bytes 32800 | tf_op jit(solution)/shard_map/all_to_all | solution.py:191
  10.6 0.6 broadcast_in_dim.7
  11.2 12.6 %all-to-all-start.1 = ((bf16[8,32,128]{2,1,0:T(8,128)(2,1)}), bf16[8,32,128]{2,1,0:T(8,128)(2,1)S(1)}, u32[]{:S(2)}, u32[]{:S(2)}) async-start(bf16[8,32,128]{2,1,0:T(8,128)(2,1)} %broadcast_in_dim.7), calls=%async_computation.1 | async-start | bytes 131072 | tf_op jit(solution)/shard_map/all_to_all | solution.py:191
  23.8 1.1 slice_bitcast_fusion
  25.0 4.7 %collective-permute-start.2 = (bf16[2,8,128,128]{3,2,1,0:T(8,128)(2,1)}, bf16[2,8,128,128]{3,2,1,0:T(8,128)(2,1)S(1)}, u32[]{:S(2)}, u32[]{:S(2)}) collective-permute-start(bf16[2,8,128,128]{3,2,1,0:T(8,128)(2,1)} %get-tuple-element.30), channel_id=1, source_target_pairs={{0,6},{2,0},{4,2},{6,4},{1,7},{3,1},{5,3},{7,5},{8,14},{10,8},{12,... | collective-permute-start | bytes 1572872 | tf_op jit(solution)/shard_map/ppermute | solution.py:223
  29.6 2.7 %collective-permute-start.1 = (bf16[2,8,128,128]{3,2,1,0:T(8,128)(2,1)}, bf16[2,8,128,128]{3,2,1,0:T(8,128)(2,1)S(1)}, u32[]{:S(2)}, u32[]{:S(2)}) collective-permute-start(bf16[2,8,128,128]{3,2,1,0:T(8,128)(2,1)} %get-tuple-element.31), channel_id=1, source_target_pairs={{0,4},{2,6},{4,0},{6,2},{1,5},{3,7},{5,1},{7,3},{8,12},{10,14},{12... | collective-permute-start | bytes 1572872 | tf_op jit(solution)/shard_map/ppermute | solution.py:223
  32.4 2.8 %collective-permute-start = (bf16[2,8,128,128]{3,2,1,0:T(8,128)(2,1)S(1)}, bf16[2,8,128,128]{3,2,1,0:T(8,128)(2,1)S(1)}, u32[]{:S(2)}, u32[]{:S(2)}) collective-permute-start(bf16[2,8,128,128]{3,2,1,0:T(8,128)(2,1)S(1)} %get-tuple-element.32), channel_id=1, source_target_pairs={{0,2},{2,4},{4,6},{6,0},{1,3},{3,5},{5,7},{7,1},{8,10},{10,12},{12... | collective-permute-start | bytes 1572872 | tf_op jit(solution)/shard_map/ppermute | solution.py:223
  35.2 0.0 copy-done.3
  35.2 0.0 all-to-all-done.1
  35.2 0.9 broadcast_in_dim.8
  36.1 3.5 %all-to-all-start.2 = ((bf16[8,8,32,128]{3,2,1,0:T(8,128)(2,1)}), bf16[8,8,32,128]{3,2,1,0:T(8,128)(2,1)S(1)}, u32[]{:S(2)}, u32[]{:S(2)}) async-start(bf16[8,8,32,128]{3,2,1,0:T(8,128)(2,1)} %broadcast_in_dim.8), calls=%async_computation.2 | async-start | bytes 1048576 | tf_op jit(solution)/shard_map/all_to_all | solution.py:191
  39.6 8.2 %collective-permute-start.3 = (bf16[80,128]{1,0:T(8,128)(2,1)S(1)}, bf16[80,128]{1,0:T(8,128)(2,1)S(1)}, u32[]{:S(2)}, u32[]{:S(2)}) collective-permute-start(bf16[80,128]{1,0:T(8,128)(2,1)S(1)} %pad_maximum_fusion.pack_ref), channel_id=1, source_target_pairs={{0,1},{1,0},{2,3},{3,2},{4,5},{5,4},{6,7},{7,6},{8,9},{9,8},{10,11... | collective-permute-start | bytes 61448 | tf_op jit(solution)/shard_map/ppermute | solution.py:195
  47.9 6.2 %collective-permute-done.3.pack_other_ref = bf16[80,128]{1,0:T(8,128)(2,1)S(1)} collective-permute-done((bf16[80,128]{1,0:T(8,128)(2,1)S(1)}, bf16[80,128]{1,0:T(8,128)(2,1)S(1)}, u32[]{:S(2)}, u32[]{:S(2)}) %collective-permute-start.3) | collective-permute-done | bytes 20512 | tf_op jit(solution)/shard_map/ppermute | solution.py:195
  54.0 0.0 collective-permute-done.2.d3_ref
  54.0 0.0 collective-permute-done.1.d2_ref
  54.0 1.8 %collective-permute-done.d1_ref = bf16[2,8,128,128]{3,2,1,0:T(8,128)(2,1)S(1)} collective-permute-done((bf16[2,8,128,128]{3,2,1,0:T(8,128)(2,1)S(1)}, bf16[2,8,128,128]{3,2,1,0:T(8,128)(2,1)S(1)}, u32[]{:S(2)}, u32[]{:S(2)}) %collective-permute-start) | collective-permute-done | bytes 524320 | tf_op jit(solution)/shard_map/ppermute | solution.py:223
  55.9 0.0 all-to-all-done.2
  55.9 0.4 shard_map.94
  56.3 9.8 %all_to_all.35.packs_ref = bf16[4,288,128]{2,1,0:T(8,128)(2,1)S(1)} all-to-all(bf16[4,288,128]{2,1,0:T(8,128)(2,1)S(1)} %get-tuple-element.23), channel_id=1, replica_groups=mesh['y'=4,'zl'=8,'c'=2,'x'=4,'zh'=2] {'x'}, dimensions={0} | all-to-all | bytes 589824 | tf_op jit(solution)/shard_map/all_to_all | solution.py:191
  66.1 8.2 %collective-permute-start.4 = (bf16[128,128]{1,0:T(8,128)(2,1)S(1)}, bf16[128,128]{1,0:T(8,128)(2,1)S(1)}, u32[]{:S(2)}, u32[]{:S(2)}) collective-permute-start(bf16[128,128]{1,0:T(8,128)(2,1)S(1)} %slice_reduce_fusion.sum_ref), channel_id=1, source_target_pairs={{0,1},{1,0},{2,3},{3,2},{4,5},{5,4},{6,7},{7,6},{8,9},{9,8},{10,11... | collective-permute-start | bytes 98312 | tf_op jit(solution)/shard_map/ppermute | solution.py:195
  74.4 6.6 %collective-permute-done.4.other_ref = bf16[128,128]{1,0:T(8,128)(2,1)S(1)} collective-permute-done((bf16[128,128]{1,0:T(8,128)(2,1)S(1)}, bf16[128,128]{1,0:T(8,128)(2,1)S(1)}, u32[]{:S(2)}, u32[]{:S(2)}) %collective-permute-start.4) | collective-permute-done | bytes 32800 | tf_op jit(solution)/shard_map/ppermute | solution.py:195
  81.0 1.3 shard_map.95
  82.3 14.6 %all_to_all.36.in_ref = bf16[8,272,128]{2,1,0:T(8,128)(2,1)S(1)} all-to-all(bf16[8,272,128]{2,1,0:T(8,128)(2,1)S(1)} %bitcast.25), channel_id=1, replica_groups=mesh['y'=4,'zl'=8,'c'=2,'x'=4,'zh'=2] {'y','c'}, dimensions={0} | all-to-all | bytes 1114112 | tf_op jit(solution)/shard_map/all_to_all | solution.py:191
  97.0 0.1 shard_map.96
  97.0 27.5 %all_to_all.37.in_ref = bf16[16,48,128]{2,1,0:T(8,128)(2,1)S(1)} all-to-all(bf16[16,48,128]{2,1,0:T(8,128)(2,1)S(1)} %bitcast.24), channel_id=1, replica_groups=mesh['y'=4,'zl'=8,'c'=2,'x'=4,'zh'=2] {'zl','zh'}, dimensions={0} | all-to-all | bytes 393216 | tf_op jit(solution)/shard_map/all_to_all | solution.py:191
  124.6 11.3 %all_to_all.38.in_ref = bf16[16,48,128]{2,1,0:T(8,128)(2,1)S(1)} all-to-all(bf16[16,48,128]{2,1,0:T(8,128)(2,1)S(1)} %shard_map.97), channel_id=1, replica_groups=mesh['y'=4,'zl'=8,'c'=2,'x'=4,'zh'=2] {'y','x'}, dimensions={0} | all-to-all | bytes 393216 | tf_op jit(solution)/shard_map/all_to_all | solution.py:191
  135.9 0.7 shard_map.98
  (10 shorter events, 0.1 us)
Async XLA Ops:
  0.6 9.9 %all-to-all-start = ((bf16[4,32,128]{2,1,0:T(8,128)(2,1)}), bf16[4,32,128]{2,1,0:T(8,128)(2,1)S(1)}, u32[]{:S(2)}, u32[]{:S(2)}) async-start(bf16[4,32,128]{2,1,0:T(8,128)(2,1)} %bitcast.28), calls=%async_computation | async-start | bytes 65536 | tf_op jit(solution)/shard_map/all_to_all | solution.py:191
  5.1 1.2 copy-start
  6.3 0.7 copy-start.1
  7.0 0.7 copy-start.2
  11.2 24.0 %all-to-all-start.1 = ((bf16[8,32,128]{2,1,0:T(8,128)(2,1)}), bf16[8,32,128]{2,1,0:T(8,128)(2,1)S(1)}, u32[]{:S(2)}, u32[]{:S(2)}) async-start(bf16[8,32,128]{2,1,0:T(8,128)(2,1)} %broadcast_in_dim.7), calls=%async_computation.1 | async-start | bytes 131072 | tf_op jit(solution)/shard_map/all_to_all | solution.py:191
  23.8 11.3 %copy-start.3 = (bf16[128,32]{0,1:T(8,128)(2,1)S(1)}, bf16[128,32]{0,1:T(8,128)(2,1)}, u32[]{:S(2)}) copy-start(bf16[128,32]{0,1:T(8,128)(2,1)} %param.11) | copy-start | bytes 24580
  23.8 11.3 %copy-start.4 = (bf16[128,32]{0,1:T(8,128)(2,1)S(1)}, bf16[128,32]{0,1:T(8,128)(2,1)}, u32[]{:S(2)}) copy-start(bf16[128,32]{0,1:T(8,128)(2,1)} %param.9) | copy-start | bytes 24580
  25.0 29.1 %collective-permute-start.2 = (bf16[2,8,128,128]{3,2,1,0:T(8,128)(2,1)}, bf16[2,8,128,128]{3,2,1,0:T(8,128)(2,1)S(1)}, u32[]{:S(2)}, u32[]{:S(2)}) collective-permute-start(bf16[2,8,128,128]{3,2,1,0:T(8,128)(2,1)} %get-tuple-element.30), channel_id=1, source_target_pairs={{0,6},{2,0},{4,2},{6,4},{1,7},{3,1},{5,3},{7,5},{8,14},{10,8},{12,... | collective-permute-start | bytes 1572872 | tf_op jit(solution)/shard_map/ppermute | solution.py:223
  29.6 24.4 %collective-permute-start.1 = (bf16[2,8,128,128]{3,2,1,0:T(8,128)(2,1)}, bf16[2,8,128,128]{3,2,1,0:T(8,128)(2,1)S(1)}, u32[]{:S(2)}, u32[]{:S(2)}) collective-permute-start(bf16[2,8,128,128]{3,2,1,0:T(8,128)(2,1)} %get-tuple-element.31), channel_id=1, source_target_pairs={{0,4},{2,6},{4,0},{6,2},{1,5},{3,7},{5,1},{7,3},{8,12},{10,14},{12... | collective-permute-start | bytes 1572872 | tf_op jit(solution)/shard_map/ppermute | solution.py:223
  32.4 23.5 %collective-permute-start = (bf16[2,8,128,128]{3,2,1,0:T(8,128)(2,1)S(1)}, bf16[2,8,128,128]{3,2,1,0:T(8,128)(2,1)S(1)}, u32[]{:S(2)}, u32[]{:S(2)}) collective-permute-start(bf16[2,8,128,128]{3,2,1,0:T(8,128)(2,1)S(1)} %get-tuple-element.32), channel_id=1, source_target_pairs={{0,2},{2,4},{4,6},{6,0},{1,3},{3,5},{5,7},{7,1},{8,10},{10,12},{12... | collective-permute-start | bytes 1572872 | tf_op jit(solution)/shard_map/ppermute | solution.py:223
  36.1 19.8 %all-to-all-start.2 = ((bf16[8,8,32,128]{3,2,1,0:T(8,128)(2,1)}), bf16[8,8,32,128]{3,2,1,0:T(8,128)(2,1)S(1)}, u32[]{:S(2)}, u32[]{:S(2)}) async-start(bf16[8,8,32,128]{3,2,1,0:T(8,128)(2,1)} %broadcast_in_dim.8), calls=%async_computation.2 | async-start | bytes 1048576 | tf_op jit(solution)/shard_map/all_to_all | solution.py:191
  39.6 14.4 %collective-permute-start.3 = (bf16[80,128]{1,0:T(8,128)(2,1)S(1)}, bf16[80,128]{1,0:T(8,128)(2,1)S(1)}, u32[]{:S(2)}, u32[]{:S(2)}) collective-permute-start(bf16[80,128]{1,0:T(8,128)(2,1)S(1)} %pad_maximum_fusion.pack_ref), channel_id=1, source_target_pairs={{0,1},{1,0},{2,3},{3,2},{4,5},{5,4},{6,7},{7,6},{8,9},{9,8},{10,11... | collective-permute-start | bytes 61448 | tf_op jit(solution)/shard_map/ppermute | solution.py:195
  66.1 14.9 %collective-permute-start.4 = (bf16[128,128]{1,0:T(8,128)(2,1)S(1)}, bf16[128,128]{1,0:T(8,128)(2,1)S(1)}, u32[]{:S(2)}, u32[]{:S(2)}) collective-permute-start(bf16[128,128]{1,0:T(8,128)(2,1)S(1)} %slice_reduce_fusion.sum_ref), channel_id=1, source_target_pairs={{0,1},{1,0},{2,3},{3,2},{4,5},{5,4},{6,7},{7,6},{8,9},{9,8},{10,11... | collective-permute-start | bytes 98312 | tf_op jit(solution)/shard_map/ppermute | solution.py:195
